TPU v7x, 32 devices: a whole 2x2x4 slice. The times are simulated.
32 devices in a mesh: section: 2 (over core), dp: 4 (over y, x), mp: 4 (over z).
Axes of the slice: x: 2, y: 2, z: 4, core: 2. Of those that a mesh axis runs over, the one named last changes fastest.
Arguments:
- layer_input: bfloat16 [2, 4, 1024, 1024], P(None, 'dp', 'mp'), may hold values from -6 to 6
- cotangent: bfloat16 [2, 4, 1024, 1024], P(None, 'dp', 'mp'), may hold values from -6 to 6
- example_lengths: int32 [2, 4, 4], P(None, 'dp'), may hold values from 1 to 976, as said below
- attn_gain: bfloat16 [2, 1024], P('section'), may hold values from 0.5 to 1.5
- attn_shift: bfloat16 [2, 1024], P('section'), may hold values from -1.75 to 1.75
- query_key_value_weight: bfloat16 [2, 1024, 3072], P('section', None, 'mp'), may hold values from -0.1875 to 0.1875
- qkv_bias: bfloat16 [2, 3072], P('section', 'mp'), may hold values from -1.75 to 1.75
- attention_output_weight: bfloat16 [2, 1024, 1024], P('section', 'mp'), may hold values from -0.75 to 0.75
- out_bias: bfloat16 [2, 1024], P('section'), may hold values from -1.75 to 1.75
- ffn_gain: bfloat16 [2, 1024], P('section'), may hold values from 0.5 to 1.5
- ffn_shift: bfloat16 [2, 1024], P('section'), may hold values from -1.75 to 1.75
- up_projection_weight: bfloat16 [2, 1024, 4096], P('section', None, 'mp'), may hold values from -0.1875 to 0.1875
- up_projection_bias: bfloat16 [2, 4096], P('section', 'mp'), may hold values from -1.75 to 1.75
- down_projection_weight: bfloat16 [2, 4096, 1024], P('section', 'mp'), may hold values from -0.09375 to 0.09375
- down_bias: bfloat16 [2, 1024], P('section'), may hold values from -1.75 to 1.75
- prefix_table: bfloat16 [10, 1024], replicated, may hold values from -6 to 6
- mid_weight: bfloat16 [1024, 512], replicated, may hold values from -0.1875 to 0.1875
- mid_bias: bfloat16 [512], replicated, may hold values from -1.75 to 1.75
- prefix_weight: bfloat16 [512, 4096], P(None, ('section', 'mp')), may hold values from -0.25 to 0.25
- prefix_bias: bfloat16 [4096], P(('section', 'mp')), may hold values from -1.75 to 1.75
Outputs:
- activations: bfloat16 [2, 2, 4, 1024, 1024], P('section', None, 'dp', 'mp')
- input_grads: bfloat16 [2, 2, 4, 1024, 1024], P('section', None, 'dp', 'mp')
- table_grad: float32 [10, 1024], replicated
- mid_weight_grad: float32 [1024, 512], replicated
- mid_bias_grad: float32 [512], replicated
- prefix_weight_grad: float32 [512, 4096], P(None, ('section', 'mp'))
- prefix_bias_grad: float32 [4096], P(('section', 'mp'))
Inputs may be any that keep to these rules, and one draw needn't show every extreme that they name: `example_lengths`: the 4 examples of a sequence are consecutive runs of rows that together fill its 1024 rows.
All inputs are finite; a program needn't handle non-finite values.
Results may differ from a plain program's by a relative error of at most 0.02.
Values may be sent and summed in bfloat16 or wider, within the bound.
A program may use at most 256 MiB of HBM per device.

v0:
```python
import jax
import jax.numpy as jnp
from jax import lax
from jax.sharding import PartitionSpec as P

HEAD_DIM = 64
PREFIX = 10
SEQ_LEN = 1024


EPSILON = 1e-05
NEG_LARGE = -1e30


def passed_along(x, axis, by):
    length = lax.axis_size(axis)
    pairs = [(i, i + by) for i in range(length) if 0 <= i + by < length]
    return lax.ppermute(x, axis, pairs)


def norm_rows(values, gain, shift):
    average = jnp.mean(values, axis=-1, keepdims=True)
    centred = values - average
    spread = jnp.mean(centred * centred, axis=-1, keepdims=True)
    return centred * lax.rsqrt(spread + EPSILON) * gain + shift


def norm_input_grad(values, gain, shift, incoming):

    def apply_norm(inputs):
        return norm_rows(inputs, gain, shift)

    norm_value, norm_back = jax.vjp(apply_norm, values)
    return norm_back(incoming)[0]


def gelu_tanh(values):
    return jax.nn.gelu(values, approximate=True)


def visible_of(lengths, first_row, count):
    run_ends = jnp.cumsum(lengths, axis=-1)
    keys_at = jnp.arange(SEQ_LEN, dtype=jnp.int32)
    query_at = first_row + jnp.arange(count, dtype=jnp.int32)
    key_seg = jnp.sum((keys_at[None, :, None] >= run_ends[:, None, :]).astype(jnp.int32), axis=-1)
    query_seg = jnp.sum(
        (query_at[None, :, None] >= run_ends[:, None, :]).astype(jnp.int32), axis=-1
    )
    causal = (query_at[:, None] >= keys_at[None, :])[None]
    inside = (query_seg[:, :, None] == key_seg[:, None, :]) & causal
    leading = jnp.ones((lengths.shape[0], count, PREFIX), dtype=bool)
    return jnp.concatenate([leading, inside], axis=2)


def gather_rows(piece):
    return lax.all_gather(piece, "mp", axis=1, tiled=True)


def reduce_rows(partial_sum):
    return lax.psum_scatter(
        partial_sum.astype(jnp.bfloat16), "mp", scatter_dimension=1, tiled=True
    ).astype(jnp.float32)


def with_prefix(prefix_kv, pair_keys, pair_values, heads_count):
    prefix_pair = prefix_kv.reshape(PREFIX, heads_count, 2, HEAD_DIM)
    key_rows = jnp.concatenate([prefix_pair[None, :, :, 0], pair_keys], axis=1)
    value_rows = jnp.concatenate([prefix_pair[None, :, :, 1], pair_values], axis=1)
    return (key_rows, value_rows)


def attend(query_rows, key_rows, value_rows, visible):
    score_scale = HEAD_DIM ** (-0.5)
    scores = (
        jnp.einsum("sqhd,skhd->shqk", query_rows, key_rows, preferred_element_type=jnp.float32)
        * score_scale
    )
    scores = jnp.where(visible[:, None], scores, NEG_LARGE)
    highest = jnp.max(scores, axis=-1, keepdims=True)
    raised = jnp.exp(scores - highest)
    softmax_probs = raised / jnp.sum(raised, axis=-1, keepdims=True)
    probs_low = softmax_probs.astype(jnp.bfloat16)
    head_mixed_rows = jnp.einsum(
        "shqk,skhd->sqhd", probs_low, value_rows, preferred_element_type=jnp.float32
    )
    batch_size, query_count, heads_count, head_size = head_mixed_rows.shape
    head_mixed_rows = head_mixed_rows.astype(jnp.bfloat16).reshape(
        batch_size, query_count, heads_count * head_size
    )
    return (softmax_probs, probs_low, head_mixed_rows)


def attend_back(grad_mix, query_rows, key_rows, value_rows, softmax_probs, probs_low):
    grad_heads = grad_mix.reshape(query_rows.shape)
    grad_probs = jnp.einsum(
        "sqhd,skhd->shqk", grad_heads, value_rows, preferred_element_type=jnp.float32
    )
    value_grad = jnp.einsum(
        "shqk,sqhd->skhd", probs_low, grad_heads, preferred_element_type=jnp.float32
    )
    row_term = jnp.sum(grad_probs * softmax_probs, axis=-1, keepdims=True)
    grad_scores = (softmax_probs * (grad_probs - row_term)).astype(jnp.bfloat16)
    score_scale = HEAD_DIM ** (-0.5)
    query_grad = (
        jnp.einsum("shqk,skhd->sqhd", grad_scores, key_rows, preferred_element_type=jnp.float32)
        * score_scale
    )
    key_grad = (
        jnp.einsum("shqk,sqhd->skhd", grad_scores, query_rows, preferred_element_type=jnp.float32)
        * score_scale
    )
    return (query_grad, key_grad, value_grad)


def prefix_part(key_grad, value_grad):
    pair_sum = jnp.stack(
        [jnp.sum(key_grad[:, :PREFIX], axis=0), jnp.sum(value_grad[:, :PREFIX], axis=0)], axis=2
    )
    return pair_sum.reshape(PREFIX, -1)


def tensor_forward(own_rows, weights, prefix_kv, visible):
    (
        attn_gain,
        attn_shift,
        query_key_value_weight,
        qkv_bias,
        attention_output_weight,
        out_bias,
        ffn_gain,
        ffn_shift,
        up_projection_weight,
        up_projection_bias,
        down_projection_weight,
        down_bias,
        out_full,
    ) = weights
    normed = norm_rows(own_rows, attn_gain, attn_shift).astype(jnp.bfloat16)
    normalized_input_rows = gather_rows(normed)
    batch_size, seq_len, model_width = normalized_input_rows.shape
    heads_here = query_key_value_weight.shape[1] // (3 * HEAD_DIM)
    projected = (
        jnp.einsum(
            "naj,jk->nak",
            normalized_input_rows,
            query_key_value_weight,
            preferred_element_type=jnp.float32,
        )
        + qkv_bias
    )
    triple = projected.astype(jnp.bfloat16).reshape(batch_size, seq_len, heads_here, 3, HEAD_DIM)
    query_rows = triple[:, :, :, 0]
    key_rows, value_rows = with_prefix(
        prefix_kv, triple[:, :, :, 1], triple[:, :, :, 2], heads_here
    )
    softmax_probs, probs_low, head_mixed_rows = attend(query_rows, key_rows, value_rows, visible)
    attn_part = reduce_rows(
        jnp.einsum(
            "hgm,mt->hgt",
            head_mixed_rows,
            attention_output_weight,
            preferred_element_type=jnp.float32,
        )
    )
    after_attn = own_rows + attn_part + out_bias
    normed_two = norm_rows(after_attn, ffn_gain, ffn_shift).astype(jnp.bfloat16)
    second_norm_rows = gather_rows(normed_two)
    up_pre = (
        jnp.einsum(
            "rmy,yq->rmq",
            second_norm_rows,
            up_projection_weight,
            preferred_element_type=jnp.float32,
        )
        + up_projection_bias
    )
    gelu_output_rows = gelu_tanh(up_pre).astype(jnp.bfloat16)
    mlp_part = reduce_rows(
        jnp.einsum(
            "epj,jq->epq",
            gelu_output_rows,
            down_projection_weight,
            preferred_element_type=jnp.float32,
        )
    )
    result = after_attn + mlp_part + down_bias
    kept_values = (query_rows, key_rows, value_rows, softmax_probs, probs_low, after_attn, up_pre)
    return (result, kept_values)


def tensor_backward(own_rows, arriving, weights, prefix_kv, visible):
    (
        attn_gain,
        attn_shift,
        query_key_value_weight,
        qkv_bias,
        attention_output_weight,
        out_bias,
        ffn_gain,
        ffn_shift,
        up_projection_weight,
        up_projection_bias,
        down_projection_weight,
        down_bias,
        out_full,
    ) = weights
    result, kept_values = tensor_forward(own_rows, weights, prefix_kv, visible)
    query_rows, key_rows, value_rows, softmax_probs, probs_low, after_attn, up_pre = kept_values
    gradient_gathered = gather_rows(arriving)
    gradient_activation = jnp.einsum(
        "bhi,vi->bhv", gradient_gathered, down_projection_weight, preferred_element_type=jnp.float32
    )
    gelu_value, gelu_back = jax.vjp(gelu_tanh, up_pre)
    gradient_up_projection = gelu_back(gradient_activation)[0].astype(jnp.bfloat16)
    grad_two = reduce_rows(
        jnp.einsum(
            "yca,ja->ycj",
            gradient_up_projection,
            up_projection_weight,
            preferred_element_type=jnp.float32,
        )
    )
    grad_after = norm_input_grad(after_attn, ffn_gain, ffn_shift, grad_two)
    grad_mid = (grad_after + arriving.astype(jnp.float32)).astype(jnp.bfloat16)
    middle_gathered = gather_rows(grad_mid)
    grad_mix = jnp.einsum(
        "taq,kq->tak", middle_gathered, attention_output_weight, preferred_element_type=jnp.float32
    ).astype(jnp.bfloat16)
    query_grad, key_grad, value_grad = attend_back(
        grad_mix, query_rows, key_rows, value_rows, softmax_probs, probs_low
    )
    prefix_g = prefix_part(key_grad, value_grad)
    batch_size, seq_len = (query_grad.shape[0], query_grad.shape[1])
    gradient_query_key_value = jnp.stack(
        [query_grad, key_grad[:, PREFIX:], value_grad[:, PREFIX:]], axis=3
    )
    gradient_query_key_value = gradient_query_key_value.astype(jnp.bfloat16).reshape(
        batch_size, seq_len, -1
    )
    grad_one = reduce_rows(
        jnp.einsum(
            "tvq,xq->tvx",
            gradient_query_key_value,
            query_key_value_weight,
            preferred_element_type=jnp.float32,
        )
    )
    grad_input = norm_input_grad(own_rows, attn_gain, attn_shift, grad_one)
    grad_input = (grad_input + grad_mid.astype(jnp.float32)).astype(jnp.bfloat16)
    return (grad_input, prefix_g)


def layer_step(own_rows, weights, prefix_use, visible):
    return tensor_forward(own_rows, weights, prefix_use, visible)


def layer_back(own_rows, arriving, weights, prefix_use, visible):
    return tensor_backward(own_rows, arriving, weights, prefix_use, visible)


def body(
    layer_input,
    cotangent,
    example_lengths,
    attn_gain,
    attn_shift,
    query_key_value_weight,
    qkv_bias,
    attention_output_weight,
    out_bias,
    ffn_gain,
    ffn_shift,
    up_projection_weight,
    up_projection_bias,
    down_projection_weight,
    down_bias,
    prefix_table,
    mid_weight,
    mid_bias,
    prefix_weight,
    prefix_bias,
):
    sections = lax.axis_size("section")
    section_index = lax.axis_index("section")
    micro_count = layer_input.shape[0]
    tick_count = micro_count + sections - 1
    hidden_pre = jnp.dot(
        prefix_table, mid_weight, preferred_element_type=jnp.float32
    ) + mid_bias.astype(jnp.float32)
    hidden_act = jnp.tanh(hidden_pre)
    hidden_low = hidden_act.astype(jnp.bfloat16)
    prefix_kv = (
        jnp.dot(hidden_low, prefix_weight, preferred_element_type=jnp.float32)
        + prefix_bias.astype(jnp.float32)
    ).astype(jnp.bfloat16)
    small_parts = (
        attn_gain[0].astype(jnp.float32),
        attn_shift[0].astype(jnp.float32),
        out_bias[0].astype(jnp.float32),
        ffn_gain[0].astype(jnp.float32),
        ffn_shift[0].astype(jnp.float32),
        down_bias[0].astype(jnp.float32),
    )
    weights = (
        small_parts[0],
        small_parts[1],
        query_key_value_weight[0],
        qkv_bias[0].astype(jnp.float32),
        attention_output_weight[0],
        small_parts[2],
        small_parts[3],
        small_parts[4],
        up_projection_weight[0],
        up_projection_bias[0].astype(jnp.float32),
        down_projection_weight[0],
        small_parts[5],
        attention_output_weight[0],
    )
    first_row = 0
    query_count = SEQ_LEN
    received = jnp.zeros_like(layer_input[0])
    entered = []
    produced = []
    for tick_index in range(tick_count):
        batch_index = jnp.clip(tick_index - section_index, 0, micro_count - 1)
        own_input = layer_input[min(tick_index, micro_count - 1)]
        entering = jnp.where(section_index == 0, own_input, received)
        lengths_now = lax.dynamic_index_in_dim(example_lengths, batch_index, 0, keepdims=False)
        visible = visible_of(lengths_now, first_row, query_count)
        result, kept_values = layer_step(entering.astype(jnp.float32), weights, prefix_kv, visible)
        leaving = result.astype(jnp.bfloat16)
        entered.append(entering)
        produced.append(leaving)
        if tick_index + 1 < tick_count:
            received = passed_along(leaving, "section", 1)
    kept_inputs = lax.dynamic_slice_in_dim(jnp.stack(entered), section_index, micro_count, 0)
    activations = lax.dynamic_slice_in_dim(jnp.stack(produced), section_index, micro_count, 0)
    back_offset = sections - 1 - section_index
    received_grad = jnp.zeros_like(cotangent[0])
    sent_grads = []
    prefix_total = None
    for tick_index in range(tick_count):
        raw_index = tick_index - back_offset
        is_valid = ((raw_index >= 0) & (raw_index < micro_count)).astype(jnp.float32)
        batch_index = jnp.clip(raw_index, 0, micro_count - 1)
        own_grad = cotangent[min(tick_index, micro_count - 1)]
        arriving = jnp.where(section_index == sections - 1, own_grad, received_grad)
        entering = lax.dynamic_index_in_dim(kept_inputs, batch_index, 0, keepdims=False)
        lengths_now = lax.dynamic_index_in_dim(example_lengths, batch_index, 0, keepdims=False)
        visible = visible_of(lengths_now, first_row, query_count)
        grad_input, prefix_g = layer_back(
            entering.astype(jnp.float32), arriving, weights, prefix_kv, visible
        )
        if tick_index == 0:
            prefix_total = is_valid * prefix_g
        else:
            prefix_total = prefix_total + is_valid * prefix_g
        sent_grads.append(grad_input)
        if tick_index + 1 < tick_count:
            received_grad = passed_along(grad_input, "section", -1)
    input_grads = lax.dynamic_slice_in_dim(jnp.stack(sent_grads), back_offset, micro_count, 0)
    prefix_sum = lax.psum(prefix_total, "dp")
    prefix_low = prefix_sum.astype(jnp.bfloat16)
    prefix_bias_grad = jnp.sum(prefix_low.astype(jnp.float32), axis=0)
    prefix_weight_grad = jnp.dot(hidden_low.T, prefix_low, preferred_element_type=jnp.float32)
    hidden_part = jnp.dot(prefix_low, prefix_weight.T, preferred_element_type=jnp.float32)
    hidden_grad = lax.psum(hidden_part, ("section", "mp"))
    pre_grad = (hidden_grad * (1.0 - hidden_act * hidden_act)).astype(jnp.bfloat16)
    mid_bias_grad = jnp.sum(pre_grad.astype(jnp.float32), axis=0)
    mid_weight_grad = jnp.dot(prefix_table.T, pre_grad, preferred_element_type=jnp.float32)
    table_grad = jnp.dot(pre_grad, mid_weight.T, preferred_element_type=jnp.float32)
    return (
        activations[None],
        input_grads[None],
        table_grad,
        mid_weight_grad,
        mid_bias_grad,
        prefix_weight_grad,
        prefix_bias_grad,
    )


def solution(mesh):
    placed = (
        P(None, "dp", "mp", None),
        P(None, "dp", "mp", None),
        P(None, "dp", None),
        P("section", None),
        P("section", None),
        P("section", None, "mp"),
        P("section", "mp"),
        P("section", "mp", None),
        P("section", None),
        P("section", None),
        P("section", None),
        P("section", None, "mp"),
        P("section", "mp"),
        P("section", "mp", None),
        P("section", None),
        P(),
        P(),
        P(),
        P(None, ("section", "mp")),
        P(("section", "mp")),
    )
    return jax.shard_map(
        body,
        mesh=mesh,
        in_specs=placed,
        out_specs=(
            P("section", None, "dp", "mp", None),
            P("section", None, "dp", "mp", None),
            P(),
            P(),
            P(),
            P(None, ("section", "mp")),
            P(("section", "mp")),
        ),
        check_vma=False,
    )
```

profile of v0, /device:TPU:0, one launch (start us, length us, event | category | flops | bytes accessed | tf_op | source)
XLA Modules:
  0.0 1768.3 jit_solution(4225618501653134843)
XLA Ops:
  17.1 43.2 %all-gather.20.cloned.1.call-done = bf16[1,1024,1024]{2,1,0:T(8,128)(2,1)} async-done(((bf16[1,256,1024]{2,1,0:T(8,128)(2,1)}), bf16[1,1024,1024]{2,1,0:T(8,128)(2,1)}) %all-gather.20.cloned.1.call-update) | async-done | bytes 2097168 | tf_op jit(solution)/shard_map/all_gather | solution.py:56
  89.0 42.4 %reduce-scatter.16.cloned.1.call-done = bf16[1,256,1024]{2,1,0:T(8,128)(2,1)} async-done(((bf16[1,1024,1024]{2,1,0:T(8,128)(2,1)}), bf16[1,256,1024]{2,1,0:T(8,128)(2,1)}) %reduce-scatter.16.cloned.1.call-update) | async-done | bytes 524304 | tf_op jit(solution)/shard_map/reduce_scatter | solution.py:60
  135.4 45.3 %all-gather.22.cloned.1.call-done = bf16[1,1024,1024]{2,1,0:T(8,128)(2,1)} async-done(((bf16[1,256,1024]{2,1,0:T(8,128)(2,1)}), bf16[1,1024,1024]{2,1,0:T(8,128)(2,1)}) %all-gather.22.cloned.1.call-update) | async-done | bytes 2097168 | tf_op jit(solution)/shard_map/all_gather | solution.py:56
  189.7 42.1 %reduce-scatter.18.cloned.1.call-done = bf16[1,256,1024]{2,1,0:T(8,128)(2,1)} async-done(((bf16[1,1024,1024]{2,1,0:T(8,128)(2,1)}), bf16[1,256,1024]{2,1,0:T(8,128)(2,1)}) %reduce-scatter.18.cloned.1.call-update) | async-done | bytes 524304 | tf_op jit(solution)/shard_map/reduce_scatter | solution.py:60
  240.5 43.1 %all-gather.24.cloned.1.call-done = bf16[1,1024,1024]{2,1,0:T(8,128)(2,1)} async-done(((bf16[1,256,1024]{2,1,0:T(8,128)(2,1)}), bf16[1,1024,1024]{2,1,0:T(8,128)(2,1)}) %all-gather.24.cloned.1.call-update) | async-done | bytes 2097168 | tf_op jit(solution)/shard_map/all_gather | solution.py:56
  312.5 42.5 %reduce-scatter.20.cloned.1.call-done = bf16[1,256,1024]{2,1,0:T(8,128)(2,1)} async-done(((bf16[1,1024,1024]{2,1,0:T(8,128)(2,1)}), bf16[1,256,1024]{2,1,0:T(8,128)(2,1)}) %reduce-scatter.20.cloned.1.call-update) | async-done | bytes 524304 | tf_op jit(solution)/shard_map/reduce_scatter | solution.py:60
  359.0 45.3 %all-gather.26.cloned.1.call-done = bf16[1,1024,1024]{2,1,0:T(8,128)(2,1)} async-done(((bf16[1,256,1024]{2,1,0:T(8,128)(2,1)}), bf16[1,1024,1024]{2,1,0:T(8,128)(2,1)}) %all-gather.26.cloned.1.call-update) | async-done | bytes 2097168 | tf_op jit(solution)/shard_map/all_gather | solution.py:56
  412.7 42.7 %reduce-scatter.22.cloned.1.call-done = bf16[1,256,1024]{2,1,0:T(8,128)(2,1)} async-done(((bf16[1,1024,1024]{2,1,0:T(8,128)(2,1)}), bf16[1,256,1024]{2,1,0:T(8,128)(2,1)}) %reduce-scatter.22.cloned.1.call-update) | async-done | bytes 524304 | tf_op jit(solution)/shard_map/reduce_scatter | solution.py:60
  468.2 42.6 %all-gather.28.cloned.1.call-done = bf16[1,1024,1024]{2,1,0:T(8,128)(2,1)} async-done(((bf16[1,256,1024]{2,1,0:T(8,128)(2,1)}), bf16[1,1024,1024]{2,1,0:T(8,128)(2,1)}) %all-gather.28.cloned.1.call-update) | async-done | bytes 2097168 | tf_op jit(solution)/shard_map/all_gather | solution.py:56
  602.4 46.0 %reduce-scatter.28.cloned.1.call-done = bf16[1,256,1024]{2,1,0:T(8,128)(2,1)} async-done(((bf16[1,1024,1024]{2,1,0:T(8,128)(2,1)}), bf16[1,256,1024]{2,1,0:T(8,128)(2,1)}) %reduce-scatter.28.cloned.1.call-update) | async-done | bytes 524304 | tf_op jit(solution)/shard_map/reduce_scatter | solution.py:60
  660.5 39.3 %all-gather.38.cloned.1.call-done = bf16[1,1024,1024]{2,1,0:T(8,128)(2,1)} async-done(((bf16[1,256,1024]{2,1,0:T(8,128)(2,1)}), bf16[1,1024,1024]{2,1,0:T(8,128)(2,1)}) %all-gather.38.cloned.1.call-update) | async-done | bytes 2097168 | tf_op jit(solution)/shard_map/all_gather | solution.py:56
  799.2 39.5 %all-gather.34.cloned.1.call-done = bf16[1,1024,1024]{2,1,0:T(8,128)(2,1)} async-done(((bf16[1,256,1024]{2,1,0:T(8,128)(2,1)}), bf16[1,1024,1024]{2,1,0:T(8,128)(2,1)}) %all-gather.34.cloned.1.call-update) | async-done | bytes 2097168 | tf_op jit(solution)/shard_map/all_gather | solution.py:56
  883.5 46.0 %reduce-scatter.40.cloned.1.call-done = bf16[1,256,1024]{2,1,0:T(8,128)(2,1)} async-done(((bf16[1,1024,1024]{2,1,0:T(8,128)(2,1)}), bf16[1,256,1024]{2,1,0:T(8,128)(2,1)}) %reduce-scatter.40.cloned.1.call-update) | async-done | bytes 524304 | tf_op jit(solution)/shard_map/reduce_scatter | solution.py:60
  929.5 45.5 %reduce-scatter.30.cloned.1.call-done = bf16[1,256,1024]{2,1,0:T(8,128)(2,1)} async-done(((bf16[1,1024,1024]{2,1,0:T(8,128)(2,1)}), bf16[1,256,1024]{2,1,0:T(8,128)(2,1)}) %reduce-scatter.30.cloned.1.call-update) | async-done | bytes 524304 | tf_op jit(solution)/shard_map/reduce_scatter | solution.py:60
  981.1 45.3 %all-gather.36.cloned.1.call-done = bf16[1,1024,1024]{2,1,0:T(8,128)(2,1)} async-done(((bf16[1,256,1024]{2,1,0:T(8,128)(2,1)}), bf16[1,1024,1024]{2,1,0:T(8,128)(2,1)}) %all-gather.36.cloned.1.call-update) | async-done | bytes 2097168 | tf_op jit(solution)/shard_map/all_gather | solution.py:56
  1079.1 41.9 %reduce-scatter.32.cloned.1.call-done = bf16[1,256,1024]{2,1,0:T(8,128)(2,1)} async-done(((bf16[1,1024,1024]{2,1,0:T(8,128)(2,1)}), bf16[1,256,1024]{2,1,0:T(8,128)(2,1)}) %reduce-scatter.32.cloned.1.call-update) | async-done | bytes 524304 | tf_op jit(solution)/shard_map/reduce_scatter | solution.py:60
  1131.4 36.5 %all-gather.42.cloned.1.call-done = bf16[1,1024,1024]{2,1,0:T(8,128)(2,1)} async-done(((bf16[1,256,1024]{2,1,0:T(8,128)(2,1)}), bf16[1,1024,1024]{2,1,0:T(8,128)(2,1)}) %all-gather.42.cloned.1.call-update) | async-done | bytes 2097168 | tf_op jit(solution)/shard_map/all_gather | solution.py:56
  1173.9 40.8 %all-gather.40.cloned.1.call-done = bf16[1,1024,1024]{2,1,0:T(8,128)(2,1)} async-done(((bf16[1,256,1024]{2,1,0:T(8,128)(2,1)}), bf16[1,1024,1024]{2,1,0:T(8,128)(2,1)}) %all-gather.40.cloned.1.call-update) | async-done | bytes 2097168 | tf_op jit(solution)/shard_map/all_gather | solution.py:56
  1224.2 42.7 %reduce-scatter.36.cloned.1.call-done = bf16[1,256,1024]{2,1,0:T(8,128)(2,1)} async-done(((bf16[1,1024,1024]{2,1,0:T(8,128)(2,1)}), bf16[1,256,1024]{2,1,0:T(8,128)(2,1)}) %reduce-scatter.36.cloned.1.call-update) | async-done | bytes 524304 | tf_op jit(solution)/shard_map/reduce_scatter | solution.py:60
  1271.8 45.4 %all-gather.44.cloned.1.call-done = bf16[1,1024,1024]{2,1,0:T(8,128)(2,1)} async-done(((bf16[1,256,1024]{2,1,0:T(8,128)(2,1)}), bf16[1,1024,1024]{2,1,0:T(8,128)(2,1)}) %all-gather.44.cloned.1.call-update) | async-done | bytes 2097168 | tf_op jit(solution)/shard_map/all_gather | solution.py:56
  1369.6 42.1 %reduce-scatter.38.cloned.1.call-done = bf16[1,256,1024]{2,1,0:T(8,128)(2,1)} async-done(((bf16[1,1024,1024]{2,1,0:T(8,128)(2,1)}), bf16[1,256,1024]{2,1,0:T(8,128)(2,1)}) %reduce-scatter.38.cloned.1.call-update) | async-done | bytes 524304 | tf_op jit(solution)/shard_map/reduce_scatter | solution.py:60
  1464.3 41.0 %all-gather.48.cloned.1.call-done = bf16[1,1024,1024]{2,1,0:T(8,128)(2,1)} async-done(((bf16[1,256,1024]{2,1,0:T(8,128)(2,1)}), bf16[1,1024,1024]{2,1,0:T(8,128)(2,1)}) %all-gather.48.cloned.1.call-update) | async-done | bytes 2097168 | tf_op jit(solution)/shard_map/all_gather | solution.py:56
  1515.3 42.1 %reduce-scatter.42.cloned.1.call-done = bf16[1,256,1024]{2,1,0:T(8,128)(2,1)} async-done(((bf16[1,1024,1024]{2,1,0:T(8,128)(2,1)}), bf16[1,256,1024]{2,1,0:T(8,128)(2,1)}) %reduce-scatter.42.cloned.1.call-update) | async-done | bytes 524304 | tf_op jit(solution)/shard_map/reduce_scatter | solution.py:60
  1565.2 44.6 %all-gather.52.cloned.1.call-done = bf16[1,1024,1024]{2,1,0:T(8,128)(2,1)} async-done(((bf16[1,256,1024]{2,1,0:T(8,128)(2,1)}), bf16[1,1024,1024]{2,1,0:T(8,128)(2,1)}) %all-gather.52.cloned.1.call-update) | async-done | bytes 2097168 | tf_op jit(solution)/shard_map/all_gather | solution.py:56
  (519 shorter events, 724.0 us)
Async XLA Ops:
  11.5 119.9 %reduce-scatter.16.cloned.1.call-start = ((), (), s32[]{:S(2)}) async-start(), calls=%async_computation.16 | async-start | bytes 2621440 | tf_op jit(solution)/shard_map/reduce_scatter | solution.py:60
  135.3 96.5 %reduce-scatter.18.cloned.1.call-start = ((), (), s32[]{:S(2)}) async-start(), calls=%async_computation.18 | async-start | bytes 2621440 | tf_op jit(solution)/shard_map/reduce_scatter | solution.py:60
  189.0 94.6 %all-gather.24.cloned.1.call-start = ((), (), s32[]{:S(2)}) async-start(), calls=%async_computation.19 | async-start | bytes 2621440 | tf_op jit(solution)/shard_map/all_gather | solution.py:56
  237.9 117.1 %reduce-scatter.20.cloned.1.call-start = ((), (), s32[]{:S(2)}) async-start(), calls=%async_computation.20 | async-start | bytes 2621440 | tf_op jit(solution)/shard_map/reduce_scatter | solution.py:60
  358.9 96.5 %reduce-scatter.22.cloned.1.call-start = ((), (), s32[]{:S(2)}) async-start(), calls=%async_computation.22 | async-start | bytes 2621440 | tf_op jit(solution)/shard_map/reduce_scatter | solution.py:60
  412.7 98.2 %all-gather.28.cloned.1.call-start = ((), (), s32[]{:S(2)}) async-start(), calls=%async_computation.23 | async-start | bytes 2621440 | tf_op jit(solution)/shard_map/all_gather | solution.py:56
  465.6 136.8 %reduce-scatter.24.cloned.1.call-start = ((), (), s32[]{:S(2)}) async-start(), calls=%async_computation.24 | async-start | bytes 2621440 | tf_op jit(solution)/shard_map/reduce_scatter | solution.py:60
  538.5 110.0 %reduce-scatter.28.cloned.1.call-start = ((), (), s32[]{:S(2)}) async-start(), calls=%async_computation.28 | async-start | bytes 2621440 | tf_op jit(solution)/shard_map/reduce_scatter | solution.py:60
  589.5 110.3 %all-gather.38.cloned.1.call-start = ((), (), s32[]{:S(2)}) async-start(), calls=%async_computation.33 | async-start | bytes 2621440 | tf_op jit(solution)/shard_map/all_gather | solution.py:56
  654.9 137.6 %all-gather.54.cloned.1.call-start = ((), (), s32[]{:S(2)}) async-start(), calls=%async_computation.47 | async-start | bytes 2621440 | tf_op jit(solution)/shard_map/all_gather | solution.py:56
  656.9 181.8 %all-gather.34.cloned.1.call-start = ((), (), s32[]{:S(2)}) async-start(), calls=%async_computation.29 | async-start | bytes 2621440 | tf_op jit(solution)/shard_map/all_gather | solution.py:56
  657.5 226.0 %reduce-scatter.34.cloned.1.call-start = ((), (), s32[]{:S(2)}) async-start(), calls=%async_computation.35 | async-start | bytes 2621440 | tf_op jit(solution)/shard_map/reduce_scatter | solution.py:60
  732.1 197.4 %reduce-scatter.40.cloned.1.call-start = ((), (), s32[]{:S(2)}) async-start(), calls=%async_computation.42 | async-start | bytes 2621440 | tf_op jit(solution)/shard_map/reduce_scatter | solution.py:60
  778.6 196.4 %reduce-scatter.30.cloned.1.call-start = ((), (), s32[]{:S(2)}) async-start(), calls=%async_computation.30 | async-start | bytes 2621440 | tf_op jit(solution)/shard_map/reduce_scatter | solution.py:60
  847.5 178.9 %all-gather.36.cloned.1.call-start = ((), (), s32[]{:S(2)}) async-start(), calls=%async_computation.31 | async-start | bytes 2621440 | tf_op jit(solution)/shard_map/all_gather | solution.py:56
  981.0 140.0 %reduce-scatter.32.cloned.1.call-start = ((), (), s32[]{:S(2)}) async-start(), calls=%async_computation.32 | async-start | bytes 2621440 | tf_op jit(solution)/shard_map/reduce_scatter | solution.py:60
  1079.0 135.7 %all-gather.40.cloned.1.call-start = ((), (), s32[]{:S(2)}) async-start(), calls=%async_computation.34 | async-start | bytes 2621440 | tf_op jit(solution)/shard_map/all_gather | solution.py:56
  1131.3 135.5 %reduce-scatter.36.cloned.1.call-start = ((), (), s32[]{:S(2)}) async-start(), calls=%async_computation.37 | async-start | bytes 2621440 | tf_op jit(solution)/shard_map/reduce_scatter | solution.py:60
  1271.7 140.0 %reduce-scatter.38.cloned.1.call-start = ((), (), s32[]{:S(2)}) async-start(), calls=%async_computation.39 | async-start | bytes 2621440 | tf_op jit(solution)/shard_map/reduce_scatter | solution.py:60
  1369.6 135.7 %all-gather.48.cloned.1.call-start = ((), (), s32[]{:S(2)}) async-start(), calls=%async_computation.41 | async-start | bytes 2621440 | tf_op jit(solution)/shard_map/all_gather | solution.py:56
  1422.0 135.3 %reduce-scatter.42.cloned.1.call-start = ((), (), s32[]{:S(2)}) async-start(), calls=%async_computation.44 | async-start | bytes 2621440 | tf_op jit(solution)/shard_map/reduce_scatter | solution.py:60
  1514.6 95.2 %all-gather.52.cloned.1.call-start = ((), (), s32[]{:S(2)}) async-start(), calls=%async_computation.45 | async-start | bytes 2621440 | tf_op jit(solution)/shard_map/all_gather | solution.py:56
  1564.4 101.1 %all-gather.30.cloned.1.call-start = ((), (), s32[]{:S(2)}) async-start(), calls=%async_computation.25 | async-start | bytes 2621440 | tf_op jit(solution)/shard_map/all_gather | solution.py:56
  1565.2 168.4 %reduce-scatter.44.cloned.1.call-start = ((), (), s32[]{:S(2)}) async-start(), calls=%async_computation.46 | async-start | bytes 2621440 | tf_op jit(solution)/shard_map/reduce_scatter | solution.py:60
  (122 other events, 3701.8 us)
Sparse Core Ops, SparseCore 0:
  11.6 48.6 all-gather.19
  88.8 42.5 reduce-scatter.15
  135.4 45.2 all-gather.21
  238.0 45.4 all-gather.23
  359.1 45.2 all-gather.25
  465.1 45.6 all-gather.27
  512.8 44.6 all-gather.31
  605.2 43.1 reduce-scatter.27
  654.5 45.2 all-gather.37
  701.8 44.6 all-gather.45
  747.9 44.6 all-gather.53
  794.0 44.6 all-gather.33
  886.3 43.1 reduce-scatter.39
  931.8 43.1 reduce-scatter.29
  981.2 45.2 all-gather.35
  1122.6 45.2 all-gather.41
  1170.0 44.6 all-gather.39
  1271.8 45.2 all-gather.43
  1413.1 45.2 all-gather.49
  1460.6 44.6 all-gather.47
  1564.5 45.2 all-gather.51
  1612.1 44.6 all-gather.29
  1665.6 42.6 reduce-scatter.43
  1710.4 43.5 reduce-scatter.25
  (9 shorter events, 382.7 us)
where the time goes:
time: 1770 us
  waiting for transfers between devices  1180 us (67%)
  matrix products  354 us (20%)
  other arithmetic  114 us (6%)
  local copies, waits for them, and re-layouts  48 us (3%)
  blocking collectives  43.6 us (2%)
    all_gather x18, waiting for transfers between devices, gather_rows(): return lax.all_gather(piece, 'mp', axis=1, tiled=True)  630 us
    reduce_scatter x15, waiting for transfers between devices, reduce_rows(): lax.psum_scatter(partial_sum.astype(jnp.bfloat16), 'mp', scatter_dimensio...  542 us
    dot_general x6, matrix products, attend(): jnp.einsum('shqk,skhd->sqhd', probs_low, value_rows, preferred_element_ty...  65.1 us
    sub x6, matrix products, attend(): raised = jnp.exp(scores - highest)  61.6 us
    convert_element_type x3, other arithmetic, attend_back(): grad_scores = (softmax_probs * (grad_probs - row_term)).astype(jnp.bfloat16)  39.8 us
  transfers between devices with their start and end apart: 37, of which 35 were waited for; matrix products, arithmetic and copies ran while one was open for 15% of the time, Pallas kernels for 0%

commit v1 on v0

--- a/solution.py
+++ b/solution.py
@@ -10,12 +10,6 @@
 
 EPSILON = 1e-05
 NEG_LARGE = -1e30
-
-
-def passed_along(x, axis, by):
-    length = lax.axis_size(axis)
-    pairs = [(i, i + by) for i in range(length) if 0 <= i + by < length]
-    return lax.ppermute(x, axis, pairs)
 
 
 def norm_rows(values, gain, shift):
@@ -188,7 +182,7 @@
     return (result, kept_values)
 
 
-def tensor_backward(own_rows, arriving, weights, prefix_kv, visible):
+def tensor_backward(own_rows, arriving, weights, kept_values):
     (
         attn_gain,
         attn_shift,
@@ -204,7 +198,6 @@
         down_bias,
         out_full,
     ) = weights
-    result, kept_values = tensor_forward(own_rows, weights, prefix_kv, visible)
     query_rows, key_rows, value_rows, softmax_probs, probs_low, after_attn, up_pre = kept_values
     gradient_gathered = gather_rows(arriving)
     gradient_activation = jnp.einsum(
@@ -250,12 +243,8 @@
     return (grad_input, prefix_g)
 
 
-def layer_step(own_rows, weights, prefix_use, visible):
-    return tensor_forward(own_rows, weights, prefix_use, visible)
-
-
-def layer_back(own_rows, arriving, weights, prefix_use, visible):
-    return tensor_backward(own_rows, arriving, weights, prefix_use, visible)
+def both_layers(piece):
+    return lax.all_gather(piece[0], "section", axis=0, tiled=False)
 
 
 def body(
@@ -280,10 +269,8 @@
     prefix_weight,
     prefix_bias,
 ):
-    sections = lax.axis_size("section")
+    layers = lax.axis_size("section")
     section_index = lax.axis_index("section")
-    micro_count = layer_input.shape[0]
-    tick_count = micro_count + sections - 1
     hidden_pre = jnp.dot(
         prefix_table, mid_weight, preferred_element_type=jnp.float32
     ) + mid_bias.astype(jnp.float32)
@@ -293,73 +280,50 @@
         jnp.dot(hidden_low, prefix_weight, preferred_element_type=jnp.float32)
         + prefix_bias.astype(jnp.float32)
     ).astype(jnp.bfloat16)
-    small_parts = (
-        attn_gain[0].astype(jnp.float32),
-        attn_shift[0].astype(jnp.float32),
-        out_bias[0].astype(jnp.float32),
-        ffn_gain[0].astype(jnp.float32),
-        ffn_shift[0].astype(jnp.float32),
-        down_bias[0].astype(jnp.float32),
-    )
-    weights = (
-        small_parts[0],
-        small_parts[1],
-        query_key_value_weight[0],
-        qkv_bias[0].astype(jnp.float32),
-        attention_output_weight[0],
-        small_parts[2],
-        small_parts[3],
-        small_parts[4],
-        up_projection_weight[0],
-        up_projection_bias[0].astype(jnp.float32),
-        down_projection_weight[0],
-        small_parts[5],
-        attention_output_weight[0],
-    )
-    first_row = 0
-    query_count = SEQ_LEN
-    received = jnp.zeros_like(layer_input[0])
-    entered = []
-    produced = []
-    for tick_index in range(tick_count):
-        batch_index = jnp.clip(tick_index - section_index, 0, micro_count - 1)
-        own_input = layer_input[min(tick_index, micro_count - 1)]
-        entering = jnp.where(section_index == 0, own_input, received)
-        lengths_now = lax.dynamic_index_in_dim(example_lengths, batch_index, 0, keepdims=False)
-        visible = visible_of(lengths_now, first_row, query_count)
-        result, kept_values = layer_step(entering.astype(jnp.float32), weights, prefix_kv, visible)
-        leaving = result.astype(jnp.bfloat16)
-        entered.append(entering)
-        produced.append(leaving)
-        if tick_index + 1 < tick_count:
-            received = passed_along(leaving, "section", 1)
-    kept_inputs = lax.dynamic_slice_in_dim(jnp.stack(entered), section_index, micro_count, 0)
-    activations = lax.dynamic_slice_in_dim(jnp.stack(produced), section_index, micro_count, 0)
-    back_offset = sections - 1 - section_index
-    received_grad = jnp.zeros_like(cotangent[0])
-    sent_grads = []
-    prefix_total = None
-    for tick_index in range(tick_count):
-        raw_index = tick_index - back_offset
-        is_valid = ((raw_index >= 0) & (raw_index < micro_count)).astype(jnp.float32)
-        batch_index = jnp.clip(raw_index, 0, micro_count - 1)
-        own_grad = cotangent[min(tick_index, micro_count - 1)]
-        arriving = jnp.where(section_index == sections - 1, own_grad, received_grad)
-        entering = lax.dynamic_index_in_dim(kept_inputs, batch_index, 0, keepdims=False)
-        lengths_now = lax.dynamic_index_in_dim(example_lengths, batch_index, 0, keepdims=False)
-        visible = visible_of(lengths_now, first_row, query_count)
-        grad_input, prefix_g = layer_back(
-            entering.astype(jnp.float32), arriving, weights, prefix_kv, visible
-        )
-        if tick_index == 0:
-            prefix_total = is_valid * prefix_g
-        else:
-            prefix_total = prefix_total + is_valid * prefix_g
-        sent_grads.append(grad_input)
-        if tick_index + 1 < tick_count:
-            received_grad = passed_along(grad_input, "section", -1)
-    input_grads = lax.dynamic_slice_in_dim(jnp.stack(sent_grads), back_offset, micro_count, 0)
-    prefix_sum = lax.psum(prefix_total, "dp")
+    prefix_all = lax.all_gather(prefix_kv, "section", axis=0, tiled=False)
+    floats = [
+        both_layers(piece).astype(jnp.float32)
+        for piece in (attn_gain, attn_shift, qkv_bias, out_bias, ffn_gain, ffn_shift,
+                      up_projection_bias, down_bias)
+    ]
+    matrices = [
+        both_layers(piece)
+        for piece in (query_key_value_weight, attention_output_weight,
+                      up_projection_weight, down_projection_weight)
+    ]
+
+    def weights_of(layer):
+        g1, s1, bq, bo, g2, s2, bu, bd = [piece[layer] for piece in floats]
+        wq, wo, wu, wd = [piece[layer] for piece in matrices]
+        return (g1, s1, wq, bq, wo, bo, g2, s2, wu, bu, wd, bd, wo)
+
+    batch_count = layer_input.shape[0]
+    own_input = lax.dynamic_index_in_dim(layer_input, section_index, 0, keepdims=False)
+    own_cotangent = lax.dynamic_index_in_dim(cotangent, section_index, 0, keepdims=False)
+    lengths = lax.dynamic_index_in_dim(example_lengths, section_index, 0, keepdims=False)
+    visible = visible_of(lengths, 0, SEQ_LEN)
+    entering = own_input
+    entered, produced, kept = [], [], []
+    for layer in range(layers):
+        entered.append(entering.astype(jnp.float32))
+        result, kept_values = tensor_forward(
+            entered[layer], weights_of(layer), prefix_all[layer], visible
+        )
+        entering = result.astype(jnp.bfloat16)
+        produced.append(entering)
+        kept.append(kept_values)
+    gradient = own_cotangent
+    sent_grads = [None] * layers
+    prefix_parts = [None] * layers
+    for layer in reversed(range(layers)):
+        gradient, prefix_parts[layer] = tensor_backward(
+            entered[layer], gradient, weights_of(layer), kept[layer]
+        )
+        sent_grads[layer] = gradient
+    activations = lax.all_to_all(jnp.stack(produced), "section", 0, 0, tiled=False)
+    input_grads = lax.all_to_all(jnp.stack(sent_grads), "section", 0, 0, tiled=False)
+    prefix_sum = lax.psum(jnp.stack(prefix_parts), ("dp", "section"))
+    prefix_sum = lax.dynamic_index_in_dim(prefix_sum, section_index, 0, keepdims=False)
     prefix_low = prefix_sum.astype(jnp.bfloat16)
     prefix_bias_grad = jnp.sum(prefix_low.astype(jnp.float32), axis=0)
     prefix_weight_grad = jnp.dot(hidden_low.T, prefix_low, preferred_element_type=jnp.float32)

time: 1770 us -> 1050 us (0.59)
  waiting for transfers between devices: 1180 us -> 671 us
  matrix products: 354 us -> 183 us
  other arithmetic: 114 us -> 64.9 us
  blocking collectives: 43.6 us -> 80.1 us
  local copies, waits for them, and re-layouts: 48 us -> 21.5 us
    all_gather x18 -> x8, waiting for transfers between devices: 630 us -> 352 us  [gather_rows(): return lax.all_gather(piece, 'mp', axis=1, tiled=True)]
    reduce_scatter x15 -> x8, waiting for transfers between devices: 542 us -> 290 us  [reduce_rows(): lax.psum_scatter(partial_sum.astype(jnp.bfloat16), 'mp', scatter_dimensio...]
    dot_general x6 -> x2, matrix products: 65.1 us -> 21.4 us  [attend(): jnp.einsum('shqk,skhd->sqhd', probs_low, value_rows, preferred_element_ty...]
    sub x6 -> x2, matrix products: 61.6 us -> 23.9 us  [attend(): raised = jnp.exp(scores - highest)]
    all_gather x0 -> x4, waiting for transfers between devices: none -> 26.1 us  [both_layers(): return lax.all_gather(piece[0], 'section', axis=0, tiled=False)]
    convert_element_type x3 -> x2, other arithmetic: 39.8 us -> 23.6 us  [attend_back(): grad_scores = (softmax_probs * (grad_probs - row_term)).astype(jnp.bfloat16)]
  transfers between devices with their start and end apart: 37 -> 20, of which waited for: 35 -> 18; matrix products, arithmetic and copies ran while one was open for 15% -> 7% of each run, Pallas kernels for 0% -> 0%
where the time goes in v1:
time: 1050 us; the launch traced here: 1040 us
  waiting for transfers between devices  671 us (64%)
  matrix products  183 us (17%)
  blocking collectives  80.1 us (8%)
  other arithmetic  64.9 us (6%)
  local copies, waits for them, and re-layouts  21.5 us (2%)
  between operations  15.3 us (1%)
    all_gather x8, waiting for transfers between devices, gather_rows(): return lax.all_gather(piece, 'mp', axis=1, tiled=True)  352 us
    reduce_scatter x8, waiting for transfers between devices, reduce_rows(): lax.psum_scatter(partial_sum.astype(jnp.bfloat16), 'mp', scatter_dimensio...  290 us
    psum x1, blocking collectives, body(): prefix_sum = lax.psum(jnp.stack(prefix_parts), ('dp', 'section'))  26.3 us
    all_gather x4, waiting for transfers between devices, both_layers(): return lax.all_gather(piece[0], 'section', axis=0, tiled=False)  26.1 us
    psum x1, blocking collectives, body(): hidden_grad = lax.psum(hidden_part, ('section', 'mp'))  26.1 us
    sub x2, matrix products, attend(): raised = jnp.exp(scores - highest)  23.9 us
    dot_general x2, matrix products, attend_back(): jnp.einsum('sqhd,skhd->shqk', grad_heads, value_rows, preferred_element_t...  23.6 us
    convert_element_type x2, other arithmetic, attend_back(): grad_scores = (softmax_probs * (grad_probs - row_term)).astype(jnp.bfloat16)  23.6 us
  transfers between devices with their start and end apart: 20, of which 18 were waited for; matrix products, arithmetic and copies ran while one was open for 7% of the time, Pallas kernels for 0%

profile of v1, /device:TPU:0, one launch (start us, length us, event | category | flops | bytes accessed | tf_op | source)
XLA Modules:
  0.0 1037.4 jit_solution(9193330081518600851)
XLA Ops:
  25.8 39.8 %all-gather.24.cloned.1.call-done = bf16[1,1024,1024]{2,1,0:T(8,128)(2,1)} async-done(((bf16[1,256,1024]{2,1,0:T(8,128)(2,1)}), bf16[1,1024,1024]{2,1,0:T(8,128)(2,1)}) %all-gather.24.cloned.1.call-update) | async-done | bytes 2097168 | tf_op jit(solution)/shard_map/all_gather | solution.py:50
  65.6 12.2 %all-gather.26.cloned.1.call-done = bf16[2,1024,768]{2,1,0:T(8,128)(2,1)} async-done(((bf16[1,1024,768]{2,1,0:T(8,128)(2,1)}), bf16[2,1024,768]{2,1,0:T(8,128)(2,1)}) %all-gather.26.cloned.1.call-update) | async-done | bytes 3145744 | tf_op jit(solution)/shard_map/all_gather | solution.py:247
  82.7 12.1 %fusion.183 = (f32[4,1024]{1,0:T(4,128)S(1)}, f32[4,1024,1034]{1,2,0:T(8,128)}) fusion(pred[1024,1034]{0,1:T(8,128)(4,1)} %pad_bitcast_fusion, bf16[1,1024,4,3,64]{1,4,3,2,0:T(8,128)(2,1)S(1)} %bitcast.380, bf16[1,1024,4,64]{1,3,2,0:T(8,128)(2,1)S(1)} %get-tuple-element.56, bf16[1,10,4,64]{1,3,2,0:T(8,128)(2,1)S(1)} %bitcast.393), kind=kOutput, calls=%fused_computation.274 | convolution fusion | flops 560114688 | bytes 19130368 | tf_op jit(solution)/shard_map/sub | solution.py:74
  114.9 39.1 %reduce-scatter.9.cloned.1.call-done = bf16[1,256,1024]{2,1,0:T(8,128)(2,1)} async-done(((bf16[1,1024,1024]{2,1,0:T(8,128)(2,1)}), bf16[1,256,1024]{2,1,0:T(8,128)(2,1)}) %reduce-scatter.9.cloned.1.call-update) | async-done | bytes 524304 | tf_op jit(solution)/shard_map/reduce_scatter | solution.py:54
  168.5 49.2 %all-gather.30.cloned.1.call-done = bf16[1,1024,1024]{2,1,0:T(8,128)(2,1)} async-done(((bf16[1,256,1024]{2,1,0:T(8,128)(2,1)}), bf16[1,1024,1024]{2,1,0:T(8,128)(2,1)}) %all-gather.30.cloned.1.call-update) | async-done | bytes 2097168 | tf_op jit(solution)/shard_map/all_gather | solution.py:50
  240.7 43.3 %reduce-scatter.11.cloned.1.call-done = bf16[1,256,1024]{2,1,0:T(8,128)(2,1)} async-done(((bf16[1,1024,1024]{2,1,0:T(8,128)(2,1)}), bf16[1,256,1024]{2,1,0:T(8,128)(2,1)}) %reduce-scatter.11.cloned.1.call-update) | async-done | bytes 524304 | tf_op jit(solution)/shard_map/reduce_scatter | solution.py:54
  287.3 45.0 %all-gather.36.cloned.1.call-done = bf16[1,1024,1024]{2,1,0:T(8,128)(2,1)} async-done(((bf16[1,256,1024]{2,1,0:T(8,128)(2,1)}), bf16[1,1024,1024]{2,1,0:T(8,128)(2,1)}) %all-gather.36.cloned.1.call-update) | async-done | bytes 2097168 | tf_op jit(solution)/shard_map/all_gather | solution.py:50
  338.4 11.8 %fusion.184 = (f32[4,1024]{1,0:T(4,128)S(1)}, f32[4,1024,1034]{1,2,0:T(8,128)}) fusion(pred[1024,1034]{0,1:T(8,128)(4,1)} %pad_bitcast_fusion, bf16[1,1024,4,3,64]{1,4,3,2,0:T(8,128)(2,1)} %bitcast.385, bf16[1,1024,4,64]{1,3,2,0:T(8,128)(2,1)} %get-tuple-element.54, bf16[1,10,4,64]{1,3,2,0:T(8,128)(2,1)S(1)} %bitcast.397), kind=kOutput, calls=%fused_computation.275 | convolution fusion | flops 560114688 | bytes 19076096 | tf_op jit(solution)/shard_map/sub | solution.py:74
  364.6 42.5 %reduce-scatter.13.cloned.1.call-done = bf16[1,256,1024]{2,1,0:T(8,128)(2,1)} async-done(((bf16[1,1024,1024]{2,1,0:T(8,128)(2,1)}), bf16[1,256,1024]{2,1,0:T(8,128)(2,1)}) %reduce-scatter.13.cloned.1.call-update) | async-done | bytes 524304 | tf_op jit(solution)/shard_map/reduce_scatter | solution.py:54
  413.9 43.4 %all-gather.38.cloned.1.call-done = bf16[1,1024,1024]{2,1,0:T(8,128)(2,1)} async-done(((bf16[1,256,1024]{2,1,0:T(8,128)(2,1)}), bf16[1,1024,1024]{2,1,0:T(8,128)(2,1)}) %all-gather.38.cloned.1.call-update) | async-done | bytes 2097168 | tf_op jit(solution)/shard_map/all_gather | solution.py:50
  463.9 39.6 %all-gather.46.cloned.1.call-done = bf16[1,1,1024,1024]{3,2,1,0:T(8,128)(2,1)} async-done(((bf16[1,1,256,1024]{3,2,1,0:T(8,128)(2,1)}), bf16[1,1,1024,1024]{3,2,1,0:T(8,128)(2,1)}) %all-gather.46.cloned.1.call-update) | async-done | bytes 2097168 | tf_op jit(solution)/shard_map/all_gather | solution.py:50
  521.6 35.6 %reduce-scatter.17.cloned.1.call-done = bf16[1,256,1024]{2,1,0:T(8,128)(2,1)} async-done(((bf16[1,1024,1024]{2,1,0:T(8,128)(2,1)}), bf16[1,256,1024]{2,1,0:T(8,128)(2,1)}) %reduce-scatter.17.cloned.1.call-update) | async-done | bytes 524304 | tf_op jit(solution)/shard_map/reduce_scatter | solution.py:54
  558.9 43.7 %reduce-scatter.15.cloned.1.call-done = bf16[1,256,1024]{2,1,0:T(8,128)(2,1)} async-done(((bf16[1,1024,1024]{2,1,0:T(8,128)(2,1)}), bf16[1,256,1024]{2,1,0:T(8,128)(2,1)}) %reduce-scatter.15.cloned.1.call-update) | async-done | bytes 524304 | tf_op jit(solution)/shard_map/reduce_scatter | solution.py:54
  607.9 45.0 %all-gather.40.cloned.1.call-done = bf16[1,1024,1024]{2,1,0:T(8,128)(2,1)} async-done(((bf16[1,256,1024]{2,1,0:T(8,128)(2,1)}), bf16[1,1024,1024]{2,1,0:T(8,128)(2,1)}) %all-gather.40.cloned.1.call-update) | async-done | bytes 2097168 | tf_op jit(solution)/shard_map/all_gather | solution.py:50
  666.9 11.7 %multiply_reduce_fusion.1 = (f32[4,1024]{1,0:T(4,128)S(1)}, f32[4,1024,1034]{1,2,0:T(8,128)}) fusion(f32[4,1024,1034]{1,2,0:T(8,128)} %get-tuple-element.82, f32[4,1024]{1,0:T(4,128)S(1)} %get-tuple-element.81, bf16[1024,4,64]{0,2,1:T(8,128)(2,1)} %bitcast.452, bf16[1,1024,4,64]{1,3,2,0:T(8,128)(2,1)} %get-tuple-element.55, ...), kind=kOutput, calls=%fused_computation.11 | convolution fusion | flops 555874304 | bytes 34968576 | tf_op jit(solution)/shard_map/sqhd,skhd->shqk/dot_general | solution.py:89
  678.6 11.8 %multiply_convert_fusion.1 = bf16[4,1024,1034]{1,2,0:T(8,128)(2,1)S(1)} fusion(f32[4,1024,1034]{1,2,0:T(8,128)} %get-tuple-element.84, f32[4,1024]{1,0:T(4,128)S(1)} %get-tuple-element.83, f32[4,1024,1034]{1,2,0:T(8,128)} %get-tuple-element.82, f32[4,1024]{1,0:T(4,128)S(1)} %get-tuple-element.81), kind=kLoop, calls=%fused_computation.10 | loop fusion | flops 16941056 | bytes 42385408 | tf_op jit(solution)/shard_map/convert_element_type | solution.py:96
  702.0 42.7 %reduce-scatter.19.cloned.1.call-done = bf16[1,256,1024]{2,1,0:T(8,128)(2,1)} async-done(((bf16[1,1024,1024]{2,1,0:T(8,128)(2,1)}), bf16[1,256,1024]{2,1,0:T(8,128)(2,1)}) %reduce-scatter.19.cloned.1.call-update) | async-done | bytes 524304 | tf_op jit(solution)/shard_map/reduce_scatter | solution.py:54
  750.4 45.1 %all-gather.42.cloned.1.call-done = bf16[1,1024,1024]{2,1,0:T(8,128)(2,1)} async-done(((bf16[1,256,1024]{2,1,0:T(8,128)(2,1)}), bf16[1,1024,1024]{2,1,0:T(8,128)(2,1)}) %all-gather.42.cloned.1.call-update) | async-done | bytes 2097168 | tf_op jit(solution)/shard_map/all_gather | solution.py:50
  806.6 42.7 %reduce-scatter.21.cloned.1.call-done = bf16[1,256,1024]{2,1,0:T(8,128)(2,1)} async-done(((bf16[1,1024,1024]{2,1,0:T(8,128)(2,1)}), bf16[1,256,1024]{2,1,0:T(8,128)(2,1)}) %reduce-scatter.21.cloned.1.call-update) | async-done | bytes 524304 | tf_op jit(solution)/shard_map/reduce_scatter | solution.py:54
  853.7 45.1 %all-gather.44.cloned.1.call-done = bf16[1,1024,1024]{2,1,0:T(8,128)(2,1)} async-done(((bf16[1,256,1024]{2,1,0:T(8,128)(2,1)}), bf16[1,1024,1024]{2,1,0:T(8,128)(2,1)}) %all-gather.44.cloned.1.call-update) | async-done | bytes 2097168 | tf_op jit(solution)/shard_map/all_gather | solution.py:50
  912.8 12.0 %multiply_reduce_fusion = (f32[4,1024]{1,0:T(4,128)S(1)}, f32[4,1024,1034]{1,2,0:T(8,128)}) fusion(f32[4,1024,1034]{1,2,0:T(8,128)} %get-tuple-element.80, f32[4,1024]{1,0:T(4,128)S(1)} %copy-done.33, bf16[1024,4,64]{0,2,1:T(8,128)(2,1)} %bitcast.450, bf16[1,1024,4,64]{1,3,2,0:T(8,128)(2,1)} %get-tuple-element.57, bf16[1,10,4,64]{1,3,2,0:T(8,128)(2,1)S(1)} %bitcast.427), kind=kOutput, calls=%fused_computation.9 | convolution fusion | flops 555874304 | bytes 34968576 | tf_op jit(solution)/shard_map/sqhd,skhd->shqk/dot_general | solution.py:89
  924.8 11.8 %multiply_convert_fusion = bf16[4,1024,1034]{1,2,0:T(8,128)(2,1)S(1)} fusion(f32[4,1024,1034]{1,2,0:T(8,128)} %get-tuple-element.86, f32[4,1024]{1,0:T(4,128)S(1)} %get-tuple-element.85, f32[4,1024,1034]{1,2,0:T(8,128)} %get-tuple-element.80, f32[4,1024]{1,0:T(4,128)S(1)} %copy-done.33), kind=kLoop, calls=%fused_computation.8 | loop fusion | flops 16941056 | bytes 42385408 | tf_op jit(solution)/shard_map/convert_element_type | solution.py:96
  957.7 26.3 %psum.14 = bf16[2,10,512]{2,1,0:T(8,128)(2,1)S(1)} all-reduce(f32[2,10,512]{2,1,0:T(8,128)S(1)} %pad_maximum_fusion.6), channel_id=1, replica_groups=mesh['section'=2,'dp'=4,'mp'=4] {'dp','section'}, use_global_device_ids=true, to_apply=%region_32.33 | all-reduce | flops 10240 | bytes 61440 | tf_op jit(solution)/shard_map/psum | solution.py:325
  984.8 26.1 %psum.15 = f32[10,512]{1,0:T(8,128)S(1)} all-reduce(f32[10,512]{1,0:T(8,128)S(1)} %fusion.185), channel_id=1, replica_groups=mesh['section'=2,'dp'=4,'mp'=4] {'section','mp'}, use_global_device_ids=true, to_apply=%region_33.34 | all-reduce | flops 5120 | bytes 40960 | tf_op jit(solution)/shard_map/psum | solution.py:331
  (281 shorter events, 244.6 us)
Async XLA Ops:
  7.2 58.4 %all-gather.24.cloned.1.call-start = ((), (), s32[]{:S(2)}) async-start(), calls=%async_computation.10 | async-start | bytes 2621440 | tf_op jit(solution)/shard_map/all_gather | solution.py:50
  16.7 61.0 %all-gather.26.cloned.1.call-start = ((), (), s32[]{:S(2)}) async-start(), calls=%async_computation.11 | async-start | bytes 4718592 | tf_op jit(solution)/shard_map/all_gather | solution.py:247
  17.5 87.9 %all-gather.28.cloned.1.call-start = ((), (), s32[]{:S(2)}) async-start(), calls=%async_computation.12 | async-start | bytes 1572864 | tf_op jit(solution)/shard_map/all_gather | solution.py:247
  18.2 135.8 %reduce-scatter.9.cloned.1.call-start = ((), (), s32[]{:S(2)}) async-start(), calls=%async_computation.13 | async-start | bytes 2621440 | tf_op jit(solution)/shard_map/reduce_scatter | solution.py:54
  108.8 59.7 %all-gather.32.cloned.1.call-start = ((), (), s32[]{:S(2)}) async-start(), calls=%async_computation.15 | async-start | bytes 6291456 | tf_op jit(solution)/shard_map/all_gather | solution.py:247
  109.4 108.3 %all-gather.30.cloned.1.call-start = ((), (), s32[]{:S(2)}) async-start(), calls=%async_computation.14 | async-start | bytes 2621440 | tf_op jit(solution)/shard_map/all_gather | solution.py:50
  114.9 109.4 %copy-start.24 = (f32[1,1,1024]{2,1,0:T(1,128)}, f32[1,1,1024]{2,1,0:T(1,128)S(1)}, u32[]{:S(2)}) copy-start(f32[1,1,1024]{2,1,0:T(1,128)S(1)} %get-tuple-element.75) | copy-start | bytes 12292
  158.9 72.9 %all-gather.34.cloned.1.call-start = ((), (), s32[]{:S(2)}) async-start(), calls=%async_computation.16 | async-start | bytes 6291456 | tf_op jit(solution)/shard_map/all_gather | solution.py:247
  159.7 124.4 %reduce-scatter.11.cloned.1.call-start = ((), (), s32[]{:S(2)}) async-start(), calls=%async_computation.17 | async-start | bytes 2621440 | tf_op jit(solution)/shard_map/reduce_scatter | solution.py:54
  238.8 93.4 %all-gather.36.cloned.1.call-start = ((), (), s32[]{:S(2)}) async-start(), calls=%async_computation.18 | async-start | bytes 2621440 | tf_op jit(solution)/shard_map/all_gather | solution.py:50
  286.8 120.2 %reduce-scatter.13.cloned.1.call-start = ((), (), s32[]{:S(2)}) async-start(), calls=%async_computation.19 | async-start | bytes 2621440 | tf_op jit(solution)/shard_map/reduce_scatter | solution.py:54
  364.3 93.0 %all-gather.38.cloned.1.call-start = ((), (), s32[]{:S(2)}) async-start(), calls=%async_computation.20 | async-start | bytes 2621440 | tf_op jit(solution)/shard_map/all_gather | solution.py:50
  411.9 91.6 %all-gather.46.cloned.1.call-start = ((), (), s32[]{:S(2)}) async-start(), calls=%async_computation.29 | async-start | bytes 2621440 | tf_op jit(solution)/shard_map/all_gather | solution.py:50
  413.8 143.4 %reduce-scatter.17.cloned.1.call-start = ((), (), s32[]{:S(2)}) async-start(), calls=%async_computation.22 | async-start | bytes 2621440 | tf_op jit(solution)/shard_map/reduce_scatter | solution.py:54
  514.5 88.1 %reduce-scatter.15.cloned.1.call-start = ((), (), s32[]{:S(2)}) async-start(), calls=%async_computation.21 | async-start | bytes 2621440 | tf_op jit(solution)/shard_map/reduce_scatter | solution.py:54
  521.6 131.2 %all-gather.40.cloned.1.call-start = ((), (), s32[]{:S(2)}) async-start(), calls=%async_computation.23 | async-start | bytes 2621440 | tf_op jit(solution)/shard_map/all_gather | solution.py:50
  607.4 137.3 %reduce-scatter.19.cloned.1.call-start = ((), (), s32[]{:S(2)}) async-start(), calls=%async_computation.24 | async-start | bytes 2621440 | tf_op jit(solution)/shard_map/reduce_scatter | solution.py:54
  702.0 93.5 %all-gather.42.cloned.1.call-start = ((), (), s32[]{:S(2)}) async-start(), calls=%async_computation.25 | async-start | bytes 2621440 | tf_op jit(solution)/shard_map/all_gather | solution.py:50
  750.1 99.2 %copy-start.25 = (f32[1,1,1024]{2,1,0:T(1,128)S(1)}, f32[1,1,1024]{2,1,0:T(1,128)}, u32[]{:S(2)}) copy-start(f32[1,1,1024]{2,1,0:T(1,128)} %copy-done.24) | copy-start | bytes 12292
  750.1 100.7 %copy-start.41 = (f32[256]{0:T(256)S(1)}, f32[256]{0:T(256)}, u32[]{:S(2)}) copy-start(f32[256]{0:T(256)} %copy-done.40) | copy-start | bytes 3076
  750.1 100.7 %copy-start.39 = (f32[256]{0:T(256)S(1)}, f32[256]{0:T(256)}, u32[]{:S(2)}) copy-start(f32[256]{0:T(256)} %copy-done.38) | copy-start | bytes 3076
  750.1 99.1 %reduce-scatter.21.cloned.1.call-start = ((), (), s32[]{:S(2)}) async-start(), calls=%async_computation.26 | async-start | bytes 2621440 | tf_op jit(solution)/shard_map/reduce_scatter | solution.py:54
  806.5 92.3 %all-gather.44.cloned.1.call-start = ((), (), s32[]{:S(2)}) async-start(), calls=%async_computation.27 | async-start | bytes 2621440 | tf_op jit(solution)/shard_map/all_gather | solution.py:50
  853.4 165.2 %reduce-scatter.23.cloned.1.call-start = ((), (), s32[]{:S(2)}) async-start(), calls=%async_computation.28 | async-start | bytes 2621440 | tf_op jit(solution)/shard_map/reduce_scatter | solution.py:54
  (49 other events, 1057.1 us)
Sparse Core Ops, SparseCore 0:
  16.9 48.6 all-gather.23
  67.1 10.5 all-gather.25
  79.3 10.1 all-gather.27
  108.9 45.0 reduce-scatter.8
  155.5 12.9 all-gather.31
  170.6 47.0 all-gather.29
  219.3 12.3 all-gather.33
  238.9 45.0 reduce-scatter.10
  287.0 45.2 all-gather.35
  364.4 42.5 reduce-scatter.12
  412.0 45.2 all-gather.37
  458.8 44.6 all-gather.45
  514.6 42.5 reduce-scatter.16
  559.4 43.1 reduce-scatter.14
  607.5 45.2 all-gather.39
  702.1 42.5 reduce-scatter.18
  750.2 45.2 all-gather.41
  806.6 42.5 reduce-scatter.20
  853.5 45.2 all-gather.43
  947.8 42.6 reduce-scatter.22

commit v2 on v1

--- a/solution.py
+++ b/solution.py
@@ -1,6 +1,8 @@
 import jax
 import jax.numpy as jnp
 from jax import lax
+from jax.experimental import pallas as pl
+from jax.experimental.pallas import tpu as pltpu
 from jax.sharding import PartitionSpec as P
 
 HEAD_DIM = 64
@@ -10,6 +12,8 @@
 
 EPSILON = 1e-05
 NEG_LARGE = -1e30
+GELU_A = 0.7978845608028654
+GELU_B = 0.044715
 
 
 def norm_rows(values, gain, shift):
@@ -241,6 +245,19 @@
     grad_input = norm_input_grad(own_rows, attn_gain, attn_shift, grad_one)
     grad_input = (grad_input + grad_mid.astype(jnp.float32)).astype(jnp.bfloat16)
     return (grad_input, prefix_g)
+
+
+def prefix_back(prefix_sum, hidden_act, hidden_low, prefix_table, mid_weight, prefix_weight):
+    prefix_low = prefix_sum.astype(jnp.bfloat16)
+    prefix_bias_grad = jnp.sum(prefix_low.astype(jnp.float32), axis=0)
+    prefix_weight_grad = jnp.dot(hidden_low.T, prefix_low, preferred_element_type=jnp.float32)
+    hidden_part = jnp.dot(prefix_low, prefix_weight.T, preferred_element_type=jnp.float32)
+    hidden_grad = lax.psum(hidden_part, ("section", "mp"))
+    pre_grad = (hidden_grad * (1.0 - hidden_act * hidden_act)).astype(jnp.bfloat16)
+    mid_bias_grad = jnp.sum(pre_grad.astype(jnp.float32), axis=0)
+    mid_weight_grad = jnp.dot(prefix_table.T, pre_grad, preferred_element_type=jnp.float32)
+    table_grad = jnp.dot(pre_grad, mid_weight.T, preferred_element_type=jnp.float32)
+    return (table_grad, mid_weight_grad, mid_bias_grad, prefix_weight_grad, prefix_bias_grad)
 
 
 def both_layers(piece):
@@ -324,23 +341,634 @@
     input_grads = lax.all_to_all(jnp.stack(sent_grads), "section", 0, 0, tiled=False)
     prefix_sum = lax.psum(jnp.stack(prefix_parts), ("dp", "section"))
     prefix_sum = lax.dynamic_index_in_dim(prefix_sum, section_index, 0, keepdims=False)
-    prefix_low = prefix_sum.astype(jnp.bfloat16)
-    prefix_bias_grad = jnp.sum(prefix_low.astype(jnp.float32), axis=0)
-    prefix_weight_grad = jnp.dot(hidden_low.T, prefix_low, preferred_element_type=jnp.float32)
-    hidden_part = jnp.dot(prefix_low, prefix_weight.T, preferred_element_type=jnp.float32)
-    hidden_grad = lax.psum(hidden_part, ("section", "mp"))
-    pre_grad = (hidden_grad * (1.0 - hidden_act * hidden_act)).astype(jnp.bfloat16)
-    mid_bias_grad = jnp.sum(pre_grad.astype(jnp.float32), axis=0)
-    mid_weight_grad = jnp.dot(prefix_table.T, pre_grad, preferred_element_type=jnp.float32)
-    table_grad = jnp.dot(pre_grad, mid_weight.T, preferred_element_type=jnp.float32)
-    return (
-        activations[None],
-        input_grads[None],
-        table_grad,
-        mid_weight_grad,
-        mid_bias_grad,
-        prefix_weight_grad,
-        prefix_bias_grad,
+    return (activations[None], input_grads[None]) + prefix_back(
+        prefix_sum, hidden_act, hidden_low, prefix_table, mid_weight, prefix_weight
+    )
+
+
+MESH = pl.DeviceIdType.MESH
+BLOCK = 256
+LOG2E = 1.4426950408889634
+CHUNK = 32
+
+
+def role_of(z):
+    return (((z + 1) // 2) + 1) % 2
+
+
+def block_of(s, j):
+    return j * 3 + s * (1 - 2 * j)
+
+
+def core_of(block):
+    return ((block + 1) // 2) % 2
+
+
+def guarded(when, action):
+    if when is None:
+        action()
+    else:
+        pl.when(when)(action)
+
+
+def dot_nn(a, b):
+    return lax.dot_general(a, b, (((1,), (0,)), ((), ())), preferred_element_type=jnp.float32)
+
+
+def dot_nt(a, b):
+    return lax.dot_general(a, b, (((1,), (1,)), ((), ())), preferred_element_type=jnp.float32)
+
+
+def dot_tn(a, b):
+    return lax.dot_general(a, b, (((0,), (0,)), ((), ())), preferred_element_type=jnp.float32)
+
+
+class Sends:
+    def __init__(self, sems):
+        self.sems, self.used, self.pending = sems, 0, []
+
+    def start(self, src, dst, recv_sem, target, when=None):
+        copy = pltpu.make_async_remote_copy(
+            src_ref=src, dst_ref=dst, send_sem=self.sems.at[self.used], recv_sem=recv_sem,
+            device_id=target, device_id_type=MESH,
+        )
+        self.used += 1
+        guarded(when, copy.start)
+        self.pending.append((when, copy))
+
+    def start_or_keep(self, src, dst, recv_sem, target, is_here):
+        @pl.when(is_here)
+        def _():
+            pltpu.make_async_copy(src, dst, recv_sem).start()
+
+        self.start(src, dst, recv_sem, target, when=jnp.logical_not(is_here))
+
+    def finish(self):
+        for when, copy in self.pending:
+            guarded(when, copy.wait_send)
+        self.pending = []
+
+
+def layer_kernel(
+    x_hbm, cot_hbm, wq_hbm, wo_hbm, wu_hbm, wd_hbm, vec_hbm, pre_hbm, ends,
+    act_out, ig_out, pg_out,
+    wq, wo, wu, wd, vec, pre,
+    x_in, g_in, y_out, normed, kv, q_own, o_own, lse, bias, after, acc, slope, wide,
+    ts, m_acc, l_acc, o_acc, dk_acc, dv_acc, dkv_own, dkv_send, dkv_recv, kp, vp, pk_acc, pv_acc, gt,
+    ssem, vec_sem, pre_sem, x_sem, g_sem, act_sem, ig_sem, own_sem, z_sem, a_sem, b_sem, c_sem,
+    kv_ssem, kv_rsem, dkv_ssem, dkv_rsem,
+):
+    s, d, z = lax.axis_index("section"), lax.axis_index("dp"), lax.axis_index("mp")
+    role, micro = role_of(z), z // 2
+    other = 1 - s
+    partner = z + 1 - 2 * (z % 2)
+    x_near, y_near = d + 1 - 2 * (d % 2), (d + 2) % 4
+    near1 = jnp.where(s == 0, x_near, y_near)
+    near2 = jnp.where(s == 0, y_near, x_near)
+    sends = Sends(ssem)
+
+    barrier = pltpu.get_barrier_semaphore()
+    for ds in range(2):
+        for dz in range(4):
+            if ds or dz:
+                pl.semaphore_signal(barrier, inc=1, device_id=((s + ds) % 2, d, (z + dz) % 4), device_id_type=MESH)
+    for near in (x_near, y_near):
+        pl.semaphore_signal(barrier, inc=1, device_id=(s, near, z), device_id_type=MESH)
+    pl.semaphore_wait(barrier, 9)
+
+    def arrived(dst, sem):
+        pltpu.make_async_remote_copy(
+            src_ref=dst, dst_ref=dst, send_sem=ssem.at[0], recv_sem=sem,
+            device_id=(other, d, z), device_id_type=MESH,
+        ).wait_recv()
+
+    low_plane, high_plane = jnp.where(s == 0, 1, 0), jnp.where(s == 0, 2, 3)
+    planes = (low_plane, high_plane)
+    owner = core_of(z)
+    mine = s == owner
+    for k, chip in ((0, 1), (1, 2)):
+        slot = pl.ds(pl.multiple_of((z // 2) * BLOCK, BLOCK), BLOCK)
+        target = (s, d, chip)
+        is_here = z == chip
+
+        @pl.when(jnp.logical_and(mine, is_here))
+        def _():
+            pltpu.make_async_copy(x_hbm.at[k], x_in.at[slot], x_sem.at[z // 2]).start()
+
+        sends.start(x_hbm.at[k], x_in.at[slot], x_sem.at[z // 2], target,
+                    when=jnp.logical_and(mine, jnp.logical_not(is_here)))
+    for t in planes:
+        for h in range(2):
+            is_here = jnp.logical_and(z == t, s == h)
+            sends.start_or_keep(vec_hbm, vec.at[z], vec_sem.at[z], (h, d, t), is_here)
+            sends.start_or_keep(pre_hbm, pre.at[z], pre_sem.at[z], (h, d, t), is_here)
+    matrices = ((wq_hbm, wq), (wo_hbm, wo), (wu_hbm, wu), (wd_hbm, wd))
+    swapped = (d % 2) * 2 + d // 2
+
+    def part(w, h):
+        rows = matrices[w][1].shape[1] // 8
+        place = swapped if h else d
+        return pl.ds(pl.multiple_of((place + 4 * h) * rows, rows), rows)
+
+    for w, (held, full) in enumerate(matrices):
+        for t in planes:
+            for h in range(2):
+                sends.start(held.at[part(w, h)], full.at[z, part(w, h)], z_sem.at[w, z], (h, d, t), when=z != t)
+
+        @pl.when(role == s)
+        def _():
+            pltpu.make_async_copy(held, full.at[z], own_sem.at[w]).start()
+
+        sends.start(held, full.at[z], own_sem.at[w], (other, d, z), when=role == s)
+    for k, chip in ((0, 0), (1, 3)):
+        slot = pl.ds(pl.multiple_of((z // 2) * BLOCK, BLOCK), BLOCK)
+        is_here = z == chip
+
+        @pl.when(jnp.logical_and(mine, is_here))
+        def _():
+            pltpu.make_async_copy(cot_hbm.at[k], g_in.at[slot], g_sem.at[z // 2]).start()
+
+        sends.start(cot_hbm.at[k], g_in.at[slot], g_sem.at[z // 2], (s, d, chip),
+                    when=jnp.logical_and(mine, jnp.logical_not(is_here)))
+
+    place = jnp.where(s == 0, d, swapped)
+
+    def mine_part(w, start, count):
+        rows = matrices[w][1].shape[1] // 8
+        return pl.ds(pl.multiple_of((start + 4 * s) * rows, rows), rows * count)
+
+    units = [(w, i) for w in (0, 1) for i in range(1, 4)] + [(w, i) for i in range(1, 4) for w in (2, 3)]
+
+    def piece(w, i, start, count):
+        return matrices[w][1].at[(z + i) % 4, mine_part(w, start, count)]
+
+    pair_start = (place // 2) * 2
+    far_start = 2 - pair_start
+
+    def relay(step):
+        stages = [units[step - k] if 0 <= step - k < len(units) else None for k in range(4)]
+        if stages[0]:
+            w, i = stages[0]
+            q = (z + i) % 4
+            arrived(piece(w, i, place, 1), z_sem.at[w, q])
+            sends.start(piece(w, i, place, 1), piece(w, i, place, 1), a_sem.at[w, q], (s, near1, z))
+        if stages[1]:
+            w, i = stages[1]
+            q = (z + i) % 4
+            arrived(piece(w, i, pair_start + 1 - place % 2, 1), a_sem.at[w, q])
+            sends.start(piece(w, i, pair_start, 2), piece(w, i, pair_start, 2), b_sem.at[w, q], (s, near2, z))
+        if stages[2]:
+            w, i = stages[2]
+            q = (z + i) % 4
+            arrived(piece(w, i, far_start, 2), b_sem.at[w, q])
+            sends.start(piece(w, i, 0, 4), piece(w, i, 0, 4), c_sem.at[w, q], (other, d, z))
+        if stages[3]:
+            w, i = stages[3]
+            q = (z + i) % 4
+            rows = matrices[w][1].shape[1] // 2
+            half = pl.ds(pl.multiple_of(other * rows, rows), rows)
+            arrived(matrices[w][1].at[q, half], c_sem.at[w, q])
+
+    for step in range(len(units) + 3):
+        relay(step)
+    for w, (held, full) in enumerate(matrices):
+        arrived(full.at[z], own_sem.at[w])
+    for q in range(4):
+        arrived(vec.at[q], vec_sem.at[q])
+        arrived(pre.at[q], pre_sem.at[q])
+
+    first16 = lax.broadcasted_iota(jnp.int32, (16, 128), 1) < HEAD_DIM
+    first = lax.broadcasted_iota(jnp.int32, (BLOCK, 128), 1) < HEAD_DIM
+    lane = lax.broadcasted_iota(jnp.int32, (1, 128), 1)
+    half0 = jnp.where(lane < HEAD_DIM, 1.0, 0.0).astype(jnp.bfloat16)
+    half1 = jnp.where(lane < HEAD_DIM, 0.0, 1.0).astype(jnp.bfloat16)
+    pre_mask = jnp.where(lane % HEAD_DIM < PREFIX, 0.0, NEG_LARGE)
+    kp[...] = jnp.zeros(kp.shape, kp.dtype)
+    vp[...] = jnp.zeros(vp.shape, vp.dtype)
+    for q in range(4):
+        for p in range(2):
+            t0 = pre[q, :, p * 256 : p * 256 + 128].astype(jnp.float32)
+            t1 = pre[q, :, p * 256 + 128 : p * 256 + 256].astype(jnp.float32)
+            kp[2 * q + p, 0:16, :] = jnp.where(first16, t0, 0.0).astype(jnp.bfloat16)
+            kp[2 * q + p, 64:80, :] = jnp.where(first16, 0.0, pltpu.roll(t1, 64, 1)).astype(jnp.bfloat16)
+            vp[2 * q + p, 0:16, :] = jnp.where(first16, pltpu.roll(t0, 64, 1), 0.0).astype(jnp.bfloat16)
+            vp[2 * q + p, 64:80, :] = jnp.where(first16, 0.0, t1).astype(jnp.bfloat16)
+
+    for j in range(2):
+        row0 = block_of(s, j) * BLOCK
+        row_at = row0 + lax.broadcasted_iota(jnp.int32, (BLOCK, 1), 0)
+        begin = jnp.zeros((BLOCK, 1), jnp.int32)
+        for e in range(ends.shape[1]):
+            begin = jnp.where(row_at >= ends[micro, e], ends[micro, e], begin)
+
+        def mask_block(kb, carry):
+            key_at = kb * BLOCK + lax.broadcasted_iota(jnp.int32, (BLOCK, BLOCK), 1)
+            keep = jnp.logical_and(key_at <= row_at, key_at >= begin)
+            bias[j, kb] = jnp.where(keep, 0.0, NEG_LARGE)
+            return carry
+
+        lax.fori_loop(0, 4, mask_block, 0)
+
+    def vector(k, q=0, width=1024):
+        return vec[q, k : k + 1, 0:width]
+
+    rows_total = 2 * BLOCK
+    chunks = rows_total // CHUNK
+
+    def over_rows(action, start=0, stop=chunks):
+        def one(c, carry):
+            action(pl.ds(pl.multiple_of(c * CHUNK, CHUNK), CHUNK))
+            return carry
+
+        lax.fori_loop(start, stop, one, 0)
+
+    def standardize(v):
+        average = jnp.mean(v, axis=-1, keepdims=True)
+        centred = v - average
+        spread = jnp.mean(centred * centred, axis=-1, keepdims=True)
+        return centred, lax.rsqrt(spread + EPSILON)
+
+    def norm_back(v, gain, incoming):
+        centred, inverse = standardize(v)
+        xhat = centred * inverse
+        e = incoming * gain
+        return (e - jnp.mean(e, axis=-1, keepdims=True) - xhat * jnp.mean(e * xhat, axis=-1, keepdims=True)) * inverse
+
+    def columns(n, width=256):
+        return pl.ds(pl.multiple_of(n * width, width), width)
+
+    for j in range(2):
+        arrived(x_in.at[j * BLOCK : (j + 1) * BLOCK], x_sem.at[j])
+
+    def norm_one(rows):
+        centred, inverse = standardize(x_in[rows, :].astype(jnp.float32))
+        normed[rows, :] = (centred * inverse * vector(0) + vector(1)).astype(jnp.bfloat16)
+
+    over_rows(norm_one)
+    first_all = lax.broadcasted_iota(jnp.int32, (rows_total, 128), 1) < HEAD_DIM
+
+    def project(q, carry):
+        triple = dot_nn(normed[...], wq[q]) + vec[q, 7:8, 0:768]
+        for p in range(2):
+            t0, t1, t2 = (triple[:, p * 384 + n * 128 : p * 384 + n * 128 + 128] for n in range(3))
+            q_own[2 * q + p] = jnp.where(first_all, t0, t1).astype(jnp.bfloat16)
+            kv[s, 2 * q + p, 0] = pltpu.roll(jnp.where(first_all, t2, t0), 64, 1).astype(jnp.bfloat16)
+            kv[s, 2 * q + p, 1] = jnp.where(first_all, t1, t2).astype(jnp.bfloat16)
+        pltpu.make_async_remote_copy(
+            src_ref=kv.at[s, pl.ds(2 * q, 2)], dst_ref=kv.at[s, pl.ds(2 * q, 2)],
+            send_sem=kv_ssem.at[q], recv_sem=kv_rsem.at[q], device_id=(other, d, z), device_id_type=MESH,
+        ).start()
+        return carry
+
+    lax.fori_loop(0, 4, project, 0)
+
+    def kv_wait(q, carry):
+        pltpu.make_async_remote_copy(
+            src_ref=kv.at[s, pl.ds(2 * q, 2)], dst_ref=kv.at[other, pl.ds(2 * q, 2)],
+            send_sem=kv_ssem.at[q], recv_sem=kv_rsem.at[q], device_id=(other, d, z), device_id_type=MESH,
+        ).wait()
+        return carry
+
+    lax.fori_loop(0, 4, kv_wait, 0)
+
+    scale = LOG2E * HEAD_DIM ** (-0.5)
+
+    def key_rows(kb):
+        return pl.ds(pl.multiple_of((kb // 2) * BLOCK, BLOCK), BLOCK)
+
+    def attend_pair(pair, carry):
+        cols = columns(pair, 128)
+
+        def attend_block(j, carry):
+            rows = pl.ds(pl.multiple_of(j * BLOCK, BLOCK), BLOCK)
+            blocks = block_of(s, j) + 1
+            q_pair = q_own[pair, rows, :]
+            q_half = (q_pair * half0, q_pair * half1)
+            t_pre = dot_nt(q_pair, kp[pair]) * scale + pre_mask
+            m_acc[0] = jnp.where(first, t_pre, NEG_LARGE)
+            m_acc[1] = jnp.where(first, NEG_LARGE, t_pre)
+
+            def scores(kb, carry):
+                keys = kv[core_of(kb), pair, 0, key_rows(kb), :]
+                for h in range(2):
+                    t = dot_nt(q_half[h], keys) * scale + bias[j, kb]
+                    ts[h, kb] = t
+                    m_acc[h] = jnp.maximum(m_acc[h], jnp.maximum(t[:, :128], t[:, 128:]))
+                return carry
+
+            lax.fori_loop(0, blocks, scores, 0)
+            highest = [jnp.max(m_acc[h], axis=1, keepdims=True) for h in range(2)]
+            e_pre = jnp.exp2(t_pre - jnp.where(first, highest[0], highest[1]))
+            l_acc[0] = jnp.where(first, e_pre, 0.0)
+            l_acc[1] = jnp.where(first, 0.0, e_pre)
+            o_acc[...] = jnp.zeros(o_acc.shape, jnp.float32)
+
+            def mix(kb, carry):
+                values = kv[core_of(kb), pair, 1, key_rows(kb), :]
+                for h in range(2):
+                    e = jnp.exp2(ts[h, kb] - highest[h])
+                    l_acc[h] += e[:, :128] + e[:, 128:]
+                    o_acc[h] += dot_nn(e.astype(jnp.bfloat16), values)
+                return carry
+
+            lax.fori_loop(0, blocks, mix, 0)
+            total = [jnp.sum(l_acc[h], axis=1, keepdims=True) for h in range(2)]
+            share = [1.0 / total[h] for h in range(2)]
+            p_pre = (e_pre * jnp.where(first, share[0], share[1])).astype(jnp.bfloat16)
+            mixed = jnp.where(first, o_acc[0] * share[0], o_acc[1] * share[1]) + dot_nn(p_pre, vp[pair])
+            o_own[rows, cols] = mixed.astype(jnp.bfloat16)
+            logs = [highest[h] + jnp.log(total[h]) * LOG2E for h in range(2)]
+            lse[pair, rows, :] = jnp.where(first, logs[0], logs[1])
+            return carry
+
+        return lax.fori_loop(0, 2, attend_block, carry)
+
+    lax.fori_loop(0, 8, attend_pair, 0)
+
+    def out_project(n, carry):
+        cols = columns(n)
+        part_sum = jnp.zeros((rows_total, 256), jnp.float32)
+        for q in range(4):
+            part_sum += dot_nn(o_own[:, q * 256 : q * 256 + 256], wo[q, :, cols])
+        after[:, cols] = x_in[:, cols].astype(jnp.float32) + part_sum + vec[0, 2:3, cols]
+        return carry
+
+    lax.fori_loop(0, 4, out_project, 0)
+
+    def norm_two(rows):
+        centred, inverse = standardize(after[rows, :])
+        normed[rows, :] = (centred * inverse * vector(3) + vector(4)).astype(jnp.bfloat16)
+        acc[rows, :] = after[rows, :] + vector(5)
+
+    over_rows(norm_two)
+
+    def feed_quarter(q, carry):
+        def up(n, carry):
+            cols = columns(n)
+            for half in range(2):
+                rows = slice(half * BLOCK, half * BLOCK + BLOCK)
+                u = dot_nn(normed[rows, :], wu[q, :, cols]) + vec[q, 6:7, cols]
+                u2 = u * u
+                t = jnp.tanh(u * (GELU_A + (GELU_A * GELU_B) * u2))
+                half_t = 0.5 + 0.5 * t
+                wide[rows, cols] = (u * half_t).astype(jnp.bfloat16)
+                inner = u * (GELU_A + (3.0 * GELU_A * GELU_B) * u2)
+                slope[q, rows, cols] = (half_t + 0.5 * inner * (1.0 - t * t)).astype(jnp.bfloat16)
+            return carry
+
+        lax.fori_loop(0, 4, up, 0)
+
+        def down(n, carry):
+            cols = columns(n)
+            acc[:, cols] += dot_nn(wide[...], wd[q, :, cols])
+            return carry
+
+        lax.fori_loop(0, 4, down, 0)
+        return carry
+
+    lax.fori_loop(0, 4, feed_quarter, 0)
+
+    def give_out(rows):
+        y_out[rows, :] = acc[rows, :].astype(jnp.bfloat16)
+
+    def send_rows(j, out, sem):
+        block = block_of(s, j)
+        rows = slice(j * BLOCK, j * BLOCK + BLOCK)
+        sends.start_or_keep(
+            y_out.at[rows], out.at[micro], sem.at[micro], (role, d, block),
+            jnp.logical_and(role == s, z == block),
+        )
+
+    for j in range(2):
+        over_rows(give_out, j * chunks // 2, (j + 1) * chunks // 2)
+        rows = slice(j * BLOCK, j * BLOCK + BLOCK)
+        sends.start(y_out.at[rows], x_in.at[rows], x_sem.at[j], (s, d, partner), when=role == 0)
+    for j in range(2):
+        send_rows(j, act_out, act_sem)
+
+    for j in range(2):
+        arrived(g_in.at[j * BLOCK : (j + 1) * BLOCK], g_sem.at[j])
+
+    def clear(rows):
+        acc[rows, :] = jnp.zeros((CHUNK, 1024), jnp.float32)
+
+    over_rows(clear)
+
+    def feed_back(q, carry):
+        def down(n, carry):
+            cols = columns(n)
+            for half in range(2):
+                rows = slice(half * BLOCK, half * BLOCK + BLOCK)
+                grad_act = dot_nt(g_in[rows, :], wd[q, cols, :])
+                wide[rows, cols] = (grad_act * slope[q, rows, cols].astype(jnp.float32)).astype(jnp.bfloat16)
+            return carry
+
+        lax.fori_loop(0, 4, down, 0)
+
+        def up(n, carry):
+            cols = columns(n)
+            acc[:, cols] += dot_nt(wide[...], wu[q, cols, :])
+            return carry
+
+        lax.fori_loop(0, 4, up, 0)
+        return carry
+
+    lax.fori_loop(0, 4, feed_back, 0)
+
+    def middle(rows):
+        dv = norm_back(after[rows, :], vector(3), acc[rows, :])
+        normed[rows, :] = (g_in[rows, :].astype(jnp.float32) + dv).astype(jnp.bfloat16)
+
+    over_rows(middle)
+
+    def mix_back(q, carry):
+        wide[:, columns(q)] = dot_nt(normed[...], wo[q]).astype(jnp.bfloat16)
+        return carry
+
+    lax.fori_loop(0, 4, mix_back, 0)
+
+    def back_pair(pair, carry):
+        cols = columns(pair, 128)
+        dk_acc[...] = jnp.zeros(dk_acc.shape, jnp.float32)
+        dv_acc[...] = jnp.zeros(dv_acc.shape, jnp.float32)
+        pk_acc[...] = jnp.zeros(pk_acc.shape, jnp.float32)
+        pv_acc[...] = jnp.zeros(pv_acc.shape, jnp.float32)
+
+        def back_block(j, carry):
+            rows = pl.ds(pl.multiple_of(j * BLOCK, BLOCK), BLOCK)
+            blocks = block_of(s, j) + 1
+            q_pair = q_own[pair, rows, :]
+            q_half = (q_pair * half0, q_pair * half1)
+            g_pair = wide[rows, cols]
+            g_half = (g_pair * half0, g_pair * half1)
+            product = g_pair.astype(jnp.float32) * o_own[rows, cols].astype(jnp.float32)
+            row_term = [
+                jnp.sum(jnp.where(first, product, 0.0), axis=1, keepdims=True),
+                jnp.sum(jnp.where(first, 0.0, product), axis=1, keepdims=True),
+            ]
+            logs = lse[pair, rows, :]
+            log_half = (logs[:, 0:1], logs[:, 64:65])
+            p_pre = jnp.exp2(dot_nt(q_pair, kp[pair]) * scale + pre_mask - logs)
+            dp_pre = dot_nt(g_pair, vp[pair])
+            ds_pre = (p_pre * (dp_pre - jnp.where(first, row_term[0], row_term[1]))).astype(jnp.bfloat16)
+            pv_acc[...] += dot_tn(p_pre.astype(jnp.bfloat16), g_pair)
+            pk_acc[...] += dot_tn(ds_pre, q_pair)
+            dq_pre = dot_nn(ds_pre, kp[pair])
+            o_acc[...] = jnp.zeros(o_acc.shape, jnp.float32)
+
+            def back_keys(kb, carry):
+                keys = kv[core_of(kb), pair, 0, key_rows(kb), :]
+                values = kv[core_of(kb), pair, 1, key_rows(kb), :]
+                at = pl.ds(pl.multiple_of(kb * BLOCK, BLOCK), BLOCK)
+                for h in range(2):
+                    probs = jnp.exp2(dot_nt(q_half[h], keys) * scale + bias[j, kb] - log_half[h])
+                    grad_probs = dot_nt(g_half[h], values)
+                    grad_scores = (probs * (grad_probs - row_term[h])).astype(jnp.bfloat16)
+                    dv_acc[at, :] += dot_tn(probs.astype(jnp.bfloat16), g_half[h])
+                    dk_acc[at, :] += dot_tn(grad_scores, q_half[h])
+                    o_acc[h] += dot_nn(grad_scores, keys)
+                return carry
+
+            lax.fori_loop(0, blocks, back_keys, 0)
+            dq = (jnp.where(first, o_acc[0], o_acc[1]) + dq_pre) * HEAD_DIM ** (-0.5)
+            q_own[pair, rows, :] = dq.astype(jnp.bfloat16)
+            return carry
+
+        lax.fori_loop(0, 2, back_block, 0)
+        for j in range(2):
+            rows = slice(j * BLOCK, j * BLOCK + BLOCK)
+            for owner_core, held in ((s, dkv_own), (other, dkv_send)):
+                at = pl.ds(pl.multiple_of(block_of(owner_core, j) * BLOCK, BLOCK), BLOCK)
+                held[pair, 0, rows, :] = dk_acc[at, :].astype(jnp.bfloat16)
+                held[pair, 1, rows, :] = dv_acc[at, :].astype(jnp.bfloat16)
+        pltpu.make_async_remote_copy(
+            src_ref=dkv_send.at[pair], dst_ref=dkv_recv.at[pair], send_sem=dkv_ssem.at[pair],
+            recv_sem=dkv_rsem.at[pair], device_id=(other, d, z), device_id_type=MESH,
+        ).start()
+        pg_out[pair, 0] = jnp.where(first16, pk_acc[0:16, :], pk_acc[64:80, :]) * HEAD_DIM ** (-0.5)
+        pg_out[pair, 1] = jnp.where(first16, pv_acc[0:16, :], pv_acc[64:80, :])
+        return carry
+
+    lax.fori_loop(0, 8, back_pair, 0)
+    over_rows(clear)
+
+    def project_back(q, carry):
+        for p in range(2):
+            pair = 2 * q + p
+            pltpu.make_async_remote_copy(
+                src_ref=dkv_send.at[pair], dst_ref=dkv_recv.at[pair], send_sem=dkv_ssem.at[pair],
+                recv_sem=dkv_rsem.at[pair], device_id=(other, d, z), device_id_type=MESH,
+            ).wait()
+            dq = q_own[pair].astype(jnp.float32)
+            dk = (dkv_own[pair, 0].astype(jnp.float32) + dkv_recv[pair, 0].astype(jnp.float32)) * HEAD_DIM ** (-0.5)
+            dv = dkv_own[pair, 1].astype(jnp.float32) + dkv_recv[pair, 1].astype(jnp.float32)
+            dk = pltpu.roll(dk, 64, 1)
+            gt[:, p * 384 : p * 384 + 128] = jnp.where(first_all, dq, dk).astype(jnp.bfloat16)
+            gt[:, p * 384 + 128 : p * 384 + 256] = jnp.where(first_all, dv, dq).astype(jnp.bfloat16)
+            gt[:, p * 384 + 256 : p * 384 + 384] = jnp.where(first_all, dk, dv).astype(jnp.bfloat16)
+
+        def columns_back(n, carry):
+            cols = columns(n)
+            acc[:, cols] += dot_nt(gt[...], wq[q, cols, :])
+            return carry
+
+        lax.fori_loop(0, 4, columns_back, 0)
+        return carry
+
+    lax.fori_loop(0, 4, project_back, 0)
+    sends.finish()
+
+    def give_back(rows):
+        dv = norm_back(x_in[rows, :].astype(jnp.float32), vector(0), acc[rows, :])
+        y_out[rows, :] = (normed[rows, :].astype(jnp.float32) + dv).astype(jnp.bfloat16)
+
+    for j in range(2):
+        over_rows(give_back, j * chunks // 2, (j + 1) * chunks // 2)
+        rows = slice(j * BLOCK, j * BLOCK + BLOCK)
+        sends.start(y_out.at[rows], g_in.at[rows], g_sem.at[j], (s, d, partner), when=role == 1)
+    for j in range(2):
+        send_rows(j, ig_out, ig_sem)
+    for k in range(2):
+        arrived(act_out.at[k], act_sem.at[k])
+        arrived(ig_out.at[k], ig_sem.at[k])
+    sends.finish()
+
+
+def run_layers(x, cot, wq, wo, wu, wd, vec, pre, ends):
+    bf, f32 = jnp.bfloat16, jnp.float32
+    vm, dma = pltpu.VMEM, pltpu.SemaphoreType.DMA
+    rows = 2 * BLOCK
+    width = x.shape[-1]
+    pairs = width // 128
+    scratch = [
+        vm((4,) + wq.shape, bf), vm((4,) + wo.shape, bf), vm((4,) + wu.shape, bf), vm((4,) + wd.shape, bf),
+        vm((4,) + vec.shape, f32), vm((4,) + pre.shape, bf),
+        vm((rows, width), bf), vm((rows, width), bf), vm((rows, width), bf), vm((rows, width), bf),
+        vm((2, pairs, 2, rows, 128), bf), vm((pairs, rows, 128), bf), vm((rows, width), bf),
+        vm((pairs, rows, 128), f32), vm((2, 4, BLOCK, BLOCK), f32), vm((rows, width), f32), vm((rows, width), f32),
+        vm((4, rows, wu.shape[1]), bf), vm((rows, wu.shape[1]), bf),
+        vm((2, 4, BLOCK, BLOCK), f32), vm((2, BLOCK, 128), f32), vm((2, BLOCK, 128), f32), vm((2, BLOCK, 128), f32),
+        vm((4 * BLOCK, 128), f32), vm((4 * BLOCK, 128), f32),
+        vm((pairs, 2, rows, 128), bf), vm((pairs, 2, rows, 128), bf), vm((pairs, 2, rows, 128), bf),
+        vm((pairs, 128, 128), bf), vm((pairs, 128, 128), bf), vm((128, 128), f32), vm((128, 128), f32),
+        vm((rows, wq.shape[1]), bf),
+        dma((96,)), dma((4,)), dma((4,)), dma((2,)), dma((2,)), dma((2,)), dma((2,)), dma((4,)),
+        dma((4, 4)), dma((4, 4)), dma((4, 4)), dma((4, 4)),
+        dma((4,)), dma((4,)), dma((pairs,)), dma((pairs,)),
+    ]
+    anywhere = pl.BlockSpec(memory_space=pl.ANY)
+    return pl.pallas_call(
+        layer_kernel,
+        out_shape=(
+            jax.ShapeDtypeStruct(x.shape, bf), jax.ShapeDtypeStruct(x.shape, bf),
+            jax.ShapeDtypeStruct((pairs, 2, 16, 128), f32),
+        ),
+        in_specs=[anywhere] * 8 + [pl.BlockSpec(memory_space=pltpu.SMEM)],
+        out_specs=(anywhere, anywhere, pl.BlockSpec(memory_space=pltpu.VMEM)),
+        scratch_shapes=scratch,
+        name="two_layers",
+        compiler_params=pltpu.CompilerParams(
+            collective_id=0, has_side_effects=True, vmem_limit_bytes=63 * 2**20
+        ),
+    )(x, cot, wq, wo, wu, wd, vec, pre, ends)
+
+
+def pair_body(
+    layer_input, cotangent, example_lengths, attn_gain, attn_shift, query_key_value_weight, qkv_bias,
+    attention_output_weight, out_bias, ffn_gain, ffn_shift, up_projection_weight, up_projection_bias,
+    down_projection_weight, down_bias, prefix_table, mid_weight, mid_bias, prefix_weight, prefix_bias,
+):
+    section_index, z = lax.axis_index("section"), lax.axis_index("mp")
+    hidden_pre = jnp.dot(
+        prefix_table, mid_weight, preferred_element_type=jnp.float32
+    ) + mid_bias.astype(jnp.float32)
+    hidden_act = jnp.tanh(hidden_pre)
+    hidden_low = hidden_act.astype(jnp.bfloat16)
+    prefix_kv = (
+        jnp.dot(hidden_low, prefix_weight, preferred_element_type=jnp.float32)
+        + prefix_bias.astype(jnp.float32)
+    ).astype(jnp.bfloat16)
+    pre = jnp.pad(prefix_kv, ((0, 6), (0, 0)))
+    pieces = [attn_gain, attn_shift, out_bias, ffn_gain, ffn_shift, down_bias, up_projection_bias, qkv_bias]
+    width = layer_input.shape[-1]
+    vec = jnp.concatenate(
+        [jnp.pad(p.astype(jnp.float32), ((0, 0), (0, width - p.shape[1]))) for p in pieces], axis=0
+    )
+    ends = jnp.cumsum(example_lengths[:, 0], axis=-1).astype(jnp.int32)
+    activations, input_grads, prefix_part = run_layers(
+        layer_input[:, 0], cotangent[:, 0], query_key_value_weight[0], attention_output_weight[0],
+        up_projection_weight[0], down_projection_weight[0], vec, pre, ends,
+    )
+    pairs = prefix_part.shape[0]
+    part = prefix_part.reshape(pairs, 2, 16, 2, HEAD_DIM)[:, :, :PREFIX]
+    part = part.transpose(2, 0, 3, 1, 4).reshape(PREFIX, -1)
+    role = role_of(z)
+    both = jnp.stack([jnp.where(role == layer, part, 0.0) for layer in range(2)])
+    prefix_sum = lax.psum(both, ("section", "dp", "mp"))
+    own = prefix_bias.shape[0]
+    prefix_sum = lax.dynamic_slice(prefix_sum, (section_index, 0, z * own), (1, PREFIX, own))[0]
+    return (activations[None, :, None], input_grads[None, :, None]) + prefix_back(
+        prefix_sum, hidden_act, hidden_low, prefix_table, mid_weight, prefix_weight
     )
 
 
@@ -367,8 +995,9 @@
         P(None, ("section", "mp")),
         P(("section", "mp")),
     )
+    paired = mesh.shape["mp"] == 4 and mesh.shape["dp"] == 4
     return jax.shard_map(
-        body,
+        pair_body if paired else body,
         mesh=mesh,
         in_specs=placed,
         out_specs=(

time: 1050 us -> 570 us (0.54); the launches traced: 1040 us -> 570 us
  waiting for transfers between devices: 671 us -> 0 us
  Pallas kernels: 0 us -> 480 us
  matrix products: 183 us -> 5.89 us
  other arithmetic: 64.9 us -> 4.85 us
  between operations: 15.3 us -> 0.75 us
  local copies, waits for them, and re-layouts: 21.5 us -> 7.45 us
    pallas_call x0 -> x1, Pallas kernels: none -> 480 us  [run_layers(): pl.pallas_call(layer_kernel, out_shape=(jax.ShapeDtypeStruct(x.shape, bf)...]
    all_gather x12 -> x0, waiting for transfers between devices: 378 us -> none  [the longest x8 352 us: gather_rows(): return lax.all_gather(piece, 'mp', axis=1, tiled=True)]
    reduce_scatter x8 -> x0, waiting for transfers between devices: 290 us -> none  [reduce_rows(): lax.psum_scatter(partial_sum.astype(jnp.bfloat16), 'mp', scatter_dimensio...]
    dot_general x30 -> x6, matrix products: 159 us -> 5.89 us  [the longest x1 2.24 us: prefix_back(): jnp.dot(pre_grad, mid_weight.T, preferred_element_type=jnp.float32)]
    convert_element_type x12 -> x2, other arithmetic: 36.6 us -> 1.42 us  [the longest x1 0.73 us: pair_body(): mid_bias.astype(jnp.float32)]
    sub x2 -> x0, matrix products: 23.9 us -> none  [attend(): raised = jnp.exp(scores - highest)]
    reduce_sum x19 -> x2, other arithmetic: 24.2 us -> 1.2 us  [the longest x1 0.6 us: prefix_back(): prefix_bias_grad = jnp.sum(prefix_low.astype(jnp.float32), axis=0)]
    psum x2, blocking collectives: 52.4 us -> 70.6 us  [the longest x1 42.4 us: pair_body(): prefix_sum = lax.psum(both, ('section', 'dp', 'mp'))]
  transfers between devices with their start and end apart: 20 -> 0, of which waited for: 18 -> 0; matrix products, arithmetic and copies ran while one was open for 7% -> 0% of each run, Pallas kernels for 0% -> 0%
where the time goes in v2:
time: 570 us
  Pallas kernels  480 us (84%)
  blocking collectives  70.6 us (12%)
  local copies, waits for them, and re-layouts  7.45 us (1%)
  matrix products  5.89 us (1%)
    pallas_call x1, Pallas kernels, run_layers(): pl.pallas_call(layer_kernel, out_shape=(jax.ShapeDtypeStruct(x.shape, bf)...  480 us
    psum x1, blocking collectives, pair_body(): prefix_sum = lax.psum(both, ('section', 'dp', 'mp'))  42.4 us
    psum x1, blocking collectives, prefix_back(): hidden_grad = lax.psum(hidden_part, ('section', 'mp'))  28.2 us

profile of v2, /device:TPU:0, one launch (start us, length us, event | category | flops | bytes accessed | tf_op | source)
XLA Modules:
  0.0 569.9 jit_solution(13465633413808676253)
XLA Ops:
  0.7 0.7 convert_element_type.39
  1.4 1.5 fusion
  2.9 0.7 convert_element_type.41
  3.8 0.6 pad.10.pre_hbm
  4.4 0.7 pad.9
  5.1 0.8 concatenate.5
  5.9 0.6 concatenate.6.vec_hbm
  6.6 1.4 reduce_window_sum.11.ends
  8.0 480.4 %two_layers.1 = (bf16[2,256,1024]{2,1,0:T(8,128)(2,1)}, bf16[2,256,1024]{2,1,0:T(8,128)(2,1)}, f32[8,2,16,128]{3,2,1,0:T(8,128)}) custom-call(bf16[2,256,1024]{2,1,0:T(8,128)(2,1)} %bitcast.37, bf16[2,256,1024]{2,1,0:T(8,128)(2,1)} %bitcast.38, bf16[1024,768]{1,0:T(8,128)(2,1)} %bitcast.36, bf16[256,1024]{1,0:T(8,128)(2,1)} %bitcast.41, ...), custom_call_target="tpu_custom_call" | custom-call | tf_op jit(solution)/shard_map/two_layers/pallas_call | solution.py:920
  488.4 1.1 reshape.47
  489.5 0.2 select_bitcast_fusion.1
  489.7 0.2 select_n.62
  489.9 0.2 select_n.66
  490.1 42.4 %all-reduce.3 = bf16[2,10,2048]{2,1,0:T(8,128)(2,1)S(1)} all-reduce(f32[2,10,2048]{2,1,0:T(8,128)S(1)} %pad_maximum_fusion), channel_id=1, replica_groups=mesh['section'=2,'dp'=4,'mp'=4] {'section','dp','mp'}, use_global_device_ids=true, to_apply=%region_1.2 | all-reduce | flops 40960 | bytes 245760 | tf_op jit(solution)/shard_map/psum | solution.py:967
  532.5 0.6 convert_reduce_fusion
  533.1 0.2 fusion.7
  533.3 28.2 %psum.15 = f32[10,512]{1,0:T(8,128)S(1)} all-reduce(f32[10,512]{1,0:T(8,128)S(1)} %fusion.7), channel_id=1, replica_groups=mesh['section'=2,'dp'=4,'mp'=4] {'section','mp'}, use_global_device_ids=true, to_apply=%region_2.3 | all-reduce | flops 5120 | bytes 40960 | tf_op jit(solution)/shard_map/psum | solution.py:255
  561.5 0.6 convert_reduce_fusion.1
  562.1 0.5 convolution_bitcast_fusion
  562.6 1.8 copy.33
  564.4 1.3 fusion.3
  565.7 2.2 fusion.8
  567.9 1.0 copy.41
  568.9 1.0 copy.42
  (11 shorter events, 0.2 us)
Async XLA Ops:
  0.6 3.0 copy-start
  488.3 73.8 %copy-start.3 = (bf16[10,1024]{1,0:T(8,128)(2,1)S(1)}, bf16[10,1024]{1,0:T(8,128)(2,1)}, u32[]{:S(2)}) copy-start(bf16[10,1024]{1,0:T(8,128)(2,1)} %param.35) | copy-start | bytes 61444
  564.4 3.5 copy-start.2
  564.4 4.5 copy-start.1

commit v3 on v2

--- a/solution.py
+++ b/solution.py
@@ -247,12 +247,10 @@
     return (grad_input, prefix_g)
 
 
-def prefix_back(prefix_sum, hidden_act, hidden_low, prefix_table, mid_weight, prefix_weight):
+def prefix_back(prefix_sum, hidden_grad, hidden_act, hidden_low, prefix_table, mid_weight):
     prefix_low = prefix_sum.astype(jnp.bfloat16)
     prefix_bias_grad = jnp.sum(prefix_low.astype(jnp.float32), axis=0)
     prefix_weight_grad = jnp.dot(hidden_low.T, prefix_low, preferred_element_type=jnp.float32)
-    hidden_part = jnp.dot(prefix_low, prefix_weight.T, preferred_element_type=jnp.float32)
-    hidden_grad = lax.psum(hidden_part, ("section", "mp"))
     pre_grad = (hidden_grad * (1.0 - hidden_act * hidden_act)).astype(jnp.bfloat16)
     mid_bias_grad = jnp.sum(pre_grad.astype(jnp.float32), axis=0)
     mid_weight_grad = jnp.dot(prefix_table.T, pre_grad, preferred_element_type=jnp.float32)
@@ -341,8 +339,12 @@
     input_grads = lax.all_to_all(jnp.stack(sent_grads), "section", 0, 0, tiled=False)
     prefix_sum = lax.psum(jnp.stack(prefix_parts), ("dp", "section"))
     prefix_sum = lax.dynamic_index_in_dim(prefix_sum, section_index, 0, keepdims=False)
+    hidden_part = jnp.dot(
+        prefix_sum.astype(jnp.bfloat16), prefix_weight.T, preferred_element_type=jnp.float32
+    )
+    hidden_grad = lax.psum(hidden_part, ("section", "mp"))
     return (activations[None], input_grads[None]) + prefix_back(
-        prefix_sum, hidden_act, hidden_low, prefix_table, mid_weight, prefix_weight
+        prefix_sum, hidden_grad, hidden_act, hidden_low, prefix_table, mid_weight
     )
 
 
@@ -350,6 +352,9 @@
 BLOCK = 256
 LOG2E = 1.4426950408889634
 CHUNK = 32
+UNITS = 12
+UNIT_ROWS = 512
+PART_ROWS = UNIT_ROWS // 8
 
 
 def role_of(z):
@@ -403,20 +408,27 @@
 
         self.start(src, dst, recv_sem, target, when=jnp.logical_not(is_here))
 
-    def finish(self):
+    def finish(self, early=None):
+        left = []
         for when, copy in self.pending:
-            guarded(when, copy.wait_send)
-        self.pending = []
+            if early is None:
+                guarded(when, copy.wait_send)
+            else:
+                guarded(early if when is None else jnp.logical_and(when, early), copy.wait_send)
+                late = jnp.logical_not(early)
+                left.append((late if when is None else jnp.logical_and(when, late), copy))
+        self.pending = left
 
 
 def layer_kernel(
-    x_hbm, cot_hbm, wq_hbm, wo_hbm, wu_hbm, wd_hbm, vec_hbm, pre_hbm, ends,
-    act_out, ig_out, pg_out,
-    wq, wo, wu, wd, vec, pre,
+    x_hbm, cot_hbm, wq_hbm, wo_hbm, wu_hbm, wd_hbm, vec_hbm, pre_hbm, pw, ends,
+    act_out, ig_out, sum_out, hidden_out,
+    wq, wo, wud, vec, pre,
     x_in, g_in, y_out, normed, kv, q_own, o_own, lse, bias, after, acc, slope, wide,
-    ts, m_acc, l_acc, o_acc, dk_acc, dv_acc, dkv_own, dkv_send, dkv_recv, kp, vp, pk_acc, pv_acc, gt,
+    pg, pg_near, pg_far, hidden_all, ts, dk_acc, dv_acc, dkv_own, dkv_send, dkv_recv, kp, vp, pk_acc, pv_acc, gt,
     ssem, vec_sem, pre_sem, x_sem, g_sem, act_sem, ig_sem, own_sem, z_sem, a_sem, b_sem, c_sem,
-    kv_ssem, kv_rsem, dkv_ssem, dkv_rsem,
+    zr_sem, ar_sem, br_sem, cr_sem, zs_sem, as_sem, bs_sem, cs_sem, go_sem,
+    kv_ssem, kv_rsem, dkv_ssem, dkv_rsem, pg_sem, far_sem, hidden_sem,
 ):
     s, d, z = lax.axis_index("section"), lax.axis_index("dp"), lax.axis_index("mp")
     role, micro = role_of(z), z // 2
@@ -432,9 +444,9 @@
         for dz in range(4):
             if ds or dz:
                 pl.semaphore_signal(barrier, inc=1, device_id=((s + ds) % 2, d, (z + dz) % 4), device_id_type=MESH)
-    for near in (x_near, y_near):
+    for near in (x_near, y_near, 3 - d):
         pl.semaphore_signal(barrier, inc=1, device_id=(s, near, z), device_id_type=MESH)
-    pl.semaphore_wait(barrier, 9)
+    pl.semaphore_wait(barrier, 10)
 
     def arrived(dst, sem):
         pltpu.make_async_remote_copy(
@@ -444,95 +456,202 @@
 
     low_plane, high_plane = jnp.where(s == 0, 1, 0), jnp.where(s == 0, 2, 3)
     planes = (low_plane, high_plane)
-    owner = core_of(z)
-    mine = s == owner
-    for k, chip in ((0, 1), (1, 2)):
-        slot = pl.ds(pl.multiple_of((z // 2) * BLOCK, BLOCK), BLOCK)
-        target = (s, d, chip)
-        is_here = z == chip
-
-        @pl.when(jnp.logical_and(mine, is_here))
+    mine = s == core_of(z)
+    row_slot = pl.ds(pl.multiple_of((z // 2) * BLOCK, BLOCK), BLOCK)
+
+    def send_block(source, landing, sem, k, chip, when):
+        when = jnp.logical_and(mine, when)
+
+        @pl.when(jnp.logical_and(when, z == chip))
         def _():
-            pltpu.make_async_copy(x_hbm.at[k], x_in.at[slot], x_sem.at[z // 2]).start()
-
-        sends.start(x_hbm.at[k], x_in.at[slot], x_sem.at[z // 2], target,
-                    when=jnp.logical_and(mine, jnp.logical_not(is_here)))
+            pltpu.make_async_copy(source.at[k], landing.at[row_slot], sem.at[z // 2]).start()
+
+        sends.start(source.at[k], landing.at[row_slot], sem.at[z // 2], (s, d, chip),
+                    when=jnp.logical_and(when, z != chip))
+
     for t in planes:
         for h in range(2):
             is_here = jnp.logical_and(z == t, s == h)
             sends.start_or_keep(vec_hbm, vec.at[z], vec_sem.at[z], (h, d, t), is_here)
             sends.start_or_keep(pre_hbm, pre.at[z], pre_sem.at[z], (h, d, t), is_here)
-    matrices = ((wq_hbm, wq), (wo_hbm, wo), (wu_hbm, wu), (wd_hbm, wd))
     swapped = (d % 2) * 2 + d // 2
-
-    def part(w, h):
-        rows = matrices[w][1].shape[1] // 8
-        place = swapped if h else d
-        return pl.ds(pl.multiple_of((place + 4 * h) * rows, rows), rows)
-
-    for w, (held, full) in enumerate(matrices):
-        for t in planes:
+    place = jnp.where(s == 0, d, swapped)
+    pair_start = (place // 2) * 2
+    far_start = 2 - pair_start
+    firsts = ((wq_hbm, wq), (wo_hbm, wo))
+
+    def eighths(rows, start, count, h):
+        return pl.ds(pl.multiple_of((start + 4 * h) * rows, rows), rows * count)
+
+    def supply_firsts(when):
+        for w, (held, full) in enumerate(firsts):
+            rows = held.shape[0] // 8
+            for t in planes:
+                for h in range(2):
+                    at = eighths(rows, swapped if h else d, 1, h)
+                    sends.start(held.at[at], full.at[z, at], z_sem.at[w, z], (h, d, t),
+                                when=jnp.logical_and(when, z != t))
+
+    def supply_copies(i, c, then):
+        t = (z + 3 - i) % 4
+        held, base = ((wu_hbm, 0), (wd_hbm, 1024))[c // 2]
+
+        @pl.when(role_of(t) == s)
+        def _():
             for h in range(2):
-                sends.start(held.at[part(w, h)], full.at[z, part(w, h)], z_sem.at[w, z], (h, d, t), when=z != t)
-
+                at = eighths(PART_ROWS, swapped if h else d, 1, h)
+                start = (c % 2) * UNIT_ROWS + at.start
+                then(pltpu.make_async_remote_copy(
+                    src_ref=held.at[pl.ds(pl.multiple_of(start, PART_ROWS), PART_ROWS)],
+                    dst_ref=wud.at[z, pl.ds(pl.multiple_of(base + start, PART_ROWS), PART_ROWS)],
+                    send_sem=zs_sem.at[4 * i + c, h], recv_sem=zr_sem.at[4 * i + c],
+                    device_id=(h, d, t), device_id_type=MESH,
+                ))
+
+    def supply_all(i, carry):
+        for c in range(4):
+            supply_copies(i, c, lambda copy: copy.start())
+        return carry
+
+    def supply_done(i, carry):
+        for c in range(4):
+            supply_copies(i, c, lambda copy: copy.wait_send())
+        return carry
+
+    def supply_paced(i, carry):
+        for c in range(4):
+            supply_copies(i, c, lambda copy: copy.start())
+            if c:
+                supply_copies(i, c - 1, lambda copy: copy.wait_send())
+        supply_copies(i, 3, lambda copy: copy.wait_send())
+        return carry
+
+    supply_firsts(s == 0)
+    for k, chip in ((0, 1), (1, 2)):
+        send_block(x_hbm, x_in, x_sem, k, chip, True)
+    owned = ((wq_hbm, wq.at[z]), (wo_hbm, wo.at[z]), (wu_hbm, wud.at[z, 0:1024]), (wd_hbm, wud.at[z, 1024:2048]))
+    for w, (held, full) in enumerate(owned):
         @pl.when(role == s)
         def _():
-            pltpu.make_async_copy(held, full.at[z], own_sem.at[w]).start()
-
-        sends.start(held, full.at[z], own_sem.at[w], (other, d, z), when=role == s)
-    for k, chip in ((0, 0), (1, 3)):
-        slot = pl.ds(pl.multiple_of((z // 2) * BLOCK, BLOCK), BLOCK)
-        is_here = z == chip
-
-        @pl.when(jnp.logical_and(mine, is_here))
-        def _():
-            pltpu.make_async_copy(cot_hbm.at[k], g_in.at[slot], g_sem.at[z // 2]).start()
-
-        sends.start(cot_hbm.at[k], g_in.at[slot], g_sem.at[z // 2], (s, d, chip),
-                    when=jnp.logical_and(mine, jnp.logical_not(is_here)))
-
-    place = jnp.where(s == 0, d, swapped)
-
-    def mine_part(w, start, count):
-        rows = matrices[w][1].shape[1] // 8
-        return pl.ds(pl.multiple_of((start + 4 * s) * rows, rows), rows * count)
-
-    units = [(w, i) for w in (0, 1) for i in range(1, 4)] + [(w, i) for i in range(1, 4) for w in (2, 3)]
-
-    def piece(w, i, start, count):
-        return matrices[w][1].at[(z + i) % 4, mine_part(w, start, count)]
-
-    pair_start = (place // 2) * 2
-    far_start = 2 - pair_start
-
-    def relay(step):
-        stages = [units[step - k] if 0 <= step - k < len(units) else None for k in range(4)]
+            pltpu.make_async_copy(held, full, own_sem.at[w]).start()
+
+        sends.start(held, full, own_sem.at[w], (other, d, z), when=role == s)
+
+    feeds_zero = jnp.logical_and(role == 1, s == 0)
+
+    sends.finish(feeds_zero)
+
+    @pl.when(feeds_zero)
+    def _():
+        lax.fori_loop(0, 3, supply_paced, 0)
+
+    @pl.when(jnp.logical_and(role == 1, s == 1))
+    def _():
+        pl.semaphore_wait(go_sem, 1)
+
+    supply_first_one = jnp.logical_and(role == 1, s == 1)
+    supply_firsts(supply_first_one)
+
+    @pl.when(supply_first_one)
+    def _():
+        lax.fori_loop(0, 3, supply_all, 0)
+
+    first_units = [(w, i) for w in (0, 1) for i in range(1, 4)]
+
+    def first_piece(w, i, start, count):
+        full = firsts[w][1]
+        return full.at[(z + i) % 4, eighths(full.shape[1] // 8, start, count, s)]
+
+    def relay_first(step):
+        stages = [first_units[step - k] if 0 <= step - k < len(first_units) else None for k in range(4)]
         if stages[0]:
             w, i = stages[0]
             q = (z + i) % 4
-            arrived(piece(w, i, place, 1), z_sem.at[w, q])
-            sends.start(piece(w, i, place, 1), piece(w, i, place, 1), a_sem.at[w, q], (s, near1, z))
+            arrived(first_piece(w, i, place, 1), z_sem.at[w, q])
+            sends.start(first_piece(w, i, place, 1), first_piece(w, i, place, 1), a_sem.at[w, q], (s, near1, z))
         if stages[1]:
             w, i = stages[1]
             q = (z + i) % 4
-            arrived(piece(w, i, pair_start + 1 - place % 2, 1), a_sem.at[w, q])
-            sends.start(piece(w, i, pair_start, 2), piece(w, i, pair_start, 2), b_sem.at[w, q], (s, near2, z))
+            arrived(first_piece(w, i, pair_start + 1 - place % 2, 1), a_sem.at[w, q])
+            sends.start(first_piece(w, i, pair_start, 2), first_piece(w, i, pair_start, 2), b_sem.at[w, q], (s, near2, z))
         if stages[2]:
             w, i = stages[2]
             q = (z + i) % 4
-            arrived(piece(w, i, far_start, 2), b_sem.at[w, q])
-            sends.start(piece(w, i, 0, 4), piece(w, i, 0, 4), c_sem.at[w, q], (other, d, z))
+            arrived(first_piece(w, i, far_start, 2), b_sem.at[w, q])
+            sends.start(first_piece(w, i, 0, 4), first_piece(w, i, 0, 4), c_sem.at[w, q], (other, d, z))
         if stages[3]:
             w, i = stages[3]
-            q = (z + i) % 4
-            rows = matrices[w][1].shape[1] // 2
-            half = pl.ds(pl.multiple_of(other * rows, rows), rows)
-            arrived(matrices[w][1].at[q, half], c_sem.at[w, q])
-
-    for step in range(len(units) + 3):
-        relay(step)
-    for w, (held, full) in enumerate(matrices):
-        arrived(full.at[z], own_sem.at[w])
+            full = firsts[w][1]
+            arrived(full.at[(z + i) % 4, eighths(full.shape[1] // 8, 0, 4, other)], c_sem.at[w, (z + i) % 4])
+
+    for step in range(len(first_units) + 3):
+        relay_first(step)
+
+    feeds_one = jnp.logical_and(role == 0, s == 1)
+
+    @pl.when(feeds_one)
+    def _():
+        pl.semaphore_signal(go_sem, inc=1, device_id=(1, d, partner), device_id_type=MESH)
+
+    supply_firsts(feeds_one)
+    feeds_zero_late = jnp.logical_and(role == 0, s == 0)
+
+    @pl.when(feeds_zero_late)
+    def _():
+        lax.fori_loop(0, 3, supply_all, 0)
+
+    def unit_piece(m, start, count, h):
+        q = (z + 1 + m // 4) % 4
+        first_row = (m % 4) * UNIT_ROWS + (start + 4 * h) * PART_ROWS
+        return wud.at[q, pl.ds(pl.multiple_of(first_row, PART_ROWS), PART_ROWS * count)]
+
+    def relay_copy(m, stage):
+        start, count = ((place, 1), (pair_start, 2), (0, 4))[stage]
+        at = unit_piece(m, start, count, s)
+        return pltpu.make_async_remote_copy(
+            src_ref=at, dst_ref=at, send_sem=(as_sem, bs_sem, cs_sem)[stage].at[m],
+            recv_sem=(ar_sem, br_sem, cr_sem)[stage].at[m],
+            device_id=((s, near1, z), (s, near2, z), (other, d, z))[stage], device_id_type=MESH,
+        )
+
+    def relay(n):
+        for c in range(4):
+
+            @pl.when(jnp.logical_and(feeds_one, jnp.logical_and(n < UNITS, n % 4 == c)))
+            def _():
+                supply_copies(n // 4, c, lambda copy: copy.start())
+
+        for k in range(4):
+            m = n - k
+
+            @pl.when(jnp.logical_and(m >= 0, m < UNITS))
+            def _():
+                if k == 0:
+                    arrived(unit_piece(m, place, 1, s), zr_sem.at[m])
+                if k == 1:
+                    arrived(unit_piece(m, pair_start + 1 - place % 2, 1, s), ar_sem.at[m])
+                if k == 2:
+                    arrived(unit_piece(m, far_start, 2, s), br_sem.at[m])
+                if k == 3:
+                    arrived(unit_piece(m, 0, 4, other), cr_sem.at[m])
+                if k < 3:
+                    relay_copy(m, k).start()
+
+    def relay_while(start, stop, when):
+        def one(n, carry):
+            relay(n)
+            return carry
+
+        lax.fori_loop(start, jnp.where(when, stop, start), one, 0)
+
+    early = role == 0
+    relay_while(0, UNITS + 3, role == 1)
+    for k, chip in ((0, 0), (1, 3)):
+        send_block(cot_hbm, g_in, g_sem, k, chip, role == 1)
+    arrived(wq.at[z], own_sem.at[0])
+    arrived(wo.at[z], own_sem.at[1])
+    arrived(wud.at[z, 0:1024], own_sem.at[2])
+    arrived(wud.at[z, 1024:2048], own_sem.at[3])
     for q in range(4):
         arrived(vec.at[q], vec_sem.at[q])
         arrived(pre.at[q], pre_sem.at[q])
@@ -636,54 +755,51 @@
     def key_rows(kb):
         return pl.ds(pl.multiple_of((kb // 2) * BLOCK, BLOCK), BLOCK)
 
-    def attend_pair(pair, carry):
+    def attend_rows(pair, j, blocks):
         cols = columns(pair, 128)
-
-        def attend_block(j, carry):
-            rows = pl.ds(pl.multiple_of(j * BLOCK, BLOCK), BLOCK)
-            blocks = block_of(s, j) + 1
-            q_pair = q_own[pair, rows, :]
-            q_half = (q_pair * half0, q_pair * half1)
-            t_pre = dot_nt(q_pair, kp[pair]) * scale + pre_mask
-            m_acc[0] = jnp.where(first, t_pre, NEG_LARGE)
-            m_acc[1] = jnp.where(first, NEG_LARGE, t_pre)
-
-            def scores(kb, carry):
-                keys = kv[core_of(kb), pair, 0, key_rows(kb), :]
-                for h in range(2):
-                    t = dot_nt(q_half[h], keys) * scale + bias[j, kb]
-                    ts[h, kb] = t
-                    m_acc[h] = jnp.maximum(m_acc[h], jnp.maximum(t[:, :128], t[:, 128:]))
-                return carry
-
-            lax.fori_loop(0, blocks, scores, 0)
-            highest = [jnp.max(m_acc[h], axis=1, keepdims=True) for h in range(2)]
-            e_pre = jnp.exp2(t_pre - jnp.where(first, highest[0], highest[1]))
-            l_acc[0] = jnp.where(first, e_pre, 0.0)
-            l_acc[1] = jnp.where(first, 0.0, e_pre)
-            o_acc[...] = jnp.zeros(o_acc.shape, jnp.float32)
-
-            def mix(kb, carry):
-                values = kv[core_of(kb), pair, 1, key_rows(kb), :]
-                for h in range(2):
-                    e = jnp.exp2(ts[h, kb] - highest[h])
-                    l_acc[h] += e[:, :128] + e[:, 128:]
-                    o_acc[h] += dot_nn(e.astype(jnp.bfloat16), values)
-                return carry
-
-            lax.fori_loop(0, blocks, mix, 0)
-            total = [jnp.sum(l_acc[h], axis=1, keepdims=True) for h in range(2)]
-            share = [1.0 / total[h] for h in range(2)]
-            p_pre = (e_pre * jnp.where(first, share[0], share[1])).astype(jnp.bfloat16)
-            mixed = jnp.where(first, o_acc[0] * share[0], o_acc[1] * share[1]) + dot_nn(p_pre, vp[pair])
-            o_own[rows, cols] = mixed.astype(jnp.bfloat16)
-            logs = [highest[h] + jnp.log(total[h]) * LOG2E for h in range(2)]
-            lse[pair, rows, :] = jnp.where(first, logs[0], logs[1])
-            return carry
-
-        return lax.fori_loop(0, 2, attend_block, carry)
-
-    lax.fori_loop(0, 8, attend_pair, 0)
+        rows = slice(j * BLOCK, j * BLOCK + BLOCK)
+        q_pair = q_own[pair, rows, :]
+        q_half = (q_pair * half0, q_pair * half1)
+        t_pre = dot_nt(q_pair, kp[pair]) * scale + pre_mask
+        tops = [jnp.where(first, t_pre, NEG_LARGE), jnp.where(first, NEG_LARGE, t_pre)]
+        for kb in range(blocks):
+            keys = kv[core_of(kb), pair, 0, (kb // 2) * BLOCK : (kb // 2 + 1) * BLOCK, :]
+            for h in range(2):
+                t = dot_nt(q_half[h], keys) * scale + bias[j, kb]
+                ts[h, kb] = t
+                tops[h] = jnp.maximum(tops[h], jnp.maximum(t[:, :128], t[:, 128:]))
+        highest = [jnp.max(tops[h], axis=1, keepdims=True) for h in range(2)]
+        e_pre = jnp.exp2(t_pre - jnp.where(first, highest[0], highest[1]))
+        sums = [jnp.where(first, e_pre, 0.0), jnp.where(first, 0.0, e_pre)]
+        mixed = [jnp.zeros((BLOCK, 128), jnp.float32) for _ in range(2)]
+        for kb in range(blocks):
+            values = kv[core_of(kb), pair, 1, (kb // 2) * BLOCK : (kb // 2 + 1) * BLOCK, :]
+            for h in range(2):
+                e = jnp.exp2(ts[h, kb] - highest[h])
+                sums[h] += e[:, :128] + e[:, 128:]
+                mixed[h] += dot_nn(e.astype(jnp.bfloat16), values)
+        total = [jnp.sum(sums[h], axis=1, keepdims=True) for h in range(2)]
+        share = [1.0 / total[h] for h in range(2)]
+        p_pre = (e_pre * jnp.where(first, share[0], share[1])).astype(jnp.bfloat16)
+        result = jnp.where(first, mixed[0] * share[0], mixed[1] * share[1]) + dot_nn(p_pre, vp[pair])
+        o_own[rows, cols] = result.astype(jnp.bfloat16)
+        logs = [highest[h] + jnp.log(total[h]) * LOG2E for h in range(2)]
+        lse[pair, rows, :] = jnp.where(first, logs[0], logs[1])
+
+    def attend_all():
+        for core in range(2):
+
+            @pl.when(s == core)
+            def _():
+                def attend_pair(pair, carry):
+                    relay_while(pair // 2, pair // 2 + pair % 2, early)
+                    for j in range(2):
+                        attend_rows(pair, j, block_of(core, j) + 1)
+                    return carry
+
+                lax.fori_loop(0, 8, attend_pair, 0)
+
+    attend_all()
 
     def out_project(n, carry):
         cols = columns(n)
@@ -694,6 +810,8 @@
         return carry
 
     lax.fori_loop(0, 4, out_project, 0)
+    relay_while(4, 5, early)
+
 
     def norm_two(rows):
         centred, inverse = standardize(after[rows, :])
@@ -702,12 +820,18 @@
 
     over_rows(norm_two)
 
-    def feed_quarter(q, carry):
+    def feed_quarter(i, carry):
+        q = (z + i) % 4
+        relay_while(jnp.where(i == 1, 6, 4 * i + 1), 4 * i + 3, jnp.logical_and(early, i > 0))
+
         def up(n, carry):
             cols = columns(n)
+            inside = jnp.logical_and(n % 2 == 1, jnp.logical_and(i < 3, jnp.logical_or(i > 0, n == 1)))
+            step = jnp.where(i == 0, 5, 4 * i + 3 + n // 2)
+            relay_while(step, step + 1, jnp.logical_and(early, inside))
             for half in range(2):
                 rows = slice(half * BLOCK, half * BLOCK + BLOCK)
-                u = dot_nn(normed[rows, :], wu[q, :, cols]) + vec[q, 6:7, cols]
+                u = dot_nn(normed[rows, :], wud[q, 0:1024, cols]) + vec[q, 6:7, cols]
                 u2 = u * u
                 t = jnp.tanh(u * (GELU_A + (GELU_A * GELU_B) * u2))
                 half_t = 0.5 + 0.5 * t
@@ -720,13 +844,15 @@
 
         def down(n, carry):
             cols = columns(n)
-            acc[:, cols] += dot_nn(wide[...], wd[q, :, cols])
+            acc[:, cols] += dot_nn(wide[...], wud[q, 1024:2048, cols])
             return carry
 
         lax.fori_loop(0, 4, down, 0)
         return carry
 
     lax.fori_loop(0, 4, feed_quarter, 0)
+    for k, chip in ((0, 0), (1, 3)):
+        send_block(cot_hbm, g_in, g_sem, k, chip, role == 0)
 
     def give_out(rows):
         y_out[rows, :] = acc[rows, :].astype(jnp.bfloat16)
@@ -759,7 +885,7 @@
             cols = columns(n)
             for half in range(2):
                 rows = slice(half * BLOCK, half * BLOCK + BLOCK)
-                grad_act = dot_nt(g_in[rows, :], wd[q, cols, :])
+                grad_act = dot_nt(g_in[rows, :], wud[q, pl.ds(pl.multiple_of(1024 + n * 256, 256), 256), :])
                 wide[rows, cols] = (grad_act * slope[q, rows, cols].astype(jnp.float32)).astype(jnp.bfloat16)
             return carry
 
@@ -767,7 +893,7 @@
 
         def up(n, carry):
             cols = columns(n)
-            acc[:, cols] += dot_nt(wide[...], wu[q, cols, :])
+            acc[:, cols] += dot_nt(wide[...], wud[q, cols, :])
             return carry
 
         lax.fori_loop(0, 4, up, 0)
@@ -794,9 +920,8 @@
         pk_acc[...] = jnp.zeros(pk_acc.shape, jnp.float32)
         pv_acc[...] = jnp.zeros(pv_acc.shape, jnp.float32)
 
-        def back_block(j, carry):
-            rows = pl.ds(pl.multiple_of(j * BLOCK, BLOCK), BLOCK)
-            blocks = block_of(s, j) + 1
+        def back_rows(j, blocks):
+            rows = slice(j * BLOCK, j * BLOCK + BLOCK)
             q_pair = q_own[pair, rows, :]
             q_half = (q_pair * half0, q_pair * half1)
             g_pair = wide[rows, cols]
@@ -814,27 +939,31 @@
             pv_acc[...] += dot_tn(p_pre.astype(jnp.bfloat16), g_pair)
             pk_acc[...] += dot_tn(ds_pre, q_pair)
             dq_pre = dot_nn(ds_pre, kp[pair])
-            o_acc[...] = jnp.zeros(o_acc.shape, jnp.float32)
-
-            def back_keys(kb, carry):
-                keys = kv[core_of(kb), pair, 0, key_rows(kb), :]
-                values = kv[core_of(kb), pair, 1, key_rows(kb), :]
-                at = pl.ds(pl.multiple_of(kb * BLOCK, BLOCK), BLOCK)
+            dqs = [jnp.zeros((BLOCK, 128), jnp.float32) for _ in range(2)]
+            for kb in range(blocks):
+                keys = kv[core_of(kb), pair, 0, (kb // 2) * BLOCK : (kb // 2 + 1) * BLOCK, :]
+                values = kv[core_of(kb), pair, 1, (kb // 2) * BLOCK : (kb // 2 + 1) * BLOCK, :]
+                at = slice(kb * BLOCK, kb * BLOCK + BLOCK)
+                dv, dk = 0.0, 0.0
                 for h in range(2):
                     probs = jnp.exp2(dot_nt(q_half[h], keys) * scale + bias[j, kb] - log_half[h])
                     grad_probs = dot_nt(g_half[h], values)
                     grad_scores = (probs * (grad_probs - row_term[h])).astype(jnp.bfloat16)
-                    dv_acc[at, :] += dot_tn(probs.astype(jnp.bfloat16), g_half[h])
-                    dk_acc[at, :] += dot_tn(grad_scores, q_half[h])
-                    o_acc[h] += dot_nn(grad_scores, keys)
-                return carry
-
-            lax.fori_loop(0, blocks, back_keys, 0)
-            dq = (jnp.where(first, o_acc[0], o_acc[1]) + dq_pre) * HEAD_DIM ** (-0.5)
+                    dv += dot_tn(probs.astype(jnp.bfloat16), g_half[h])
+                    dk += dot_tn(grad_scores, q_half[h])
+                    dqs[h] += dot_nn(grad_scores, keys)
+                dv_acc[at, :] += dv
+                dk_acc[at, :] += dk
+            dq = (jnp.where(first, dqs[0], dqs[1]) + dq_pre) * HEAD_DIM ** (-0.5)
             q_own[pair, rows, :] = dq.astype(jnp.bfloat16)
-            return carry
-
-        lax.fori_loop(0, 2, back_block, 0)
+
+        for core in range(2):
+
+            @pl.when(s == core)
+            def _():
+                for j in range(2):
+                    back_rows(j, block_of(core, j) + 1)
+
         for j in range(2):
             rows = slice(j * BLOCK, j * BLOCK + BLOCK)
             for owner_core, held in ((s, dkv_own), (other, dkv_send)):
@@ -845,11 +974,17 @@
             src_ref=dkv_send.at[pair], dst_ref=dkv_recv.at[pair], send_sem=dkv_ssem.at[pair],
             recv_sem=dkv_rsem.at[pair], device_id=(other, d, z), device_id_type=MESH,
         ).start()
-        pg_out[pair, 0] = jnp.where(first16, pk_acc[0:16, :], pk_acc[64:80, :]) * HEAD_DIM ** (-0.5)
-        pg_out[pair, 1] = jnp.where(first16, pv_acc[0:16, :], pv_acc[64:80, :])
+        pg[pair, 0] = jnp.where(first16, pk_acc[0:16, :], pk_acc[64:80, :]) * HEAD_DIM ** (-0.5)
+        pg[pair, 1] = jnp.where(first16, pv_acc[0:16, :], pv_acc[64:80, :])
         return carry
 
     lax.fori_loop(0, 8, back_pair, 0)
+    contribution = micro * 2 + s
+    for q in range(4):
+        sends.start_or_keep(
+            pg.at[2 * q : 2 * q + 2], pg_near.at[contribution], pg_sem.at[contribution], (role, d, q),
+            jnp.logical_and(role == s, z == q),
+        )
     over_rows(clear)
 
     def project_back(q, carry):
@@ -888,49 +1023,91 @@
         sends.start(y_out.at[rows], g_in.at[rows], g_sem.at[j], (s, d, partner), when=role == 1)
     for j in range(2):
         send_rows(j, ig_out, ig_sem)
+    for k in range(4):
+        arrived(pg_near.at[k], pg_sem.at[k])
+    pg_far[d] = (pg_near[0] + pg_near[1]) + (pg_near[2] + pg_near[3])
+    for k in range(1, 4):
+        sends.start(pg_far.at[d], pg_far.at[d], far_sem.at[d], (s, (d + k) % 4, z))
+    for k in range(1, 4):
+        arrived(pg_far.at[(d + k) % 4], far_sem.at[(d + k) % 4])
+    total_pg = (pg_far[0] + pg_far[1]) + (pg_far[2] + pg_far[3])
+    for p in range(2):
+        keys, values = total_pg[p, 0], total_pg[p, 1]
+        sum_out[:, p * 256 : p * 256 + 128] = jnp.where(first16, keys, pltpu.roll(values, 64, 1))
+        sum_out[:, p * 256 + 128 : p * 256 + 256] = jnp.where(first16, pltpu.roll(keys, 64, 1), values)
+    here = s * 4 + z
+    hidden_all[here] = dot_nt(sum_out[...].astype(jnp.bfloat16), pw[...])
+    for ds in range(2):
+        for dz in range(4):
+            if ds or dz:
+                sends.start(hidden_all.at[here], hidden_all.at[here], hidden_sem.at[here],
+                            ((s + ds) % 2, d, (z + dz) % 4))
+    for ds in range(2):
+        for dz in range(4):
+            if ds or dz:
+                there = ((s + ds) % 2) * 4 + (z + dz) % 4
+                arrived(hidden_all.at[there], hidden_sem.at[there])
+    hidden_sum = hidden_all[0]
+    for k in range(1, 8):
+        hidden_sum += hidden_all[k]
+    hidden_out[...] = hidden_sum
+
+    @pl.when(jnp.logical_not(feeds_zero))
+    def _():
+        lax.fori_loop(0, 3, supply_done, 0)
+
+    def relays_done(m, carry):
+        for stage in range(3):
+            relay_copy(m, stage).wait_send()
+        return carry
+
+    lax.fori_loop(0, UNITS, relays_done, 0)
     for k in range(2):
         arrived(act_out.at[k], act_sem.at[k])
         arrived(ig_out.at[k], ig_sem.at[k])
     sends.finish()
 
 
-def run_layers(x, cot, wq, wo, wu, wd, vec, pre, ends):
+def run_layers(x, cot, wq, wo, wu, wd, vec, pre, pw, ends):
     bf, f32 = jnp.bfloat16, jnp.float32
     vm, dma = pltpu.VMEM, pltpu.SemaphoreType.DMA
     rows = 2 * BLOCK
     width = x.shape[-1]
     pairs = width // 128
     scratch = [
-        vm((4,) + wq.shape, bf), vm((4,) + wo.shape, bf), vm((4,) + wu.shape, bf), vm((4,) + wd.shape, bf),
+        vm((4,) + wq.shape, bf), vm((4,) + wo.shape, bf), vm((4, 2 * wu.shape[0], width), bf),
         vm((4,) + vec.shape, f32), vm((4,) + pre.shape, bf),
         vm((rows, width), bf), vm((rows, width), bf), vm((rows, width), bf), vm((rows, width), bf),
         vm((2, pairs, 2, rows, 128), bf), vm((pairs, rows, 128), bf), vm((rows, width), bf),
         vm((pairs, rows, 128), f32), vm((2, 4, BLOCK, BLOCK), f32), vm((rows, width), f32), vm((rows, width), f32),
         vm((4, rows, wu.shape[1]), bf), vm((rows, wu.shape[1]), bf),
-        vm((2, 4, BLOCK, BLOCK), f32), vm((2, BLOCK, 128), f32), vm((2, BLOCK, 128), f32), vm((2, BLOCK, 128), f32),
+        vm((pairs, 2, 16, 128), f32), vm((4, 2, 2, 16, 128), f32), vm((4, 2, 2, 16, 128), f32), vm((8, 16, pw.shape[0]), f32),
+        vm((2, 4, BLOCK, BLOCK), f32),
         vm((4 * BLOCK, 128), f32), vm((4 * BLOCK, 128), f32),
         vm((pairs, 2, rows, 128), bf), vm((pairs, 2, rows, 128), bf), vm((pairs, 2, rows, 128), bf),
         vm((pairs, 128, 128), bf), vm((pairs, 128, 128), bf), vm((128, 128), f32), vm((128, 128), f32),
         vm((rows, wq.shape[1]), bf),
         dma((96,)), dma((4,)), dma((4,)), dma((2,)), dma((2,)), dma((2,)), dma((2,)), dma((4,)),
-        dma((4, 4)), dma((4, 4)), dma((4, 4)), dma((4, 4)),
-        dma((4,)), dma((4,)), dma((pairs,)), dma((pairs,)),
+        dma((2, 4)), dma((2, 4)), dma((2, 4)), dma((2, 4)),
+        dma((UNITS,)), dma((UNITS,)), dma((UNITS,)), dma((UNITS,)), dma((UNITS, 2)), dma((UNITS,)), dma((UNITS,)), dma((UNITS,)),
+        pltpu.SemaphoreType.REGULAR,
+        dma((4,)), dma((4,)), dma((pairs,)), dma((pairs,)), dma((4,)), dma((4,)), dma((8,)),
     ]
     anywhere = pl.BlockSpec(memory_space=pl.ANY)
     return pl.pallas_call(
         layer_kernel,
         out_shape=(
             jax.ShapeDtypeStruct(x.shape, bf), jax.ShapeDtypeStruct(x.shape, bf),
-            jax.ShapeDtypeStruct((pairs, 2, 16, 128), f32),
+            jax.ShapeDtypeStruct((16, pw.shape[1]), f32), jax.ShapeDtypeStruct((16, pw.shape[0]), f32),
         ),
-        in_specs=[anywhere] * 8 + [pl.BlockSpec(memory_space=pltpu.SMEM)],
-        out_specs=(anywhere, anywhere, pl.BlockSpec(memory_space=pltpu.VMEM)),
+        in_specs=[anywhere] * 8 + [pl.BlockSpec(memory_space=pltpu.VMEM), pl.BlockSpec(memory_space=pltpu.SMEM)],
+        out_specs=(anywhere, anywhere, pl.BlockSpec(memory_space=pltpu.VMEM), pl.BlockSpec(memory_space=pltpu.VMEM)),
         scratch_shapes=scratch,
         name="two_layers",
         compiler_params=pltpu.CompilerParams(
             collective_id=0, has_side_effects=True, vmem_limit_bytes=63 * 2**20
         ),
-    )(x, cot, wq, wo, wu, wd, vec, pre, ends)
+    )(x, cot, wq, wo, wu, wd, vec, pre, pw, ends)
 
 
 def pair_body(
@@ -938,7 +1115,6 @@
     attention_output_weight, out_bias, ffn_gain, ffn_shift, up_projection_weight, up_projection_bias,
     down_projection_weight, down_bias, prefix_table, mid_weight, mid_bias, prefix_weight, prefix_bias,
 ):
-    section_index, z = lax.axis_index("section"), lax.axis_index("mp")
     hidden_pre = jnp.dot(
         prefix_table, mid_weight, preferred_element_type=jnp.float32
     ) + mid_bias.astype(jnp.float32)
@@ -955,20 +1131,12 @@
         [jnp.pad(p.astype(jnp.float32), ((0, 0), (0, width - p.shape[1]))) for p in pieces], axis=0
     )
     ends = jnp.cumsum(example_lengths[:, 0], axis=-1).astype(jnp.int32)
-    activations, input_grads, prefix_part = run_layers(
+    activations, input_grads, prefix_sum, hidden_grad = run_layers(
         layer_input[:, 0], cotangent[:, 0], query_key_value_weight[0], attention_output_weight[0],
-        up_projection_weight[0], down_projection_weight[0], vec, pre, ends,
-    )
-    pairs = prefix_part.shape[0]
-    part = prefix_part.reshape(pairs, 2, 16, 2, HEAD_DIM)[:, :, :PREFIX]
-    part = part.transpose(2, 0, 3, 1, 4).reshape(PREFIX, -1)
-    role = role_of(z)
-    both = jnp.stack([jnp.where(role == layer, part, 0.0) for layer in range(2)])
-    prefix_sum = lax.psum(both, ("section", "dp", "mp"))
-    own = prefix_bias.shape[0]
-    prefix_sum = lax.dynamic_slice(prefix_sum, (section_index, 0, z * own), (1, PREFIX, own))[0]
+        up_projection_weight[0], down_projection_weight[0], vec, pre, prefix_weight, ends,
+    )
     return (activations[None, :, None], input_grads[None, :, None]) + prefix_back(
-        prefix_sum, hidden_act, hidden_low, prefix_table, mid_weight, prefix_weight
+        prefix_sum[:PREFIX], hidden_grad[:PREFIX], hidden_act, hidden_low, prefix_table, mid_weight
     )
 
 

time: 570 us -> 420 us (0.74)
  Pallas kernels: 480 us -> 401 us
  blocking collectives: 70.6 us -> 0 us
    pallas_call x1, Pallas kernels: 480 us -> 401 us  [run_layers(): pl.pallas_call(layer_kernel, out_shape=(jax.ShapeDtypeStruct(x.shape, bf)...]
    psum x2 -> x0, blocking collectives: 70.6 us -> none  [the longest x1 42.4 us: pair_body(): prefix_sum = lax.psum(both, ('section', 'dp', 'mp'))]
where the time goes in v3:
time: 420 us; the launch traced here: 418 us
  Pallas kernels  401 us (95%)
  local copies, waits for them, and re-layouts  6 us (1%)
  matrix products  5.45 us (1%)
  other arithmetic  4.77 us (1%)
    pallas_call x1, Pallas kernels, run_layers(): pl.pallas_call(layer_kernel, out_shape=(jax.ShapeDtypeStruct(x.shape, bf)...  401 us

profile of v3, /device:TPU:0, one launch (start us, length us, event | category | flops | bytes accessed | tf_op | source)
XLA Modules:
  0.0 418.0 jit_solution(9452946634291557966)
XLA Ops:
  0.6 0.0 copy-start
  0.6 0.7 convert_element_type.18
  1.3 0.1 copy-done
  1.4 1.5 fusion
  2.9 0.7 convert_element_type.36
  3.6 1.2 fusion.1
  4.8 0.6 pad.10.pre_hbm
  5.4 0.7 pad.9
  6.1 0.8 concatenate.5
  6.9 0.6 concatenate.6.vec_hbm
  7.6 1.4 reduce_window_sum.11.ends
  9.0 401.1 %two_layers.1 = (bf16[2,256,1024]{2,1,0:T(8,128)(2,1)}, bf16[2,256,1024]{2,1,0:T(8,128)(2,1)}, f32[16,512]{1,0:T(8,128)}, f32[16,512]{1,0:T(8,128)}) custom-call(bf16[2,256,1024]{2,1,0:T(8,128)(2,1)} %bitcast.25, bf16[2,256,1024]{2,1,0:T(8,128)(2,1)} %bitcast.26, bf16[1024,768]{1,0:T(8,128)(2,1)} %bitcast.24, bf16[256,1024]{1,0:T(8,128)(2,1)} %bitcast.29, ...), custom_call_target="tpu_custom_call" | custom-call | tf_op jit(solution)/shard_map/two_layers/pallas_call | solution.py:1097
  410.0 1.4 convert_reduce_fusion.1
  411.4 0.5 convolution_bitcast_fusion
  411.9 0.0 copy-start.1
  411.9 0.0 copy-start.4
  411.9 1.8 copy.29
  413.7 0.0 copy-done.1
  413.7 1.0 fusion.5
  414.7 0.0 copy-done.4
  414.7 1.3 fusion.2
  416.0 0.0 copy-done.3
  416.0 1.0 copy.32
  417.0 1.0 copy.33
  (3 shorter events, 0.0 us)
Async XLA Ops:
  0.6 0.8 copy-start
  411.9 1.8 copy-start.1
  411.9 2.9 copy-start.4
  413.7 2.3 copy-start.3
  413.7 3.3 copy-start.2

commit v4 on v3

--- a/solution.py
+++ b/solution.py
@@ -353,6 +353,7 @@
 LOG2E = 1.4426950408889634
 CHUNK = 32
 UNITS = 12
+AHEAD = 8
 UNIT_ROWS = 512
 PART_ROWS = UNIT_ROWS // 8
 
@@ -401,23 +402,17 @@
         guarded(when, copy.start)
         self.pending.append((when, copy))
 
-    def start_or_keep(self, src, dst, recv_sem, target, is_here):
-        @pl.when(is_here)
+    def start_or_keep(self, src, dst, recv_sem, target, is_here, when=True):
+        @pl.when(jnp.logical_and(when, is_here))
         def _():
             pltpu.make_async_copy(src, dst, recv_sem).start()
 
-        self.start(src, dst, recv_sem, target, when=jnp.logical_not(is_here))
-
-    def finish(self, early=None):
-        left = []
+        self.start(src, dst, recv_sem, target, when=jnp.logical_and(when, jnp.logical_not(is_here)))
+
+    def finish(self):
         for when, copy in self.pending:
-            if early is None:
-                guarded(when, copy.wait_send)
-            else:
-                guarded(early if when is None else jnp.logical_and(when, early), copy.wait_send)
-                late = jnp.logical_not(early)
-                left.append((late if when is None else jnp.logical_and(when, late), copy))
-        self.pending = left
+            guarded(when, copy.wait_send)
+        self.pending = []
 
 
 def layer_kernel(
@@ -425,10 +420,11 @@
     act_out, ig_out, sum_out, hidden_out,
     wq, wo, wud, vec, pre,
     x_in, g_in, y_out, normed, kv, q_own, o_own, lse, bias, after, acc, slope, wide,
-    pg, pg_near, pg_far, hidden_all, ts, dk_acc, dv_acc, dkv_own, dkv_send, dkv_recv, kp, vp, pk_acc, pv_acc, gt,
+    pg, pg_near, pg_far, hidden_all, ts, dkv_own, dkv_send, dkv_recv, kp, vp, gt,
     ssem, vec_sem, pre_sem, x_sem, g_sem, act_sem, ig_sem, own_sem, z_sem, a_sem, b_sem, c_sem,
-    zr_sem, ar_sem, br_sem, cr_sem, zs_sem, as_sem, bs_sem, cs_sem, go_sem,
+    zr_sem, ar_sem, br_sem, cr_sem, fs_sem, zs_sem, as_sem, bs_sem, cs_sem, go_sem,
     kv_ssem, kv_rsem, dkv_ssem, dkv_rsem, pg_sem, far_sem, hidden_sem,
+    hand_sem, cot_sem,
 ):
     s, d, z = lax.axis_index("section"), lax.axis_index("dp"), lax.axis_index("mp")
     role, micro = role_of(z), z // 2
@@ -469,11 +465,26 @@
         sends.start(source.at[k], landing.at[row_slot], sem.at[z // 2], (s, d, chip),
                     when=jnp.logical_and(when, z != chip))
 
-    for t in planes:
-        for h in range(2):
-            is_here = jnp.logical_and(z == t, s == h)
-            sends.start_or_keep(vec_hbm, vec.at[z], vec_sem.at[z], (h, d, t), is_here)
-            sends.start_or_keep(pre_hbm, pre.at[z], pre_sem.at[z], (h, d, t), is_here)
+    def send_small(when):
+        for t in planes:
+            for h in range(2):
+                is_here = jnp.logical_and(z == t, s == h)
+                sends.start_or_keep(vec_hbm, vec.at[z], vec_sem.at[z], (h, d, t), is_here, when)
+                sends.start_or_keep(pre_hbm, pre.at[z], pre_sem.at[z], (h, d, t), is_here, when)
+
+    def send_x(when):
+        for k, chip in ((0, 1), (1, 2)):
+            send_block(x_hbm, x_in, x_sem, k, chip, when)
+
+    toward = jnp.where(z < 2, 1, -1)
+
+    def quarter(i):
+        return (z + 4 + toward * i) % 4
+
+    def taker(i):
+        low, high = (z + 3 - i) % 4, (z + 1 + i) % 4
+        return jnp.where(low == low_plane, low, high), jnp.logical_or(low == low_plane, high == high_plane)
+
     swapped = (d % 2) * 2 + d // 2
     place = jnp.where(s == 0, d, swapped)
     pair_start = (place // 2) * 2
@@ -483,20 +494,43 @@
     def eighths(rows, start, count, h):
         return pl.ds(pl.multiple_of((start + 4 * h) * rows, rows), rows * count)
 
-    def supply_firsts(when):
-        for w, (held, full) in enumerate(firsts):
-            rows = held.shape[0] // 8
-            for t in planes:
-                for h in range(2):
-                    at = eighths(rows, swapped if h else d, 1, h)
-                    sends.start(held.at[at], full.at[z, at], z_sem.at[w, z], (h, d, t),
-                                when=jnp.logical_and(when, z != t))
+    def supply_first(w, i, then):
+        t, taken = taker(i)
+        held, full = firsts[w]
+
+        @pl.when(taken)
+        def _():
+            for h in range(2):
+                at = eighths(held.shape[0] // 8, swapped if h else d, 1, h)
+                then(pltpu.make_async_remote_copy(
+                    src_ref=held.at[at], dst_ref=full.at[z, at], send_sem=fs_sem.at[3 * w + i, h],
+                    recv_sem=z_sem.at[w, z], device_id=(h, d, t), device_id_type=MESH,
+                ))
+
+    def supply_firsts(when, w):
+        @pl.when(when)
+        def _():
+            def one(i, carry):
+                supply_first(w, i, lambda copy: copy.start())
+                return carry
+
+            lax.fori_loop(0, 3, one, 0)
+
+    def supply_firsts_paced(when, w):
+        @pl.when(when)
+        def _():
+            def one(i, carry):
+                supply_first(w, i, lambda copy: copy.start())
+                supply_first(w, i, lambda copy: copy.wait_send())
+                return carry
+
+            lax.fori_loop(0, 3, one, 0)
 
     def supply_copies(i, c, then):
-        t = (z + 3 - i) % 4
+        t, taken = taker(i)
         held, base = ((wu_hbm, 0), (wd_hbm, 1024))[c // 2]
 
-        @pl.when(role_of(t) == s)
+        @pl.when(taken)
         def _():
             for h in range(2):
                 at = eighths(PART_ROWS, swapped if h else d, 1, h)
@@ -526,9 +560,15 @@
         supply_copies(i, 3, lambda copy: copy.wait_send())
         return carry
 
-    supply_firsts(s == 0)
-    for k, chip in ((0, 1), (1, 2)):
-        send_block(x_hbm, x_in, x_sem, k, chip, True)
+    feeds_zero = jnp.logical_and(role == 1, s == 0)
+    feeds_zero_late = jnp.logical_and(role == 0, s == 0)
+    feeds_one = jnp.logical_and(role == 0, s == 1)
+    feeds_one_late = jnp.logical_and(role == 1, s == 1)
+    supply_firsts(feeds_zero_late, 0)
+    supply_firsts_paced(feeds_zero, 0)
+    send_x(feeds_zero)
+    send_small(feeds_zero)
+    supply_firsts_paced(feeds_zero, 1)
     owned = ((wq_hbm, wq.at[z]), (wo_hbm, wo.at[z]), (wu_hbm, wud.at[z, 0:1024]), (wd_hbm, wud.at[z, 1024:2048]))
     for w, (held, full) in enumerate(owned):
         @pl.when(role == s)
@@ -537,71 +577,73 @@
 
         sends.start(held, full, own_sem.at[w], (other, d, z), when=role == s)
 
-    feeds_zero = jnp.logical_and(role == 1, s == 0)
-
-    sends.finish(feeds_zero)
-
     @pl.when(feeds_zero)
     def _():
         lax.fori_loop(0, 3, supply_paced, 0)
 
-    @pl.when(jnp.logical_and(role == 1, s == 1))
+    @pl.when(feeds_one_late)
     def _():
         pl.semaphore_wait(go_sem, 1)
 
-    supply_first_one = jnp.logical_and(role == 1, s == 1)
-    supply_firsts(supply_first_one)
-
-    @pl.when(supply_first_one)
-    def _():
-        lax.fori_loop(0, 3, supply_all, 0)
+    send_small(feeds_one_late)
+    supply_firsts(feeds_one_late, 0)
+    supply_firsts(feeds_one_late, 1)
 
     first_units = [(w, i) for w in (0, 1) for i in range(1, 4)]
 
     def first_piece(w, i, start, count):
         full = firsts[w][1]
-        return full.at[(z + i) % 4, eighths(full.shape[1] // 8, start, count, s)]
+        return full.at[quarter(i), eighths(full.shape[1] // 8, start, count, s)]
 
     def relay_first(step):
         stages = [first_units[step - k] if 0 <= step - k < len(first_units) else None for k in range(4)]
         if stages[0]:
             w, i = stages[0]
-            q = (z + i) % 4
+            q = quarter(i)
             arrived(first_piece(w, i, place, 1), z_sem.at[w, q])
             sends.start(first_piece(w, i, place, 1), first_piece(w, i, place, 1), a_sem.at[w, q], (s, near1, z))
         if stages[1]:
             w, i = stages[1]
-            q = (z + i) % 4
+            q = quarter(i)
             arrived(first_piece(w, i, pair_start + 1 - place % 2, 1), a_sem.at[w, q])
             sends.start(first_piece(w, i, pair_start, 2), first_piece(w, i, pair_start, 2), b_sem.at[w, q], (s, near2, z))
         if stages[2]:
             w, i = stages[2]
-            q = (z + i) % 4
+            q = quarter(i)
             arrived(first_piece(w, i, far_start, 2), b_sem.at[w, q])
             sends.start(first_piece(w, i, 0, 4), first_piece(w, i, 0, 4), c_sem.at[w, q], (other, d, z))
         if stages[3]:
             w, i = stages[3]
             full = firsts[w][1]
-            arrived(full.at[(z + i) % 4, eighths(full.shape[1] // 8, 0, 4, other)], c_sem.at[w, (z + i) % 4])
+            arrived(full.at[quarter(i), eighths(full.shape[1] // 8, 0, 4, other)], c_sem.at[w, quarter(i)])
 
     for step in range(len(first_units) + 3):
         relay_first(step)
-
-    feeds_one = jnp.logical_and(role == 0, s == 1)
-
-    @pl.when(feeds_one)
-    def _():
-        pl.semaphore_signal(go_sem, inc=1, device_id=(1, d, partner), device_id_type=MESH)
-
-    supply_firsts(feeds_one)
-    feeds_zero_late = jnp.logical_and(role == 0, s == 0)
-
-    @pl.when(feeds_zero_late)
+        if step == 0:
+            send_x(role == 0)
+            send_small(feeds_zero_late)
+            supply_firsts(feeds_zero_late, 1)
+        if step == 3:
+            @pl.when(feeds_one)
+            def _():
+                pl.semaphore_signal(go_sem, inc=1, device_id=(1, d, partner), device_id_type=MESH)
+
+            supply_firsts(feeds_one, 0)
+        if step == 6:
+            send_small(feeds_one)
+            supply_firsts(feeds_one, 1)
+
+        @pl.when(feeds_zero_late)
+        def _():
+            if 1 <= step < 5:
+                supply_copies(0, step - 1, lambda copy: copy.start())
+
+    @pl.when(feeds_one_late)
     def _():
         lax.fori_loop(0, 3, supply_all, 0)
 
     def unit_piece(m, start, count, h):
-        q = (z + 1 + m // 4) % 4
+        q = quarter(1 + m // 4)
         first_row = (m % 4) * UNIT_ROWS + (start + 4 * h) * PART_ROWS
         return wud.at[q, pl.ds(pl.multiple_of(first_row, PART_ROWS), PART_ROWS * count)]
 
@@ -637,17 +679,33 @@
                 if k < 3:
                     relay_copy(m, k).start()
 
-    def relay_while(start, stop, when):
+    def cot_copies(then):
+        for k, chip in ((0, 0), (1, 3)):
+
+            @pl.when(jnp.logical_and(mine, z != chip))
+            def _():
+                then(pltpu.make_async_remote_copy(
+                    src_ref=cot_hbm.at[k], dst_ref=g_in.at[row_slot], send_sem=cot_sem.at[k],
+                    recv_sem=g_sem.at[z // 2], device_id=(s, d, chip), device_id_type=MESH,
+                ))
+
+    for k, chip in ((0, 0), (1, 3)):
+
+        @pl.when(jnp.logical_and(mine, z == chip))
+        def _():
+            pltpu.make_async_copy(cot_hbm.at[k], g_in.at[row_slot], g_sem.at[z // 2]).start()
+
+    @pl.when(role == 1)
+    def _():
+        cot_copies(lambda copy: copy.start())
+    def relay_steps(start, stop):
         def one(n, carry):
             relay(n)
             return carry
 
-        lax.fori_loop(start, jnp.where(when, stop, start), one, 0)
-
-    early = role == 0
-    relay_while(0, UNITS + 3, role == 1)
-    for k, chip in ((0, 0), (1, 3)):
-        send_block(cot_hbm, g_in, g_sem, k, chip, role == 1)
+        lax.fori_loop(start, stop, one, 0)
+
+    relay_steps(0, jnp.where(role == 1, AHEAD, 0))
     arrived(wq.at[z], own_sem.at[0])
     arrived(wo.at[z], own_sem.at[1])
     arrived(wud.at[z, 0:1024], own_sem.at[2])
@@ -691,15 +749,18 @@
     def vector(k, q=0, width=1024):
         return vec[q, k : k + 1, 0:width]
 
-    rows_total = 2 * BLOCK
-    chunks = rows_total // CHUNK
-
-    def over_rows(action, start=0, stop=chunks):
+    def columns(n, width):
+        return pl.ds(pl.multiple_of(n * width, width), width)
+
+    def block_rows(j):
+        return pl.ds(pl.multiple_of(j * BLOCK, BLOCK), BLOCK)
+
+    def over_rows(j, action):
         def one(c, carry):
-            action(pl.ds(pl.multiple_of(c * CHUNK, CHUNK), CHUNK))
+            action(pl.ds(pl.multiple_of(j * BLOCK + c * CHUNK, CHUNK), CHUNK))
             return carry
 
-        lax.fori_loop(start, stop, one, 0)
+        lax.fori_loop(0, BLOCK // CHUNK, one, 0)
 
     def standardize(v):
         average = jnp.mean(v, axis=-1, keepdims=True)
@@ -713,51 +774,40 @@
         e = incoming * gain
         return (e - jnp.mean(e, axis=-1, keepdims=True) - xhat * jnp.mean(e * xhat, axis=-1, keepdims=True)) * inverse
 
-    def columns(n, width=256):
-        return pl.ds(pl.multiple_of(n * width, width), width)
-
-    for j in range(2):
-        arrived(x_in.at[j * BLOCK : (j + 1) * BLOCK], x_sem.at[j])
-
-    def norm_one(rows):
-        centred, inverse = standardize(x_in[rows, :].astype(jnp.float32))
-        normed[rows, :] = (centred * inverse * vector(0) + vector(1)).astype(jnp.bfloat16)
-
-    over_rows(norm_one)
-    first_all = lax.broadcasted_iota(jnp.int32, (rows_total, 128), 1) < HEAD_DIM
-
-    def project(q, carry):
-        triple = dot_nn(normed[...], wq[q]) + vec[q, 7:8, 0:768]
-        for p in range(2):
-            t0, t1, t2 = (triple[:, p * 384 + n * 128 : p * 384 + n * 128 + 128] for n in range(3))
-            q_own[2 * q + p] = jnp.where(first_all, t0, t1).astype(jnp.bfloat16)
-            kv[s, 2 * q + p, 0] = pltpu.roll(jnp.where(first_all, t2, t0), 64, 1).astype(jnp.bfloat16)
-            kv[s, 2 * q + p, 1] = jnp.where(first_all, t1, t2).astype(jnp.bfloat16)
-        pltpu.make_async_remote_copy(
-            src_ref=kv.at[s, pl.ds(2 * q, 2)], dst_ref=kv.at[s, pl.ds(2 * q, 2)],
-            send_sem=kv_ssem.at[q], recv_sem=kv_rsem.at[q], device_id=(other, d, z), device_id_type=MESH,
-        ).start()
-        return carry
-
-    lax.fori_loop(0, 4, project, 0)
-
-    def kv_wait(q, carry):
-        pltpu.make_async_remote_copy(
-            src_ref=kv.at[s, pl.ds(2 * q, 2)], dst_ref=kv.at[other, pl.ds(2 * q, 2)],
-            send_sem=kv_ssem.at[q], recv_sem=kv_rsem.at[q], device_id=(other, d, z), device_id_type=MESH,
-        ).wait()
-        return carry
-
-    lax.fori_loop(0, 4, kv_wait, 0)
+    def to_core(ref, send_sem, recv_sem):
+        return pltpu.make_async_remote_copy(
+            src_ref=ref, dst_ref=ref, send_sem=send_sem, recv_sem=recv_sem,
+            device_id=(other, d, z), device_id_type=MESH,
+        )
 
     scale = LOG2E * HEAD_DIM ** (-0.5)
 
-    def key_rows(kb):
-        return pl.ds(pl.multiple_of((kb // 2) * BLOCK, BLOCK), BLOCK)
-
-    def attend_rows(pair, j, blocks):
+    def enter(j):
+        rows = block_rows(j)
+        arrived(x_in.at[rows], x_sem.at[j])
+
+        def norm_one(rows):
+            centred, inverse = standardize(x_in[rows, :].astype(jnp.float32))
+            normed[rows, :] = (centred * inverse * vector(0) + vector(1)).astype(jnp.bfloat16)
+
+        over_rows(j, norm_one)
+
+        def project(q, carry):
+            triple = dot_nn(normed[rows, :], wq[q]) + vec[q, 7:8, 0:768]
+            for p in range(2):
+                t0, t1, t2 = (triple[:, p * 384 + n * 128 : p * 384 + n * 128 + 128] for n in range(3))
+                q_own[2 * q + p, rows, :] = jnp.where(first, t0, t1).astype(jnp.bfloat16)
+                kv[s, 2 * q + p, 0, rows, :] = pltpu.roll(jnp.where(first, t2, t0), 64, 1).astype(jnp.bfloat16)
+                kv[s, 2 * q + p, 1, rows, :] = jnp.where(first, t1, t2).astype(jnp.bfloat16)
+            to_core(kv.at[s, pl.ds(2 * q, 2), :, rows], kv_ssem.at[j, q], kv_rsem.at[j, q]).start()
+            return carry
+
+        lax.fori_loop(0, 4, project, 0)
+
+    def attend_rows(pair, core, j):
         cols = columns(pair, 128)
         rows = slice(j * BLOCK, j * BLOCK + BLOCK)
+        blocks = block_of(core, j) + 1
         q_pair = q_own[pair, rows, :]
         q_half = (q_pair * half0, q_pair * half1)
         t_pre = dot_nt(q_pair, kp[pair]) * scale + pre_mask
@@ -786,243 +836,252 @@
         logs = [highest[h] + jnp.log(total[h]) * LOG2E for h in range(2)]
         lse[pair, rows, :] = jnp.where(first, logs[0], logs[1])
 
-    def attend_all():
+    def attend(j, relay_at):
+        def kv_wait(q, carry):
+            to_core(kv.at[s, pl.ds(2 * q, 2), :, block_rows(j)], kv_ssem.at[j, q], kv_rsem.at[j, q]).wait_send()
+            arrived(kv.at[other, pl.ds(2 * q, 2), :, block_rows(j)], kv_rsem.at[j, q])
+            return carry
+
+        lax.fori_loop(0, 4, kv_wait, 0)
         for core in range(2):
-
-            @pl.when(s == core)
-            def _():
-                def attend_pair(pair, carry):
-                    relay_while(pair // 2, pair // 2 + pair % 2, early)
-                    for j in range(2):
-                        attend_rows(pair, j, block_of(core, j) + 1)
-                    return carry
-
-                lax.fori_loop(0, 8, attend_pair, 0)
-
-    attend_all()
-
-    def out_project(n, carry):
-        cols = columns(n)
-        part_sum = jnp.zeros((rows_total, 256), jnp.float32)
-        for q in range(4):
-            part_sum += dot_nn(o_own[:, q * 256 : q * 256 + 256], wo[q, :, cols])
-        after[:, cols] = x_in[:, cols].astype(jnp.float32) + part_sum + vec[0, 2:3, cols]
+            for block in range(2):
+
+                @pl.when(jnp.logical_and(s == core, j == block))
+                def _():
+                    def attend_pair(pair, carry):
+                        relay_steps(relay_at, jnp.where(jnp.logical_and(pair == 4, role == 0), relay_at + 1, relay_at))
+                        attend_rows(pair, core, block)
+                        return carry
+
+                    lax.fori_loop(0, 8, attend_pair, 0)
+
+        rows = block_rows(j)
+        after[rows, :] = (
+            x_in[rows, :].astype(jnp.float32) + dot_nn(o_own[rows, :], wo[...].reshape(1024, 1024)) + vector(2)
+        )
+
+        def norm_two(rows):
+            centred, inverse = standardize(after[rows, :])
+            normed[rows, :] = (centred * inverse * vector(3) + vector(4)).astype(jnp.bfloat16)
+            acc[rows, :] = after[rows, :] + vector(5)
+
+        over_rows(j, norm_two)
+
+    def feed(j, i):
+        rows = block_rows(j)
+        q = quarter(i)
+        u = dot_nn(normed[rows, :], wud[q, 0:1024, :]) + vec[q, 6:7, :]
+        u2 = u * u
+        t = jnp.tanh(u * (GELU_A + (GELU_A * GELU_B) * u2))
+        half_t = 0.5 + 0.5 * t
+        wide[rows, :] = (u * half_t).astype(jnp.bfloat16)
+        inner = u * (GELU_A + (3.0 * GELU_A * GELU_B) * u2)
+        slope[q, rows, :] = (half_t + 0.5 * inner * (1.0 - t * t)).astype(jnp.bfloat16)
+        acc[rows, :] += dot_nn(wide[rows, :], wud[q, 1024:2048, :])
+
+    def hand_copies(j, k):
+        rows = block_rows(j)
+        landing, sem = ((x_in, x_sem), (act_out, act_sem), (g_in, g_sem), (ig_out, ig_sem))[k]
+        if k % 2:
+            dst, sem, target = landing.at[micro], sem.at[micro], (role, d, block_of(s, j))
+        else:
+            dst, sem, target = landing.at[rows], sem.at[j], (s, d, partner)
+        return pltpu.make_async_remote_copy(
+            src_ref=y_out.at[rows], dst_ref=dst, send_sem=hand_sem.at[k, j], recv_sem=sem,
+            device_id=target, device_id_type=MESH,
+        )
+
+    def hand_on(j):
+        rows = block_rows(j)
+        y_out[rows, :] = acc[rows, :].astype(jnp.bfloat16)
+
+        @pl.when(role == 0)
+        def _():
+            hand_copies(j, 0).start()
+
+        hand_copies(j, 1).start()
+
+    def upto(n, table):
+        total = jnp.int32(0)
+        for k, entry in enumerate(table):
+            total += jnp.where(n >= k, entry - (table[k - 1] if k else 0), 0)
+        return total
+
+    early_table = (0, 1, 2, 4, 6, 7, 8, 9, 11, 13, 15, 15, 15, 15)
+    late_table = (AHEAD, 9, 10, 11, 13, 15, 15, 15, 15, 15, 15, 15, 15, 15)
+
+    def forward(n, carry):
+        stage = jnp.where(role == 0, n // 2, n % 7)
+        j = jnp.where(role == 0, n % 2, n // 7)
+        before = jnp.where(
+            role == 0,
+            jnp.where(n == 0, 0, upto(n - 1, early_table)) + jnp.where(jnp.logical_or(n == 3, n == 4), 1, 0),
+            jnp.where(n == 0, AHEAD, upto(n - 1, late_table)),
+        )
+        until = jnp.where(role == 0, upto(n, early_table), upto(n, late_table))
+        relay_steps(before, until)
+
+        @pl.when(jnp.logical_and(role == 0, n == 6))
+        def _():
+            cot_copies(lambda copy: copy.start())
+
+        @pl.when(stage == 0)
+        def _():
+            enter(j)
+
+        @pl.when(stage == 1)
+        def _():
+            attend(j, until)
+
+        @pl.when(jnp.logical_and(stage >= 2, stage < 6))
+        def _():
+            feed(j, stage - 2)
+
+        @pl.when(stage == 6)
+        def _():
+            hand_on(j)
+
         return carry
 
-    lax.fori_loop(0, 4, out_project, 0)
-    relay_while(4, 5, early)
-
-
-    def norm_two(rows):
-        centred, inverse = standardize(after[rows, :])
-        normed[rows, :] = (centred * inverse * vector(3) + vector(4)).astype(jnp.bfloat16)
-        acc[rows, :] = after[rows, :] + vector(5)
-
-    over_rows(norm_two)
-
-    def feed_quarter(i, carry):
-        q = (z + i) % 4
-        relay_while(jnp.where(i == 1, 6, 4 * i + 1), 4 * i + 3, jnp.logical_and(early, i > 0))
-
-        def up(n, carry):
-            cols = columns(n)
-            inside = jnp.logical_and(n % 2 == 1, jnp.logical_and(i < 3, jnp.logical_or(i > 0, n == 1)))
-            step = jnp.where(i == 0, 5, 4 * i + 3 + n // 2)
-            relay_while(step, step + 1, jnp.logical_and(early, inside))
-            for half in range(2):
-                rows = slice(half * BLOCK, half * BLOCK + BLOCK)
-                u = dot_nn(normed[rows, :], wud[q, 0:1024, cols]) + vec[q, 6:7, cols]
-                u2 = u * u
-                t = jnp.tanh(u * (GELU_A + (GELU_A * GELU_B) * u2))
-                half_t = 0.5 + 0.5 * t
-                wide[rows, cols] = (u * half_t).astype(jnp.bfloat16)
-                inner = u * (GELU_A + (3.0 * GELU_A * GELU_B) * u2)
-                slope[q, rows, cols] = (half_t + 0.5 * inner * (1.0 - t * t)).astype(jnp.bfloat16)
+    lax.fori_loop(0, 14, forward, 0)
+
+    def back_rows(pair, core, j):
+        cols = columns(pair, 128)
+        rows = slice(j * BLOCK, j * BLOCK + BLOCK)
+        q_pair = q_own[pair, rows, :]
+        q_half = (q_pair * half0, q_pair * half1)
+        g_pair = wide[rows, cols]
+        g_half = (g_pair * half0, g_pair * half1)
+        product = g_pair.astype(jnp.float32) * o_own[rows, cols].astype(jnp.float32)
+        row_term = [
+            jnp.sum(jnp.where(first, product, 0.0), axis=1, keepdims=True),
+            jnp.sum(jnp.where(first, 0.0, product), axis=1, keepdims=True),
+        ]
+        logs = lse[pair, rows, :]
+        log_half = (logs[:, 0:1], logs[:, 64:65])
+        p_pre = jnp.exp2(dot_nt(q_pair, kp[pair]) * scale + pre_mask - logs)
+        dp_pre = dot_nt(g_pair, vp[pair])
+        ds_pre = (p_pre * (dp_pre - jnp.where(first, row_term[0], row_term[1]))).astype(jnp.bfloat16)
+        pv = dot_tn(p_pre.astype(jnp.bfloat16), g_pair)
+        pk = dot_tn(ds_pre, q_pair)
+        pk = jnp.where(first16, pk[0:16, :], pk[64:80, :]) * HEAD_DIM ** (-0.5)
+        pv = jnp.where(first16, pv[0:16, :], pv[64:80, :])
+        pg[pair, 0] = pk if j else pg[pair, 0] + pk
+        pg[pair, 1] = pv if j else pg[pair, 1] + pv
+        dq_pre = dot_nn(ds_pre, kp[pair])
+        dqs = [jnp.zeros((BLOCK, 128), jnp.float32) for _ in range(2)]
+        for kb in range(4):
+            held = dkv_own if core_of(kb) == core else dkv_send
+            at = slice((kb // 2) * BLOCK, (kb // 2 + 1) * BLOCK)
+            if kb > block_of(core, j):
+                if j:
+                    held[pair, 0, at, :] = jnp.zeros((BLOCK, 128), jnp.bfloat16)
+                    held[pair, 1, at, :] = jnp.zeros((BLOCK, 128), jnp.bfloat16)
+                continue
+            keys = kv[core_of(kb), pair, 0, at, :]
+            values = kv[core_of(kb), pair, 1, at, :]
+            dv, dk = 0.0, 0.0
+            if j == 0:
+                dk = held[pair, 0, at, :].astype(jnp.float32)
+                dv = held[pair, 1, at, :].astype(jnp.float32)
+            for h in range(2):
+                probs = jnp.exp2(dot_nt(q_half[h], keys) * scale + bias[j, kb] - log_half[h])
+                grad_probs = dot_nt(g_half[h], values)
+                grad_scores = (probs * (grad_probs - row_term[h])).astype(jnp.bfloat16)
+                dv += dot_tn(probs.astype(jnp.bfloat16), g_half[h])
+                dk += dot_tn(grad_scores, q_half[h])
+                dqs[h] += dot_nn(grad_scores, keys)
+            held[pair, 0, at, :] = dk.astype(jnp.bfloat16)
+            held[pair, 1, at, :] = dv.astype(jnp.bfloat16)
+        dq = (jnp.where(first, dqs[0], dqs[1]) + dq_pre) * HEAD_DIM ** (-0.5)
+        q_own[pair, rows, :] = dq.astype(jnp.bfloat16)
+
+    def dkv_copy(j, pair):
+        rows = block_rows(j)
+        return pltpu.make_async_remote_copy(
+            src_ref=dkv_send.at[pair, :, rows], dst_ref=dkv_recv.at[pair, :, rows],
+            send_sem=dkv_ssem.at[j, pair], recv_sem=dkv_rsem.at[j, pair],
+            device_id=(other, d, z), device_id_type=MESH,
+        )
+
+    contribution = micro * 2 + s
+
+    def backward(n, carry):
+        j = 1 - n
+        rows = block_rows(j)
+        arrived(g_in.at[rows], g_sem.at[j])
+        acc[rows, :] = jnp.zeros((BLOCK, 1024), jnp.float32)
+
+        def feed_back(q, carry):
+            grad_act = dot_nt(g_in[rows, :], wud[q, 1024:2048, :])
+            wide[rows, :] = (grad_act * slope[q, rows, :].astype(jnp.float32)).astype(jnp.bfloat16)
+            acc[rows, :] += dot_nt(wide[rows, :], wud[q, 0:1024, :])
             return carry
 
-        lax.fori_loop(0, 4, up, 0)
-
-        def down(n, carry):
-            cols = columns(n)
-            acc[:, cols] += dot_nn(wide[...], wud[q, 1024:2048, cols])
+        lax.fori_loop(0, 4, feed_back, 0)
+
+        def middle(rows):
+            dv = norm_back(after[rows, :], vector(3), acc[rows, :])
+            normed[rows, :] = (g_in[rows, :].astype(jnp.float32) + dv).astype(jnp.bfloat16)
+
+        over_rows(j, middle)
+        wide[rows, :] = dot_nt(normed[rows, :], wo[...].reshape(1024, 1024)).astype(jnp.bfloat16)
+        for core in range(2):
+            for block in range(2):
+
+                @pl.when(jnp.logical_and(s == core, j == block))
+                def _():
+                    def back_pair(pair, carry):
+                        back_rows(pair, core, block)
+                        dkv_copy(block, pair).start()
+                        return carry
+
+                    lax.fori_loop(0, 8, back_pair, 0)
+
+        acc[rows, :] = jnp.zeros((BLOCK, 1024), jnp.float32)
+
+        def project_back(q, carry):
+            for p in range(2):
+                pair = 2 * q + p
+                dkv_copy(j, pair).wait()
+                dq = q_own[pair, rows, :].astype(jnp.float32)
+                dk = dkv_own[pair, 0, rows, :].astype(jnp.float32) + dkv_recv[pair, 0, rows, :].astype(jnp.float32)
+                dv = dkv_own[pair, 1, rows, :].astype(jnp.float32) + dkv_recv[pair, 1, rows, :].astype(jnp.float32)
+                dk = pltpu.roll(dk * HEAD_DIM ** (-0.5), 64, 1)
+                gt[:, p * 384 : p * 384 + 128] = jnp.where(first, dq, dk).astype(jnp.bfloat16)
+                gt[:, p * 384 + 128 : p * 384 + 256] = jnp.where(first, dv, dq).astype(jnp.bfloat16)
+                gt[:, p * 384 + 256 : p * 384 + 384] = jnp.where(first, dk, dv).astype(jnp.bfloat16)
+            acc[rows, :] += dot_nt(gt[...], wq[q])
             return carry
 
-        lax.fori_loop(0, 4, down, 0)
+        lax.fori_loop(0, 4, project_back, 0)
+
+        @pl.when(role == 0)
+        def _():
+            hand_copies(j, 0).wait_send()
+
+        hand_copies(j, 1).wait_send()
+
+        def give_back(rows):
+            dv = norm_back(x_in[rows, :].astype(jnp.float32), vector(0), acc[rows, :])
+            y_out[rows, :] = (normed[rows, :].astype(jnp.float32) + dv).astype(jnp.bfloat16)
+
+        over_rows(j, give_back)
+
+        @pl.when(role == 1)
+        def _():
+            hand_copies(j, 2).start()
+
+        hand_copies(j, 3).start()
         return carry
 
-    lax.fori_loop(0, 4, feed_quarter, 0)
-    for k, chip in ((0, 0), (1, 3)):
-        send_block(cot_hbm, g_in, g_sem, k, chip, role == 0)
-
-    def give_out(rows):
-        y_out[rows, :] = acc[rows, :].astype(jnp.bfloat16)
-
-    def send_rows(j, out, sem):
-        block = block_of(s, j)
-        rows = slice(j * BLOCK, j * BLOCK + BLOCK)
-        sends.start_or_keep(
-            y_out.at[rows], out.at[micro], sem.at[micro], (role, d, block),
-            jnp.logical_and(role == s, z == block),
-        )
-
-    for j in range(2):
-        over_rows(give_out, j * chunks // 2, (j + 1) * chunks // 2)
-        rows = slice(j * BLOCK, j * BLOCK + BLOCK)
-        sends.start(y_out.at[rows], x_in.at[rows], x_sem.at[j], (s, d, partner), when=role == 0)
-    for j in range(2):
-        send_rows(j, act_out, act_sem)
-
-    for j in range(2):
-        arrived(g_in.at[j * BLOCK : (j + 1) * BLOCK], g_sem.at[j])
-
-    def clear(rows):
-        acc[rows, :] = jnp.zeros((CHUNK, 1024), jnp.float32)
-
-    over_rows(clear)
-
-    def feed_back(q, carry):
-        def down(n, carry):
-            cols = columns(n)
-            for half in range(2):
-                rows = slice(half * BLOCK, half * BLOCK + BLOCK)
-                grad_act = dot_nt(g_in[rows, :], wud[q, pl.ds(pl.multiple_of(1024 + n * 256, 256), 256), :])
-                wide[rows, cols] = (grad_act * slope[q, rows, cols].astype(jnp.float32)).astype(jnp.bfloat16)
-            return carry
-
-        lax.fori_loop(0, 4, down, 0)
-
-        def up(n, carry):
-            cols = columns(n)
-            acc[:, cols] += dot_nt(wide[...], wud[q, cols, :])
-            return carry
-
-        lax.fori_loop(0, 4, up, 0)
-        return carry
-
-    lax.fori_loop(0, 4, feed_back, 0)
-
-    def middle(rows):
-        dv = norm_back(after[rows, :], vector(3), acc[rows, :])
-        normed[rows, :] = (g_in[rows, :].astype(jnp.float32) + dv).astype(jnp.bfloat16)
-
-    over_rows(middle)
-
-    def mix_back(q, carry):
-        wide[:, columns(q)] = dot_nt(normed[...], wo[q]).astype(jnp.bfloat16)
-        return carry
-
-    lax.fori_loop(0, 4, mix_back, 0)
-
-    def back_pair(pair, carry):
-        cols = columns(pair, 128)
-        dk_acc[...] = jnp.zeros(dk_acc.shape, jnp.float32)
-        dv_acc[...] = jnp.zeros(dv_acc.shape, jnp.float32)
-        pk_acc[...] = jnp.zeros(pk_acc.shape, jnp.float32)
-        pv_acc[...] = jnp.zeros(pv_acc.shape, jnp.float32)
-
-        def back_rows(j, blocks):
-            rows = slice(j * BLOCK, j * BLOCK + BLOCK)
-            q_pair = q_own[pair, rows, :]
-            q_half = (q_pair * half0, q_pair * half1)
-            g_pair = wide[rows, cols]
-            g_half = (g_pair * half0, g_pair * half1)
-            product = g_pair.astype(jnp.float32) * o_own[rows, cols].astype(jnp.float32)
-            row_term = [
-                jnp.sum(jnp.where(first, product, 0.0), axis=1, keepdims=True),
-                jnp.sum(jnp.where(first, 0.0, product), axis=1, keepdims=True),
-            ]
-            logs = lse[pair, rows, :]
-            log_half = (logs[:, 0:1], logs[:, 64:65])
-            p_pre = jnp.exp2(dot_nt(q_pair, kp[pair]) * scale + pre_mask - logs)
-            dp_pre = dot_nt(g_pair, vp[pair])
-            ds_pre = (p_pre * (dp_pre - jnp.where(first, row_term[0], row_term[1]))).astype(jnp.bfloat16)
-            pv_acc[...] += dot_tn(p_pre.astype(jnp.bfloat16), g_pair)
-            pk_acc[...] += dot_tn(ds_pre, q_pair)
-            dq_pre = dot_nn(ds_pre, kp[pair])
-            dqs = [jnp.zeros((BLOCK, 128), jnp.float32) for _ in range(2)]
-            for kb in range(blocks):
-                keys = kv[core_of(kb), pair, 0, (kb // 2) * BLOCK : (kb // 2 + 1) * BLOCK, :]
-                values = kv[core_of(kb), pair, 1, (kb // 2) * BLOCK : (kb // 2 + 1) * BLOCK, :]
-                at = slice(kb * BLOCK, kb * BLOCK + BLOCK)
-                dv, dk = 0.0, 0.0
-                for h in range(2):
-                    probs = jnp.exp2(dot_nt(q_half[h], keys) * scale + bias[j, kb] - log_half[h])
-                    grad_probs = dot_nt(g_half[h], values)
-                    grad_scores = (probs * (grad_probs - row_term[h])).astype(jnp.bfloat16)
-                    dv += dot_tn(probs.astype(jnp.bfloat16), g_half[h])
-                    dk += dot_tn(grad_scores, q_half[h])
-                    dqs[h] += dot_nn(grad_scores, keys)
-                dv_acc[at, :] += dv
-                dk_acc[at, :] += dk
-            dq = (jnp.where(first, dqs[0], dqs[1]) + dq_pre) * HEAD_DIM ** (-0.5)
-            q_own[pair, rows, :] = dq.astype(jnp.bfloat16)
-
-        for core in range(2):
-
-            @pl.when(s == core)
-            def _():
-                for j in range(2):
-                    back_rows(j, block_of(core, j) + 1)
-
-        for j in range(2):
-            rows = slice(j * BLOCK, j * BLOCK + BLOCK)
-            for owner_core, held in ((s, dkv_own), (other, dkv_send)):
-                at = pl.ds(pl.multiple_of(block_of(owner_core, j) * BLOCK, BLOCK), BLOCK)
-                held[pair, 0, rows, :] = dk_acc[at, :].astype(jnp.bfloat16)
-                held[pair, 1, rows, :] = dv_acc[at, :].astype(jnp.bfloat16)
-        pltpu.make_async_remote_copy(
-            src_ref=dkv_send.at[pair], dst_ref=dkv_recv.at[pair], send_sem=dkv_ssem.at[pair],
-            recv_sem=dkv_rsem.at[pair], device_id=(other, d, z), device_id_type=MESH,
-        ).start()
-        pg[pair, 0] = jnp.where(first16, pk_acc[0:16, :], pk_acc[64:80, :]) * HEAD_DIM ** (-0.5)
-        pg[pair, 1] = jnp.where(first16, pv_acc[0:16, :], pv_acc[64:80, :])
-        return carry
-
-    lax.fori_loop(0, 8, back_pair, 0)
-    contribution = micro * 2 + s
+    lax.fori_loop(0, 2, backward, 0)
     for q in range(4):
         sends.start_or_keep(
             pg.at[2 * q : 2 * q + 2], pg_near.at[contribution], pg_sem.at[contribution], (role, d, q),
             jnp.logical_and(role == s, z == q),
         )
-    over_rows(clear)
-
-    def project_back(q, carry):
-        for p in range(2):
-            pair = 2 * q + p
-            pltpu.make_async_remote_copy(
-                src_ref=dkv_send.at[pair], dst_ref=dkv_recv.at[pair], send_sem=dkv_ssem.at[pair],
-                recv_sem=dkv_rsem.at[pair], device_id=(other, d, z), device_id_type=MESH,
-            ).wait()
-            dq = q_own[pair].astype(jnp.float32)
-            dk = (dkv_own[pair, 0].astype(jnp.float32) + dkv_recv[pair, 0].astype(jnp.float32)) * HEAD_DIM ** (-0.5)
-            dv = dkv_own[pair, 1].astype(jnp.float32) + dkv_recv[pair, 1].astype(jnp.float32)
-            dk = pltpu.roll(dk, 64, 1)
-            gt[:, p * 384 : p * 384 + 128] = jnp.where(first_all, dq, dk).astype(jnp.bfloat16)
-            gt[:, p * 384 + 128 : p * 384 + 256] = jnp.where(first_all, dv, dq).astype(jnp.bfloat16)
-            gt[:, p * 384 + 256 : p * 384 + 384] = jnp.where(first_all, dk, dv).astype(jnp.bfloat16)
-
-        def columns_back(n, carry):
-            cols = columns(n)
-            acc[:, cols] += dot_nt(gt[...], wq[q, cols, :])
-            return carry
-
-        lax.fori_loop(0, 4, columns_back, 0)
-        return carry
-
-    lax.fori_loop(0, 4, project_back, 0)
-    sends.finish()
-
-    def give_back(rows):
-        dv = norm_back(x_in[rows, :].astype(jnp.float32), vector(0), acc[rows, :])
-        y_out[rows, :] = (normed[rows, :].astype(jnp.float32) + dv).astype(jnp.bfloat16)
-
-    for j in range(2):
-        over_rows(give_back, j * chunks // 2, (j + 1) * chunks // 2)
-        rows = slice(j * BLOCK, j * BLOCK + BLOCK)
-        sends.start(y_out.at[rows], g_in.at[rows], g_sem.at[j], (s, d, partner), when=role == 1)
-    for j in range(2):
-        send_rows(j, ig_out, ig_sem)
+
     for k in range(4):
         arrived(pg_near.at[k], pg_sem.at[k])
     pg_far[d] = (pg_near[0] + pg_near[1]) + (pg_near[2] + pg_near[3])
@@ -1056,12 +1115,28 @@
     def _():
         lax.fori_loop(0, 3, supply_done, 0)
 
+        def firsts_done(i, carry):
+            for w in range(2):
+                supply_first(w, i, lambda copy: copy.wait_send())
+            return carry
+
+        lax.fori_loop(0, 3, firsts_done, 0)
+
     def relays_done(m, carry):
         for stage in range(3):
             relay_copy(m, stage).wait_send()
         return carry
 
     lax.fori_loop(0, UNITS, relays_done, 0)
+    cot_copies(lambda copy: copy.wait_send())
+    for j in range(2):
+
+        @pl.when(role == 1)
+        def _():
+            hand_copies(j, 2).wait_send()
+
+        hand_copies(j, 3).wait_send()
+
     for k in range(2):
         arrived(act_out.at[k], act_sem.at[k])
         arrived(ig_out.at[k], ig_sem.at[k])
@@ -1083,15 +1158,15 @@
         vm((4, rows, wu.shape[1]), bf), vm((rows, wu.shape[1]), bf),
         vm((pairs, 2, 16, 128), f32), vm((4, 2, 2, 16, 128), f32), vm((4, 2, 2, 16, 128), f32), vm((8, 16, pw.shape[0]), f32),
         vm((2, 4, BLOCK, BLOCK), f32),
-        vm((4 * BLOCK, 128), f32), vm((4 * BLOCK, 128), f32),
         vm((pairs, 2, rows, 128), bf), vm((pairs, 2, rows, 128), bf), vm((pairs, 2, rows, 128), bf),
-        vm((pairs, 128, 128), bf), vm((pairs, 128, 128), bf), vm((128, 128), f32), vm((128, 128), f32),
-        vm((rows, wq.shape[1]), bf),
+        vm((pairs, 128, 128), bf), vm((pairs, 128, 128), bf),
+        vm((BLOCK, wq.shape[1]), bf),
         dma((96,)), dma((4,)), dma((4,)), dma((2,)), dma((2,)), dma((2,)), dma((2,)), dma((4,)),
         dma((2, 4)), dma((2, 4)), dma((2, 4)), dma((2, 4)),
-        dma((UNITS,)), dma((UNITS,)), dma((UNITS,)), dma((UNITS,)), dma((UNITS, 2)), dma((UNITS,)), dma((UNITS,)), dma((UNITS,)),
+        dma((UNITS,)), dma((UNITS,)), dma((UNITS,)), dma((UNITS,)), dma((6, 2)), dma((UNITS, 2)), dma((UNITS,)), dma((UNITS,)), dma((UNITS,)),
         pltpu.SemaphoreType.REGULAR,
-        dma((4,)), dma((4,)), dma((pairs,)), dma((pairs,)), dma((4,)), dma((4,)), dma((8,)),
+        dma((2, 4)), dma((2, 4)), dma((2, pairs)), dma((2, pairs)), dma((4,)), dma((4,)), dma((8,)),
+        dma((4, 2)), dma((2,)),
     ]
     anywhere = pl.BlockSpec(memory_space=pl.ANY)
     return pl.pallas_call(

time: 420 us -> 362 us (0.86)
  Pallas kernels: 401 us -> 344 us
    pallas_call x1, Pallas kernels: 401 us -> 344 us  [run_layers(): pl.pallas_call(layer_kernel, out_shape=(jax.ShapeDtypeStruct(x.shape, bf)...]
where the time goes in v4:
time: 362 us; the launch traced here: 361 us
  Pallas kernels  344 us (95%)
  local copies, waits for them, and re-layouts  6 us (2%)
  matrix products  5.45 us (2%)
  other arithmetic  4.77 us (1%)
    pallas_call x1, Pallas kernels, run_layers(): pl.pallas_call(layer_kernel, out_shape=(jax.ShapeDtypeStruct(x.shape, bf)...  344 us

profile of v4, /device:TPU:0, one launch (start us, length us, event | category | flops | bytes accessed | tf_op | source)
XLA Modules:
  0.0 361.3 jit_solution(11331683401115275538)
XLA Ops:
  0.6 0.0 copy-start
  0.6 0.7 convert_element_type.18
  1.3 0.1 copy-done
  1.4 1.5 fusion
  2.9 0.7 convert_element_type.36
  3.6 1.2 fusion.1
  4.8 0.6 pad.10.pre_hbm
  5.4 0.7 pad.9
  6.1 0.8 concatenate.5
  6.9 0.6 concatenate.6.vec_hbm
  7.6 1.4 reduce_window_sum.11.ends
  9.0 344.4 %two_layers.1 = (bf16[2,256,1024]{2,1,0:T(8,128)(2,1)}, bf16[2,256,1024]{2,1,0:T(8,128)(2,1)}, f32[16,512]{1,0:T(8,128)}, f32[16,512]{1,0:T(8,128)}) custom-call(bf16[2,256,1024]{2,1,0:T(8,128)(2,1)} %bitcast.25, bf16[2,256,1024]{2,1,0:T(8,128)(2,1)} %bitcast.26, bf16[1024,768]{1,0:T(8,128)(2,1)} %bitcast.24, bf16[256,1024]{1,0:T(8,128)(2,1)} %bitcast.29, ...), custom_call_target="tpu_custom_call" | custom-call | tf_op jit(solution)/shard_map/two_layers/pallas_call | solution.py:1172
  353.4 1.4 convert_reduce_fusion.1
  354.7 0.5 convolution_bitcast_fusion
  355.2 0.0 copy-start.1
  355.2 0.0 copy-start.4
  355.2 1.8 copy.29
  357.0 0.0 copy-done.1
  357.0 1.0 fusion.5
  358.1 0.0 copy-done.4
  358.1 1.3 fusion.2
  359.4 0.0 copy-done.3
  359.4 1.0 copy.32
  360.3 1.0 copy.33
  (3 shorter events, 0.0 us)
Async XLA Ops:
  0.6 0.8 copy-start
  355.2 1.8 copy-start.1
  355.2 2.9 copy-start.4
  357.0 2.3 copy-start.3
  357.0 3.3 copy-start.2

commit v5 on v4

--- a/solution.py
+++ b/solution.py
@@ -351,7 +351,7 @@
 MESH = pl.DeviceIdType.MESH
 BLOCK = 256
 LOG2E = 1.4426950408889634
-CHUNK = 32
+CHUNK = 128
 UNITS = 12
 AHEAD = 8
 UNIT_ROWS = 512
@@ -416,15 +416,16 @@
 
 
 def layer_kernel(
-    x_hbm, cot_hbm, wq_hbm, wo_hbm, wu_hbm, wd_hbm, vec_hbm, pre_hbm, pw, ends,
-    act_out, ig_out, sum_out, hidden_out,
-    wq, wo, wud, vec, pre,
+    x_hbm, cot_hbm, wq_hbm, wo_hbm, wu_hbm, wd_hbm,
+    g1, s1, bo, g2, s2, bd, bu, bq, table, mid_w, mid_b, pw, pb, lengths,
+    act_out, ig_out, sum_out, hidden_out, tanh_out,
+    vec_own, pre_full, pre_own, wq, wo, wud, vec, pre,
     x_in, g_in, y_out, normed, kv, q_own, o_own, lse, bias, after, acc, slope, wide,
-    pg, pg_near, pg_far, hidden_all, ts, dkv_own, dkv_send, dkv_recv, kp, vp, gt,
+    pg, pg_near, pg_far, hidden_core, hidden_all, ts, dkv_own, dkv_send, dkv_recv, kp, vp, gt,
     ssem, vec_sem, pre_sem, x_sem, g_sem, act_sem, ig_sem, own_sem, z_sem, a_sem, b_sem, c_sem,
     zr_sem, ar_sem, br_sem, cr_sem, fs_sem, zs_sem, as_sem, bs_sem, cs_sem, go_sem,
-    kv_ssem, kv_rsem, dkv_ssem, dkv_rsem, pg_sem, far_sem, hidden_sem,
-    hand_sem, cot_sem,
+    kv_ssem, kv_rsem, dkv_ssem, dkv_rsem, pg_sem, far_sem, core_sem, hidden_sem,
+    hand_sem, cot_sem, pg_ssem, far_ssem, mid_sem,
 ):
     s, d, z = lax.axis_index("section"), lax.axis_index("dp"), lax.axis_index("mp")
     role, micro = role_of(z), z // 2
@@ -469,8 +470,7 @@
         for t in planes:
             for h in range(2):
                 is_here = jnp.logical_and(z == t, s == h)
-                sends.start_or_keep(vec_hbm, vec.at[z], vec_sem.at[z], (h, d, t), is_here, when)
-                sends.start_or_keep(pre_hbm, pre.at[z], pre_sem.at[z], (h, d, t), is_here, when)
+                sends.start_or_keep(pre_own, pre.at[z], pre_sem.at[z], (h, d, t), is_here, when)
 
     def send_x(when):
         for k, chip in ((0, 1), (1, 2)):
@@ -516,11 +516,10 @@
 
             lax.fori_loop(0, 3, one, 0)
 
-    def supply_firsts_paced(when, w):
+    def firsts_done(when, w):
         @pl.when(when)
         def _():
             def one(i, carry):
-                supply_first(w, i, lambda copy: copy.start())
                 supply_first(w, i, lambda copy: copy.wait_send())
                 return carry
 
@@ -564,11 +563,44 @@
     feeds_zero_late = jnp.logical_and(role == 0, s == 0)
     feeds_one = jnp.logical_and(role == 0, s == 1)
     feeds_one_late = jnp.logical_and(role == 1, s == 1)
-    supply_firsts(feeds_zero_late, 0)
-    supply_firsts_paced(feeds_zero, 0)
+    supply_firsts(s == 0, 0)
+    mid_copies = mid_w.shape[1] // 128
+
+    def mid_copy(n, half):
+        return pltpu.make_async_copy(
+            mid_w.at[half * 512 : half * 512 + 512, n * 128 : n * 128 + 128], q_own.at[2 * n + half],
+            mid_sem.at[2 * n + half],
+        )
+
+    for n in range(mid_copies):
+        for half in range(2):
+            mid_copy(n, half).start()
+    for k, row in enumerate((g1, s1, bo, g2, s2, bd)):
+        vec_own[k : k + 1, :] = row[...].astype(jnp.float32)
+
+    @pl.when(role == s)
+    def _():
+        pltpu.make_async_copy(vec_own, vec.at[0], vec_sem.at[0]).start()
+
+    sends.start(vec_own, vec.at[0], vec_sem.at[0], (other, d, z), when=role == s)
+    tanh_out[...] = jnp.zeros(tanh_out.shape, jnp.float32)
+    for n in range(mid_copies):
+        for half in range(2):
+            mid_copy(n, half).wait()
+        cols = slice(n * 128, n * 128 + 128)
+        part_sum = dot_nn(table[:, 0:512], q_own[2 * n]) + dot_nn(table[:, 512:1024], q_own[2 * n + 1])
+        tanh_out[0:PREFIX, cols] = jnp.tanh(part_sum + mid_b[...].astype(jnp.float32).reshape(1, -1)[:, cols])
+    pre_full[...] = dot_nn(tanh_out[...].astype(jnp.bfloat16), pw[...]) + pb[...].astype(jnp.float32).reshape(1, -1)
+    half_width = pre_full.shape[1]
+    for k, row in enumerate((bu, bq)):
+        for n in range(2):
+            piece = row[:, n * half_width : min((n + 1) * half_width, row.shape[1])]
+            pre_full[PREFIX + 2 * k + n : PREFIX + 2 * k + n + 1, 0 : piece.shape[1]] = piece.astype(jnp.float32)
+    pre_own[...] = pre_full[...].astype(jnp.bfloat16)
+    send_small(feeds_zero)
+    firsts_done(feeds_zero, 0)
+    supply_firsts(feeds_zero, 1)
     send_x(feeds_zero)
-    send_small(feeds_zero)
-    supply_firsts_paced(feeds_zero, 1)
     owned = ((wq_hbm, wq.at[z]), (wo_hbm, wo.at[z]), (wu_hbm, wud.at[z, 0:1024]), (wd_hbm, wud.at[z, 1024:2048]))
     for w, (held, full) in enumerate(owned):
         @pl.when(role == s)
@@ -659,9 +691,9 @@
     def relay(n):
         for c in range(4):
 
-            @pl.when(jnp.logical_and(feeds_one, jnp.logical_and(n < UNITS, n % 4 == c)))
+            @pl.when(jnp.logical_and(feeds_one, jnp.logical_and(n < UNITS // 2, n % 2 == c // 2)))
             def _():
-                supply_copies(n // 4, c, lambda copy: copy.start())
+                supply_copies(n // 2, c, lambda copy: copy.start())
 
         for k in range(4):
             m = n - k
@@ -710,9 +742,14 @@
     arrived(wo.at[z], own_sem.at[1])
     arrived(wud.at[z, 0:1024], own_sem.at[2])
     arrived(wud.at[z, 1024:2048], own_sem.at[3])
+    arrived(vec.at[0], vec_sem.at[0])
     for q in range(4):
-        arrived(vec.at[q], vec_sem.at[q])
         arrived(pre.at[q], pre_sem.at[q])
+        carried = pre[q].astype(jnp.float32)
+        for k in range(2):
+            for n in range(2):
+                row = PREFIX + 2 * k + n
+                vec[q, 6 + k : 7 + k, n * half_width : (n + 1) * half_width] = carried[row : row + 1, :]
 
     first16 = lax.broadcasted_iota(jnp.int32, (16, 128), 1) < HEAD_DIM
     first = lax.broadcasted_iota(jnp.int32, (BLOCK, 128), 1) < HEAD_DIM
@@ -735,16 +772,18 @@
         row0 = block_of(s, j) * BLOCK
         row_at = row0 + lax.broadcasted_iota(jnp.int32, (BLOCK, 1), 0)
         begin = jnp.zeros((BLOCK, 1), jnp.int32)
-        for e in range(ends.shape[1]):
-            begin = jnp.where(row_at >= ends[micro, e], ends[micro, e], begin)
+        end = 0
+        for e in range(lengths.shape[1]):
+            end = end + lengths[micro, e]
+            begin = jnp.where(row_at >= end, end, begin)
 
         def mask_block(kb, carry):
             key_at = kb * BLOCK + lax.broadcasted_iota(jnp.int32, (BLOCK, BLOCK), 1)
             keep = jnp.logical_and(key_at <= row_at, key_at >= begin)
-            bias[j, kb] = jnp.where(keep, 0.0, NEG_LARGE)
+            bias[2 * j + kb] = jnp.where(keep, 0.0, NEG_LARGE)
             return carry
 
-        lax.fori_loop(0, 4, mask_block, 0)
+        lax.fori_loop(0, 2 + 2 * j, mask_block, 0)
 
     def vector(k, q=0, width=1024):
         return vec[q, k : k + 1, 0:width]
@@ -815,7 +854,7 @@
         for kb in range(blocks):
             keys = kv[core_of(kb), pair, 0, (kb // 2) * BLOCK : (kb // 2 + 1) * BLOCK, :]
             for h in range(2):
-                t = dot_nt(q_half[h], keys) * scale + bias[j, kb]
+                t = dot_nt(q_half[h], keys) * scale + bias[2 * j + kb]
                 ts[h, kb] = t
                 tops[h] = jnp.maximum(tops[h], jnp.maximum(t[:, :128], t[:, 128:]))
         highest = [jnp.max(tops[h], axis=1, keepdims=True) for h in range(2)]
@@ -895,11 +934,21 @@
         rows = block_rows(j)
         y_out[rows, :] = acc[rows, :].astype(jnp.bfloat16)
 
-        @pl.when(role == 0)
-        def _():
-            hand_copies(j, 0).start()
-
-        hand_copies(j, 1).start()
+        @pl.when(role == 1)
+        def _():
+            hand_copies(j, 1).start()
+
+        @pl.when(jnp.logical_and(role == 0, j == 0))
+        def _():
+            hand_copies(0, 0).start()
+
+        @pl.when(jnp.logical_and(role == 0, j == 1))
+        def _():
+            hand_copies(0, 0).wait_send()
+            hand_copies(1, 0).start()
+            hand_copies(1, 0).wait_send()
+            for block in range(2):
+                hand_copies(block, 1).start()
 
     def upto(n, table):
         total = jnp.int32(0)
@@ -911,8 +960,9 @@
     late_table = (AHEAD, 9, 10, 11, 13, 15, 15, 15, 15, 15, 15, 15, 15, 15)
 
     def forward(n, carry):
-        stage = jnp.where(role == 0, n // 2, n % 7)
-        j = jnp.where(role == 0, n % 2, n // 7)
+        turn = jnp.where(n == 11, 12, jnp.where(n == 12, 11, n))
+        stage = jnp.where(role == 0, turn // 2, n % 7)
+        j = jnp.where(role == 0, turn % 2, n // 7)
         before = jnp.where(
             role == 0,
             jnp.where(n == 0, 0, upto(n - 1, early_table)) + jnp.where(jnp.logical_or(n == 3, n == 4), 1, 0),
@@ -985,7 +1035,7 @@
                 dk = held[pair, 0, at, :].astype(jnp.float32)
                 dv = held[pair, 1, at, :].astype(jnp.float32)
             for h in range(2):
-                probs = jnp.exp2(dot_nt(q_half[h], keys) * scale + bias[j, kb] - log_half[h])
+                probs = jnp.exp2(dot_nt(q_half[h], keys) * scale + bias[2 * j + kb] - log_half[h])
                 grad_probs = dot_nt(g_half[h], values)
                 grad_scores = (probs * (grad_probs - row_term[h])).astype(jnp.bfloat16)
                 dv += dot_tn(probs.astype(jnp.bfloat16), g_half[h])
@@ -1006,6 +1056,25 @@
 
     contribution = micro * 2 + s
 
+    def pg_copy(q):
+        return pltpu.make_async_remote_copy(
+            src_ref=pg.at[2 * q : 2 * q + 2], dst_ref=pg_near.at[contribution], send_sem=pg_ssem.at[q],
+            recv_sem=pg_sem.at[contribution], device_id=(role, d, q), device_id_type=MESH,
+        )
+
+    def far_copy(k):
+        return pltpu.make_async_remote_copy(
+            src_ref=pg_far.at[d], dst_ref=pg_far.at[d], send_sem=far_ssem.at[k - 1], recv_sem=far_sem.at[d],
+            device_id=(s, (d + k) % 4, z), device_id_type=MESH,
+        )
+
+    def sum_near():
+        for k in range(4):
+            arrived(pg_near.at[k], pg_sem.at[k])
+        pg_far[d] = (pg_near[0] + pg_near[1]) + (pg_near[2] + pg_near[3])
+        for k in range(1, 4):
+            far_copy(k).start()
+
     def backward(n, carry):
         j = 1 - n
         rows = block_rows(j)
@@ -1037,6 +1106,21 @@
                         return carry
 
                     lax.fori_loop(0, 8, back_pair, 0)
+
+        @pl.when(j == 0)
+        def _():
+            for q in range(4):
+                is_here = jnp.logical_and(role == s, z == q)
+
+                @pl.when(is_here)
+                def _():
+                    pltpu.make_async_copy(
+                        pg.at[2 * q : 2 * q + 2], pg_near.at[contribution], pg_sem.at[contribution]
+                    ).start()
+
+                @pl.when(jnp.logical_not(is_here))
+                def _():
+                    pg_copy(q).start()
 
         acc[rows, :] = jnp.zeros((BLOCK, 1024), jnp.float32)
 
@@ -1056,9 +1140,9 @@
 
         lax.fori_loop(0, 4, project_back, 0)
 
-        @pl.when(role == 0)
-        def _():
-            hand_copies(j, 0).wait_send()
+        @pl.when(jnp.logical_and(j == 0, role == 0))
+        def _():
+            sum_near()
 
         hand_copies(j, 1).wait_send()
 
@@ -1068,25 +1152,29 @@
 
         over_rows(j, give_back)
 
-        @pl.when(role == 1)
-        def _():
-            hand_copies(j, 2).start()
-
-        hand_copies(j, 3).start()
+        @pl.when(role == 0)
+        def _():
+            hand_copies(j, 3).start()
+
+        @pl.when(jnp.logical_and(role == 1, j == 1))
+        def _():
+            hand_copies(1, 2).start()
+
+        @pl.when(jnp.logical_and(role == 1, j == 0))
+        def _():
+            hand_copies(0, 2).start()
+            hand_copies(1, 2).wait_send()
+            hand_copies(0, 2).wait_send()
+            for block in range(2):
+                hand_copies(block, 3).start()
+
         return carry
 
     lax.fori_loop(0, 2, backward, 0)
-    for q in range(4):
-        sends.start_or_keep(
-            pg.at[2 * q : 2 * q + 2], pg_near.at[contribution], pg_sem.at[contribution], (role, d, q),
-            jnp.logical_and(role == s, z == q),
-        )
-
-    for k in range(4):
-        arrived(pg_near.at[k], pg_sem.at[k])
-    pg_far[d] = (pg_near[0] + pg_near[1]) + (pg_near[2] + pg_near[3])
-    for k in range(1, 4):
-        sends.start(pg_far.at[d], pg_far.at[d], far_sem.at[d], (s, (d + k) % 4, z))
+    @pl.when(role == 1)
+    def _():
+        sum_near()
+
     for k in range(1, 4):
         arrived(pg_far.at[(d + k) % 4], far_sem.at[(d + k) % 4])
     total_pg = (pg_far[0] + pg_far[1]) + (pg_far[2] + pg_far[3])
@@ -1094,33 +1182,22 @@
         keys, values = total_pg[p, 0], total_pg[p, 1]
         sum_out[:, p * 256 : p * 256 + 128] = jnp.where(first16, keys, pltpu.roll(values, 64, 1))
         sum_out[:, p * 256 + 128 : p * 256 + 256] = jnp.where(first16, pltpu.roll(keys, 64, 1), values)
-    here = s * 4 + z
-    hidden_all[here] = dot_nt(sum_out[...].astype(jnp.bfloat16), pw[...])
-    for ds in range(2):
-        for dz in range(4):
-            if ds or dz:
-                sends.start(hidden_all.at[here], hidden_all.at[here], hidden_sem.at[here],
-                            ((s + ds) % 2, d, (z + dz) % 4))
-    for ds in range(2):
-        for dz in range(4):
-            if ds or dz:
-                there = ((s + ds) % 2) * 4 + (z + dz) % 4
-                arrived(hidden_all.at[there], hidden_sem.at[there])
-    hidden_sum = hidden_all[0]
-    for k in range(1, 8):
-        hidden_sum += hidden_all[k]
-    hidden_out[...] = hidden_sum
+    hidden_core[s] = dot_nt(sum_out[...].astype(jnp.bfloat16), pw[...])
+    sends.start(hidden_core.at[s], hidden_core.at[s], core_sem.at[s], (other, d, z))
+    arrived(hidden_core.at[other], core_sem.at[other])
+    hidden_all[z] = hidden_core[0] + hidden_core[1]
+    for k in range(1, 4):
+        sends.start(hidden_all.at[z], hidden_all.at[z], hidden_sem.at[z], (s, d, (z + k) % 4))
+    for k in range(1, 4):
+        arrived(hidden_all.at[(z + k) % 4], hidden_sem.at[(z + k) % 4])
+    hidden_out[...] = (hidden_all[0] + hidden_all[1]) + (hidden_all[2] + hidden_all[3])
 
     @pl.when(jnp.logical_not(feeds_zero))
     def _():
         lax.fori_loop(0, 3, supply_done, 0)
 
-        def firsts_done(i, carry):
-            for w in range(2):
-                supply_first(w, i, lambda copy: copy.wait_send())
-            return carry
-
-        lax.fori_loop(0, 3, firsts_done, 0)
+    firsts_done(jnp.logical_not(feeds_zero), 0)
+    firsts_done(True, 1)
 
     def relays_done(m, carry):
         for stage in range(3):
@@ -1129,11 +1206,15 @@
 
     lax.fori_loop(0, UNITS, relays_done, 0)
     cot_copies(lambda copy: copy.wait_send())
+    for k in range(1, 4):
+        far_copy(k).wait_send()
+    for q in range(4):
+
+        @pl.when(jnp.logical_not(jnp.logical_and(role == s, z == q)))
+        def _():
+            pg_copy(q).wait_send()
+
     for j in range(2):
-
-        @pl.when(role == 1)
-        def _():
-            hand_copies(j, 2).wait_send()
 
         hand_copies(j, 3).wait_send()
 
@@ -1143,20 +1224,21 @@
     sends.finish()
 
 
-def run_layers(x, cot, wq, wo, wu, wd, vec, pre, pw, ends):
+def run_layers(x, cot, wq, wo, wu, wd, *small):
     bf, f32 = jnp.bfloat16, jnp.float32
     vm, dma = pltpu.VMEM, pltpu.SemaphoreType.DMA
     rows = 2 * BLOCK
     width = x.shape[-1]
     pairs = width // 128
+    pw = small[-3]
     scratch = [
-        vm((4,) + wq.shape, bf), vm((4,) + wo.shape, bf), vm((4, 2 * wu.shape[0], width), bf),
-        vm((4,) + vec.shape, f32), vm((4,) + pre.shape, bf),
+        vm((8, width), f32), vm((16, pw.shape[1]), f32), vm((16, pw.shape[1]), bf), vm((4,) + wq.shape, bf), vm((4,) + wo.shape, bf), vm((4, 2 * wu.shape[0], width), bf),
+        vm((4, 8, width), f32), vm((4, 16, pw.shape[1]), bf),
         vm((rows, width), bf), vm((rows, width), bf), vm((rows, width), bf), vm((rows, width), bf),
         vm((2, pairs, 2, rows, 128), bf), vm((pairs, rows, 128), bf), vm((rows, width), bf),
-        vm((pairs, rows, 128), f32), vm((2, 4, BLOCK, BLOCK), f32), vm((rows, width), f32), vm((rows, width), f32),
+        vm((pairs, rows, 128), f32), vm((6, BLOCK, BLOCK), f32), vm((rows, width), f32), vm((rows, width), f32),
         vm((4, rows, wu.shape[1]), bf), vm((rows, wu.shape[1]), bf),
-        vm((pairs, 2, 16, 128), f32), vm((4, 2, 2, 16, 128), f32), vm((4, 2, 2, 16, 128), f32), vm((8, 16, pw.shape[0]), f32),
+        vm((pairs, 2, 16, 128), f32), vm((4, 2, 2, 16, 128), f32), vm((4, 2, 2, 16, 128), f32), vm((2, 16, pw.shape[0]), f32), vm((4, 16, pw.shape[0]), f32),
         vm((2, 4, BLOCK, BLOCK), f32),
         vm((pairs, 2, rows, 128), bf), vm((pairs, 2, rows, 128), bf), vm((pairs, 2, rows, 128), bf),
         vm((pairs, 128, 128), bf), vm((pairs, 128, 128), bf),
@@ -1165,24 +1247,57 @@
         dma((2, 4)), dma((2, 4)), dma((2, 4)), dma((2, 4)),
         dma((UNITS,)), dma((UNITS,)), dma((UNITS,)), dma((UNITS,)), dma((6, 2)), dma((UNITS, 2)), dma((UNITS,)), dma((UNITS,)), dma((UNITS,)),
         pltpu.SemaphoreType.REGULAR,
-        dma((2, 4)), dma((2, 4)), dma((2, pairs)), dma((2, pairs)), dma((4,)), dma((4,)), dma((8,)),
-        dma((4, 2)), dma((2,)),
+        dma((2, 4)), dma((2, 4)), dma((2, pairs)), dma((2, pairs)), dma((4,)), dma((4,)), dma((2,)), dma((4,)),
+        dma((4, 2)), dma((2,)), dma((4,)), dma((3,)), dma((8,)),
     ]
     anywhere = pl.BlockSpec(memory_space=pl.ANY)
+    local = pl.BlockSpec(memory_space=pltpu.VMEM)
     return pl.pallas_call(
         layer_kernel,
         out_shape=(
             jax.ShapeDtypeStruct(x.shape, bf), jax.ShapeDtypeStruct(x.shape, bf),
             jax.ShapeDtypeStruct((16, pw.shape[1]), f32), jax.ShapeDtypeStruct((16, pw.shape[0]), f32),
+            jax.ShapeDtypeStruct((16, pw.shape[0]), f32),
         ),
-        in_specs=[anywhere] * 8 + [pl.BlockSpec(memory_space=pltpu.VMEM), pl.BlockSpec(memory_space=pltpu.SMEM)],
-        out_specs=(anywhere, anywhere, pl.BlockSpec(memory_space=pltpu.VMEM), pl.BlockSpec(memory_space=pltpu.VMEM)),
+        in_specs=[anywhere] * 6 + [local] * 9 + [anywhere] + [local] * 3 + [pl.BlockSpec(memory_space=pltpu.SMEM)],
+        out_specs=(anywhere, anywhere, local, local, local),
         scratch_shapes=scratch,
         name="two_layers",
         compiler_params=pltpu.CompilerParams(
             collective_id=0, has_side_effects=True, vmem_limit_bytes=63 * 2**20
         ),
-    )(x, cot, wq, wo, wu, wd, vec, pre, pw, ends)
+    )(x, cot, wq, wo, wu, wd, *small)
+
+
+def prefix_kernel(
+    prefix_sum, hidden_grad, hidden_act, table, mid_w,
+    table_grad, mid_w_grad, mid_b_grad, prefix_w_grad, prefix_b_grad, table_full,
+):
+    prefix_low = prefix_sum[...].astype(jnp.bfloat16)
+    act = hidden_act[...]
+    prefix_b_grad[...] = jnp.sum(prefix_low.astype(jnp.float32), axis=0, keepdims=True)
+    prefix_w_grad[...] = dot_tn(act.astype(jnp.bfloat16), prefix_low)
+    pre_grad = (hidden_grad[...] * (1.0 - act * act)).astype(jnp.bfloat16)
+    mid_b_grad[...] = jnp.sum(pre_grad.astype(jnp.float32), axis=0, keepdims=True)
+    table_full[...] = jnp.zeros(table_full.shape, jnp.float32)
+    table_full[0:PREFIX, :] = table[...].astype(jnp.float32)
+    mid_w_grad[...] = dot_tn(table_full[...].astype(jnp.bfloat16), pre_grad)
+    table_grad[...] = dot_nt(pre_grad, mid_w[...])[0:PREFIX, :]
+
+
+def run_prefix_back(prefix_sum, hidden_grad, hidden_act, table, mid_w):
+    f32 = jnp.float32
+    hidden, own = mid_w.shape[1], prefix_sum.shape[1]
+    return pl.pallas_call(
+        prefix_kernel,
+        out_shape=tuple(
+            jax.ShapeDtypeStruct(shape, f32)
+            for shape in (table.shape, mid_w.shape, (1, hidden), (hidden, own), (1, own))
+        ),
+        scratch_shapes=[pltpu.VMEM((16, table.shape[1]), f32)],
+        name="prefix_network",
+        compiler_params=pltpu.CompilerParams(vmem_limit_bytes=48 * 2**20),
+    )(prefix_sum, hidden_grad, hidden_act, table, mid_w)
 
 
 def pair_body(
@@ -1190,28 +1305,18 @@
     attention_output_weight, out_bias, ffn_gain, ffn_shift, up_projection_weight, up_projection_bias,
     down_projection_weight, down_bias, prefix_table, mid_weight, mid_bias, prefix_weight, prefix_bias,
 ):
-    hidden_pre = jnp.dot(
-        prefix_table, mid_weight, preferred_element_type=jnp.float32
-    ) + mid_bias.astype(jnp.float32)
-    hidden_act = jnp.tanh(hidden_pre)
-    hidden_low = hidden_act.astype(jnp.bfloat16)
-    prefix_kv = (
-        jnp.dot(hidden_low, prefix_weight, preferred_element_type=jnp.float32)
-        + prefix_bias.astype(jnp.float32)
-    ).astype(jnp.bfloat16)
-    pre = jnp.pad(prefix_kv, ((0, 6), (0, 0)))
-    pieces = [attn_gain, attn_shift, out_bias, ffn_gain, ffn_shift, down_bias, up_projection_bias, qkv_bias]
-    width = layer_input.shape[-1]
-    vec = jnp.concatenate(
-        [jnp.pad(p.astype(jnp.float32), ((0, 0), (0, width - p.shape[1]))) for p in pieces], axis=0
-    )
-    ends = jnp.cumsum(example_lengths[:, 0], axis=-1).astype(jnp.int32)
-    activations, input_grads, prefix_sum, hidden_grad = run_layers(
+    activations, input_grads, prefix_sum, hidden_grad, hidden_act = run_layers(
         layer_input[:, 0], cotangent[:, 0], query_key_value_weight[0], attention_output_weight[0],
-        up_projection_weight[0], down_projection_weight[0], vec, pre, prefix_weight, ends,
-    )
-    return (activations[None, :, None], input_grads[None, :, None]) + prefix_back(
-        prefix_sum[:PREFIX], hidden_grad[:PREFIX], hidden_act, hidden_low, prefix_table, mid_weight
+        up_projection_weight[0], down_projection_weight[0],
+        attn_gain, attn_shift, out_bias, ffn_gain, ffn_shift, down_bias, up_projection_bias, qkv_bias,
+        prefix_table, mid_weight, mid_bias, prefix_weight, prefix_bias, example_lengths[:, 0],
+    )
+    table_grad, mid_weight_grad, mid_bias_grad, prefix_weight_grad, prefix_bias_grad = run_prefix_back(
+        prefix_sum, hidden_grad, hidden_act, prefix_table, mid_weight
+    )
+    return (
+        activations[None, :, None], input_grads[None, :, None],
+        table_grad, mid_weight_grad, mid_bias_grad[0], prefix_weight_grad, prefix_bias_grad[0],
     )
 
 

time: 362 us -> 320 us (0.88)
  Pallas kernels: 344 us -> 312 us
  matrix products: 5.45 us -> 0 us
  other arithmetic: 4.77 us -> 0 us
    pallas_call x1, Pallas kernels: 344 us -> 310 us  [run_layers(): pl.pallas_call(layer_kernel, out_shape=(jax.ShapeDtypeStruct(x.shape, bf)...]
    dot_general x5 -> x0, matrix products: 5.45 us -> none  [the longest x1 1.48 us: pair_body(): jnp.dot(prefix_table, mid_weight, preferred_element_type=jnp.float32)]
where the time goes in v5:
time: 320 us
  Pallas kernels  312 us (98%)
  local copies, waits for them, and re-layouts  6.73 us (2%)
    pallas_call x1, Pallas kernels, run_layers(): pl.pallas_call(layer_kernel, out_shape=(jax.ShapeDtypeStruct(x.shape, bf)...  310 us
    unnamed x14, local copies, waits for them, and re-layouts  6.73 us

profile of v5, /device:TPU:0, one launch (start us, length us, event | category | flops | bytes accessed | tf_op | source)
XLA Modules:
  0.0 319.5 jit_solution(5682195925739108242)
XLA Ops:
  0.6 0.0 copy-start.1
  0.7 310.1 %two_layers.1 = (bf16[2,256,1024]{2,1,0:T(8,128)(2,1)}, bf16[2,256,1024]{2,1,0:T(8,128)(2,1)}, f32[16,512]{1,0:T(8,128)}, f32[16,512]{1,0:T(8,128)}, f32[16,512]{1,0:T(8,128)}) custom-call(bf16[2,256,1024]{2,1,0:T(8,128)(2,1)} %bitcast.20, bf16[2,256,1024]{2,1,0:T(8,128)(2,1)} %bitcast.21, bf16[1024,768]{1,0:T(8,128)(2,1)} %bitcast.17, ...), custom_call_target="tpu_custom_call" | custom-call | tf_op jit(solution)/shard_map/two_layers/pallas_call | solution.py:1255
  310.8 0.0 copy-done.1
  310.8 0.0 copy-start
  310.8 1.2 copy-done
  312.0 0.0 copy-start.2
  312.0 0.8 copy-done.2
  312.8 0.0 copy-start.3
  312.8 0.8 copy-done.3
  313.6 0.0 copy-start.4
  313.6 0.8 copy-done.4
  314.3 0.0 copy-start.5
  314.3 2.0 prefix_network.1
  316.3 2.3 copy.31
  318.6 0.0 copy-done.5
  318.6 1.0 copy.32
Async XLA Ops:
  0.6 310.2 %copy-start.1 = (bf16[10,1024]{1,0:T(8,128)(2,1)S(1)}, bf16[10,1024]{1,0:T(8,128)(2,1)}, u32[]{:S(2)}) copy-start(bf16[10,1024]{1,0:T(8,128)(2,1)} %table.3) | copy-start | bytes 61444
  310.8 1.2 copy-start
  312.0 0.8 copy-start.2
  312.8 0.8 copy-start.3
  313.6 0.8 copy-start.4
  314.3 4.3 %copy-start.5 = (bf16[2,256,1024]{2,1,0:T(8,128)(2,1)S(1)}, bf16[2,256,1024]{2,1,0:T(8,128)(2,1)}, u32[]{:S(2)}) copy-start(bf16[2,256,1024]{2,1,0:T(8,128)(2,1)} %get-tuple-element.18) | copy-start | bytes 3145732

commit v6 on v5

--- a/solution.py
+++ b/solution.py
@@ -353,7 +353,7 @@
 LOG2E = 1.4426950408889634
 CHUNK = 128
 UNITS = 12
-AHEAD = 8
+AHEAD = 10
 UNIT_ROWS = 512
 PART_ROWS = UNIT_ROWS // 8
 
@@ -425,7 +425,7 @@
     ssem, vec_sem, pre_sem, x_sem, g_sem, act_sem, ig_sem, own_sem, z_sem, a_sem, b_sem, c_sem,
     zr_sem, ar_sem, br_sem, cr_sem, fs_sem, zs_sem, as_sem, bs_sem, cs_sem, go_sem,
     kv_ssem, kv_rsem, dkv_ssem, dkv_rsem, pg_sem, far_sem, core_sem, hidden_sem,
-    hand_sem, cot_sem, pg_ssem, far_ssem, mid_sem,
+    hand_sem, cot_sem, x_ssem, pg_ssem, far_ssem, mid_sem,
 ):
     s, d, z = lax.axis_index("section"), lax.axis_index("dp"), lax.axis_index("mp")
     role, micro = role_of(z), z // 2
@@ -456,25 +456,37 @@
     mine = s == core_of(z)
     row_slot = pl.ds(pl.multiple_of((z // 2) * BLOCK, BLOCK), BLOCK)
 
-    def send_block(source, landing, sem, k, chip, when):
-        when = jnp.logical_and(mine, when)
-
-        @pl.when(jnp.logical_and(when, z == chip))
-        def _():
-            pltpu.make_async_copy(source.at[k], landing.at[row_slot], sem.at[z // 2]).start()
-
-        sends.start(source.at[k], landing.at[row_slot], sem.at[z // 2], (s, d, chip),
-                    when=jnp.logical_and(when, z != chip))
-
     def send_small(when):
         for t in planes:
             for h in range(2):
                 is_here = jnp.logical_and(z == t, s == h)
                 sends.start_or_keep(pre_own, pre.at[z], pre_sem.at[z], (h, d, t), is_here, when)
 
-    def send_x(when):
-        for k, chip in ((0, 1), (1, 2)):
-            send_block(x_hbm, x_in, x_sem, k, chip, when)
+    def row_copies(source, landing, send_sem, sem, chips, then):
+        for k, chip in enumerate(chips):
+
+            @pl.when(jnp.logical_and(mine, z != chip))
+            def _():
+                then(pltpu.make_async_remote_copy(
+                    src_ref=source.at[k], dst_ref=landing.at[row_slot], send_sem=send_sem.at[k],
+                    recv_sem=sem.at[z // 2], device_id=(s, d, chip), device_id_type=MESH,
+                ))
+
+    def keep_rows(source, landing, sem, chips):
+        for k, chip in enumerate(chips):
+
+            @pl.when(jnp.logical_and(mine, z == chip))
+            def _():
+                pltpu.make_async_copy(source.at[k], landing.at[row_slot], sem.at[z // 2]).start()
+
+    def x_copies(then):
+        row_copies(x_hbm, x_in, x_ssem, x_sem, (1, 2), then)
+
+    def cot_copies(then):
+        row_copies(cot_hbm, g_in, cot_sem, g_sem, (0, 3), then)
+
+    keep_rows(x_hbm, x_in, x_sem, (1, 2))
+    keep_rows(cot_hbm, g_in, g_sem, (0, 3))
 
     toward = jnp.where(z < 2, 1, -1)
 
@@ -551,19 +563,18 @@
             supply_copies(i, c, lambda copy: copy.wait_send())
         return carry
 
-    def supply_paced(i, carry):
-        for c in range(4):
-            supply_copies(i, c, lambda copy: copy.start())
-            if c:
-                supply_copies(i, c - 1, lambda copy: copy.wait_send())
-        supply_copies(i, 3, lambda copy: copy.wait_send())
-        return carry
-
     feeds_zero = jnp.logical_and(role == 1, s == 0)
     feeds_zero_late = jnp.logical_and(role == 0, s == 0)
     feeds_one = jnp.logical_and(role == 0, s == 1)
     feeds_one_late = jnp.logical_and(role == 1, s == 1)
     supply_firsts(s == 0, 0)
+
+    @pl.when(feeds_one)
+    def _():
+        for w in range(2):
+            supply_first(w, 0, lambda copy: copy.start())
+        supply_all(0, 0)
+
     mid_copies = mid_w.shape[1] // 128
 
     def mid_copy(n, half):
@@ -600,7 +611,10 @@
     send_small(feeds_zero)
     firsts_done(feeds_zero, 0)
     supply_firsts(feeds_zero, 1)
-    send_x(feeds_zero)
+
+    @pl.when(feeds_zero)
+    def _():
+        x_copies(lambda copy: copy.start())
     owned = ((wq_hbm, wq.at[z]), (wo_hbm, wo.at[z]), (wu_hbm, wud.at[z, 0:1024]), (wd_hbm, wud.at[z, 1024:2048]))
     for w, (held, full) in enumerate(owned):
         @pl.when(role == s)
@@ -611,7 +625,8 @@
 
     @pl.when(feeds_zero)
     def _():
-        lax.fori_loop(0, 3, supply_paced, 0)
+        x_copies(lambda copy: copy.wait_send())
+        lax.fori_loop(0, 3, supply_all, 0)
 
     @pl.when(feeds_one_late)
     def _():
@@ -652,7 +667,10 @@
     for step in range(len(first_units) + 3):
         relay_first(step)
         if step == 0:
-            send_x(role == 0)
+            @pl.when(role == 0)
+            def _():
+                x_copies(lambda copy: copy.start())
+
             send_small(feeds_zero_late)
             supply_firsts(feeds_zero_late, 1)
         if step == 3:
@@ -660,10 +678,14 @@
             def _():
                 pl.semaphore_signal(go_sem, inc=1, device_id=(1, d, partner), device_id_type=MESH)
 
-            supply_firsts(feeds_one, 0)
+                supply_first(0, 1, lambda copy: copy.start())
+
+            send_small(feeds_one)
         if step == 6:
-            send_small(feeds_one)
-            supply_firsts(feeds_one, 1)
+            @pl.when(feeds_one)
+            def _():
+                supply_first(1, 1, lambda copy: copy.start())
+
 
         @pl.when(feeds_zero_late)
         def _():
@@ -691,12 +713,12 @@
     def relay(n):
         for c in range(4):
 
-            @pl.when(jnp.logical_and(feeds_one, jnp.logical_and(n < UNITS // 2, n % 2 == c // 2)))
+            @pl.when(jnp.logical_and(feeds_one, n == c))
             def _():
-                supply_copies(n // 2, c, lambda copy: copy.start())
-
-        for k in range(4):
-            m = n - k
+                supply_copies(1, c, lambda copy: copy.start())
+
+        for k, lag in enumerate((0, 1, 3, 4)):
+            m = n - lag
 
             @pl.when(jnp.logical_and(m >= 0, m < UNITS))
             def _():
@@ -710,22 +732,6 @@
                     arrived(unit_piece(m, 0, 4, other), cr_sem.at[m])
                 if k < 3:
                     relay_copy(m, k).start()
-
-    def cot_copies(then):
-        for k, chip in ((0, 0), (1, 3)):
-
-            @pl.when(jnp.logical_and(mine, z != chip))
-            def _():
-                then(pltpu.make_async_remote_copy(
-                    src_ref=cot_hbm.at[k], dst_ref=g_in.at[row_slot], send_sem=cot_sem.at[k],
-                    recv_sem=g_sem.at[z // 2], device_id=(s, d, chip), device_id_type=MESH,
-                ))
-
-    for k, chip in ((0, 0), (1, 3)):
-
-        @pl.when(jnp.logical_and(mine, z == chip))
-        def _():
-            pltpu.make_async_copy(cot_hbm.at[k], g_in.at[row_slot], g_sem.at[z // 2]).start()
 
     @pl.when(role == 1)
     def _():
@@ -756,6 +762,9 @@
     lane = lax.broadcasted_iota(jnp.int32, (1, 128), 1)
     half0 = jnp.where(lane < HEAD_DIM, 1.0, 0.0).astype(jnp.bfloat16)
     half1 = jnp.where(lane < HEAD_DIM, 0.0, 1.0).astype(jnp.bfloat16)
+    upper = lax.broadcasted_iota(jnp.int32, (128, BLOCK), 0) < HEAD_DIM
+    slot = lax.broadcasted_iota(jnp.int32, (128, 1), 0)
+    pre_mask_down = jnp.where(slot % HEAD_DIM < PREFIX, 0.0, NEG_LARGE)
     pre_mask = jnp.where(lane % HEAD_DIM < PREFIX, 0.0, NEG_LARGE)
     kp[...] = jnp.zeros(kp.shape, kp.dtype)
     vp[...] = jnp.zeros(vp.shape, vp.dtype)
@@ -768,22 +777,25 @@
             vp[2 * q + p, 0:16, :] = jnp.where(first16, pltpu.roll(t0, 64, 1), 0.0).astype(jnp.bfloat16)
             vp[2 * q + p, 64:80, :] = jnp.where(first16, 0.0, t1).astype(jnp.bfloat16)
 
-    for j in range(2):
-        row0 = block_of(s, j) * BLOCK
-        row_at = row0 + lax.broadcasted_iota(jnp.int32, (BLOCK, 1), 0)
-        begin = jnp.zeros((BLOCK, 1), jnp.int32)
-        end = 0
-        for e in range(lengths.shape[1]):
-            end = end + lengths[micro, e]
-            begin = jnp.where(row_at >= end, end, begin)
-
-        def mask_block(kb, carry):
-            key_at = kb * BLOCK + lax.broadcasted_iota(jnp.int32, (BLOCK, BLOCK), 1)
-            keep = jnp.logical_and(key_at <= row_at, key_at >= begin)
-            bias[2 * j + kb] = jnp.where(keep, 0.0, NEG_LARGE)
-            return carry
-
-        lax.fori_loop(0, 2 + 2 * j, mask_block, 0)
+    def mask_blocks(keys_down):
+        for j in range(2):
+            row0 = block_of(s, j) * BLOCK
+            row_at = row0 + lax.broadcasted_iota(jnp.int32, (1, BLOCK) if keys_down else (BLOCK, 1), int(keys_down))
+            begin = jnp.zeros(row_at.shape, jnp.int32)
+            end = 0
+            for e in range(lengths.shape[1]):
+                end = end + lengths[micro, e]
+                begin = jnp.where(row_at >= end, end, begin)
+
+            def mask_block(kb, carry):
+                key_at = kb * BLOCK + lax.broadcasted_iota(jnp.int32, (BLOCK, BLOCK), 1 - int(keys_down))
+                keep = jnp.logical_and(key_at <= row_at, key_at >= begin)
+                bias[2 * j + kb] = jnp.where(keep, 0.0, NEG_LARGE)
+                return carry
+
+            lax.fori_loop(0, 2 + 2 * j, mask_block, 0)
+
+    mask_blocks(False)
 
     def vector(k, q=0, width=1024):
         return vec[q, k : k + 1, 0:width]
@@ -888,7 +900,7 @@
                 @pl.when(jnp.logical_and(s == core, j == block))
                 def _():
                     def attend_pair(pair, carry):
-                        relay_steps(relay_at, jnp.where(jnp.logical_and(pair == 4, role == 0), relay_at + 1, relay_at))
+                        relay_steps(relay_at, jnp.where(jnp.logical_and(pair == 4, relay_at < UNITS + 4), relay_at + 1, relay_at))
                         attend_rows(pair, core, block)
                         return carry
 
@@ -956,8 +968,8 @@
             total += jnp.where(n >= k, entry - (table[k - 1] if k else 0), 0)
         return total
 
-    early_table = (0, 1, 2, 4, 6, 7, 8, 9, 11, 13, 15, 15, 15, 15)
-    late_table = (AHEAD, 9, 10, 11, 13, 15, 15, 15, 15, 15, 15, 15, 15, 15)
+    early_table = (0, 1, 2, 4, 6, 7, 8, 10, 12, 14, 16, 16, 16, 16)
+    late_table = (AHEAD, 11, 13, 14, 15, 16, 16, 16, 16, 16, 16, 16, 16, 16)
 
     def forward(n, carry):
         turn = jnp.where(n == 11, 12, jnp.where(n == 12, 11, n))
@@ -966,7 +978,7 @@
         before = jnp.where(
             role == 0,
             jnp.where(n == 0, 0, upto(n - 1, early_table)) + jnp.where(jnp.logical_or(n == 3, n == 4), 1, 0),
-            jnp.where(n == 0, AHEAD, upto(n - 1, late_table)),
+            jnp.where(n == 0, AHEAD, upto(n - 1, late_table)) + jnp.where(n == 2, 1, 0),
         )
         until = jnp.where(role == 0, upto(n, early_table), upto(n, late_table))
         relay_steps(before, until)
@@ -1007,19 +1019,21 @@
             jnp.sum(jnp.where(first, product, 0.0), axis=1, keepdims=True),
             jnp.sum(jnp.where(first, 0.0, product), axis=1, keepdims=True),
         ]
-        logs = lse[pair, rows, :]
-        log_half = (logs[:, 0:1], logs[:, 64:65])
-        p_pre = jnp.exp2(dot_nt(q_pair, kp[pair]) * scale + pre_mask - logs)
-        dp_pre = dot_nt(g_pair, vp[pair])
-        ds_pre = (p_pre * (dp_pre - jnp.where(first, row_term[0], row_term[1]))).astype(jnp.bfloat16)
-        pv = dot_tn(p_pre.astype(jnp.bfloat16), g_pair)
-        pk = dot_tn(ds_pre, q_pair)
+        logs = jnp.transpose(lse[pair, rows, :])
+        terms = jnp.transpose(jnp.where(first, row_term[0], row_term[1]))
+        log_half = (logs[0:1, :], logs[64:65, :])
+        term_half = (terms[0:1, :], terms[64:65, :])
+        p_pre = jnp.exp2(dot_nt(kp[pair], q_pair) * scale + pre_mask_down - logs)
+        dp_pre = dot_nt(vp[pair], g_pair)
+        ds_pre = (p_pre * (dp_pre - terms)).astype(jnp.bfloat16)
+        pv = dot_nn(p_pre.astype(jnp.bfloat16), g_pair)
+        pk = dot_nn(ds_pre, q_pair)
         pk = jnp.where(first16, pk[0:16, :], pk[64:80, :]) * HEAD_DIM ** (-0.5)
         pv = jnp.where(first16, pv[0:16, :], pv[64:80, :])
         pg[pair, 0] = pk if j else pg[pair, 0] + pk
         pg[pair, 1] = pv if j else pg[pair, 1] + pv
-        dq_pre = dot_nn(ds_pre, kp[pair])
-        dqs = [jnp.zeros((BLOCK, 128), jnp.float32) for _ in range(2)]
+        dq_pre = dot_tn(kp[pair], ds_pre)
+        dqs = [jnp.zeros((128, BLOCK), jnp.float32) for _ in range(2)]
         for kb in range(4):
             held = dkv_own if core_of(kb) == core else dkv_send
             at = slice((kb // 2) * BLOCK, (kb // 2 + 1) * BLOCK)
@@ -1035,16 +1049,16 @@
                 dk = held[pair, 0, at, :].astype(jnp.float32)
                 dv = held[pair, 1, at, :].astype(jnp.float32)
             for h in range(2):
-                probs = jnp.exp2(dot_nt(q_half[h], keys) * scale + bias[2 * j + kb] - log_half[h])
-                grad_probs = dot_nt(g_half[h], values)
-                grad_scores = (probs * (grad_probs - row_term[h])).astype(jnp.bfloat16)
-                dv += dot_tn(probs.astype(jnp.bfloat16), g_half[h])
-                dk += dot_tn(grad_scores, q_half[h])
-                dqs[h] += dot_nn(grad_scores, keys)
+                probs = jnp.exp2(dot_nt(keys, q_half[h]) * scale + bias[2 * j + kb] - log_half[h])
+                grad_probs = dot_nt(values, g_half[h])
+                grad_scores = (probs * (grad_probs - term_half[h])).astype(jnp.bfloat16)
+                dv += dot_nn(probs.astype(jnp.bfloat16), g_half[h])
+                dk += dot_nn(grad_scores, q_half[h])
+                dqs[h] += dot_tn(keys, grad_scores)
             held[pair, 0, at, :] = dk.astype(jnp.bfloat16)
             held[pair, 1, at, :] = dv.astype(jnp.bfloat16)
-        dq = (jnp.where(first, dqs[0], dqs[1]) + dq_pre) * HEAD_DIM ** (-0.5)
-        q_own[pair, rows, :] = dq.astype(jnp.bfloat16)
+        dq = (jnp.where(upper, dqs[0], dqs[1]) + dq_pre) * HEAD_DIM ** (-0.5)
+        q_own[pair, rows, :] = jnp.transpose(dq).astype(jnp.bfloat16)
 
     def dkv_copy(j, pair):
         rows = block_rows(j)
@@ -1170,6 +1184,7 @@
 
         return carry
 
+    mask_blocks(True)
     lax.fori_loop(0, 2, backward, 0)
     @pl.when(role == 1)
     def _():
@@ -1192,9 +1207,15 @@
         arrived(hidden_all.at[(z + k) % 4], hidden_sem.at[(z + k) % 4])
     hidden_out[...] = (hidden_all[0] + hidden_all[1]) + (hidden_all[2] + hidden_all[3])
 
-    @pl.when(jnp.logical_not(feeds_zero))
+    lax.fori_loop(0, 3, supply_done, 0)
+
+    @pl.when(role == 0)
     def _():
-        lax.fori_loop(0, 3, supply_done, 0)
+        x_copies(lambda copy: copy.wait_send())
+
+    @pl.when(feeds_one_late)
+    def _():
+        x_copies(lambda copy: copy.wait_send())
 
     firsts_done(jnp.logical_not(feeds_zero), 0)
     firsts_done(True, 1)
@@ -1248,7 +1269,7 @@
         dma((UNITS,)), dma((UNITS,)), dma((UNITS,)), dma((UNITS,)), dma((6, 2)), dma((UNITS, 2)), dma((UNITS,)), dma((UNITS,)), dma((UNITS,)),
         pltpu.SemaphoreType.REGULAR,
         dma((2, 4)), dma((2, 4)), dma((2, pairs)), dma((2, pairs)), dma((4,)), dma((4,)), dma((2,)), dma((4,)),
-        dma((4, 2)), dma((2,)), dma((4,)), dma((3,)), dma((8,)),
+        dma((4, 2)), dma((2,)), dma((2,)), dma((4,)), dma((3,)), dma((8,)),
     ]
     anywhere = pl.BlockSpec(memory_space=pl.ANY)
     local = pl.BlockSpec(memory_space=pltpu.VMEM)

time: 320 us -> 293 us (0.916)
  Pallas kernels: 312 us -> 285 us
    pallas_call x1, Pallas kernels: 310 us -> 283 us  [run_layers(): pl.pallas_call(layer_kernel, out_shape=(jax.ShapeDtypeStruct(x.shape, bf)...]
where the time goes in v6:
time: 293 us
  Pallas kernels  285 us (97%)
  local copies, waits for them, and re-layouts  6.73 us (2%)
    pallas_call x1, Pallas kernels, run_layers(): pl.pallas_call(layer_kernel, out_shape=(jax.ShapeDtypeStruct(x.shape, bf)...  283 us
    unnamed x14, local copies, waits for them, and re-layouts  6.73 us

profile of v6, /device:TPU:0, one launch (start us, length us, event | category | flops | bytes accessed | tf_op | source)
XLA Modules:
  0.0 292.7 jit_solution(10948444423957548319)
XLA Ops:
  0.6 0.0 copy-start.1
  0.7 283.2 %two_layers.1 = (bf16[2,256,1024]{2,1,0:T(8,128)(2,1)}, bf16[2,256,1024]{2,1,0:T(8,128)(2,1)}, f32[16,512]{1,0:T(8,128)}, f32[16,512]{1,0:T(8,128)}, f32[16,512]{1,0:T(8,128)}) custom-call(bf16[2,256,1024]{2,1,0:T(8,128)(2,1)} %bitcast.20, bf16[2,256,1024]{2,1,0:T(8,128)(2,1)} %bitcast.21, bf16[1024,768]{1,0:T(8,128)(2,1)} %bitcast.17, ...), custom_call_target="tpu_custom_call" | custom-call | tf_op jit(solution)/shard_map/two_layers/pallas_call | solution.py:1276
  283.9 0.0 copy-done.1
  283.9 0.0 copy-start
  283.9 1.2 copy-done
  285.1 0.0 copy-start.2
  285.1 0.8 copy-done.2
  285.9 0.0 copy-start.3
  285.9 0.8 copy-done.3
  286.7 0.0 copy-start.4
  286.7 0.8 copy-done.4
  287.4 0.0 copy-start.5
  287.4 2.0 prefix_network.1
  289.4 2.3 copy.31
  291.7 0.0 copy-done.5
  291.7 1.0 copy.32
Async XLA Ops:
  0.6 283.3 %copy-start.1 = (bf16[10,1024]{1,0:T(8,128)(2,1)S(1)}, bf16[10,1024]{1,0:T(8,128)(2,1)}, u32[]{:S(2)}) copy-start(bf16[10,1024]{1,0:T(8,128)(2,1)} %table.3) | copy-start | bytes 61444
  283.9 1.2 copy-start
  285.1 0.8 copy-start.2
  285.9 0.8 copy-start.3
  286.7 0.8 copy-start.4
  287.4 4.3 %copy-start.5 = (bf16[2,256,1024]{2,1,0:T(8,128)(2,1)S(1)}, bf16[2,256,1024]{2,1,0:T(8,128)(2,1)}, u32[]{:S(2)}) copy-start(bf16[2,256,1024]{2,1,0:T(8,128)(2,1)} %get-tuple-element.18) | copy-start | bytes 3145732

commit v7 on v6

--- a/solution.py
+++ b/solution.py
@@ -1291,9 +1291,18 @@
 
 
 def prefix_kernel(
-    prefix_sum, hidden_grad, hidden_act, table, mid_w,
-    table_grad, mid_w_grad, mid_b_grad, prefix_w_grad, prefix_b_grad, table_full,
+    prefix_sum, hidden_grad, hidden_act, table, mid_w, act_held, ig_held,
+    table_grad, mid_w_grad, mid_b_grad, prefix_w_grad, prefix_b_grad, act_out, ig_out, table_full, stage, in_sem, out_sem,
 ):
+    incoming, outgoing = [], []
+    for n, (held, out) in enumerate(((act_held, act_out), (ig_held, ig_out))):
+        for k in range(2):
+            incoming.append(pltpu.make_async_copy(held.at[k], stage.at[n, k], in_sem.at[n, k]))
+            outgoing.append(pltpu.make_async_copy(stage.at[n, k], out.at[k], out_sem.at[n, k]))
+            incoming[-1].start()
+    for arriving, leaving in zip(incoming, outgoing):
+        arriving.wait()
+        leaving.start()
     prefix_low = prefix_sum[...].astype(jnp.bfloat16)
     act = hidden_act[...]
     prefix_b_grad[...] = jnp.sum(prefix_low.astype(jnp.float32), axis=0, keepdims=True)
@@ -1304,21 +1313,30 @@
     table_full[0:PREFIX, :] = table[...].astype(jnp.float32)
     mid_w_grad[...] = dot_tn(table_full[...].astype(jnp.bfloat16), pre_grad)
     table_grad[...] = dot_nt(pre_grad, mid_w[...])[0:PREFIX, :]
-
-
-def run_prefix_back(prefix_sum, hidden_grad, hidden_act, table, mid_w):
+    for leaving in outgoing:
+        leaving.wait()
+
+
+def run_prefix_back(prefix_sum, hidden_grad, hidden_act, table, mid_w, activations, input_grads):
     f32 = jnp.float32
     hidden, own = mid_w.shape[1], prefix_sum.shape[1]
+    local, anywhere = pl.BlockSpec(memory_space=pltpu.VMEM), pl.BlockSpec(memory_space=pl.ANY)
+    rows = jax.ShapeDtypeStruct(activations.shape, activations.dtype)
     return pl.pallas_call(
         prefix_kernel,
         out_shape=tuple(
             jax.ShapeDtypeStruct(shape, f32)
             for shape in (table.shape, mid_w.shape, (1, hidden), (hidden, own), (1, own))
-        ),
-        scratch_shapes=[pltpu.VMEM((16, table.shape[1]), f32)],
+        ) + (rows, rows),
+        in_specs=[local] * 5 + [anywhere] * 2,
+        out_specs=(local,) * 5 + (anywhere,) * 2,
+        scratch_shapes=[
+            pltpu.VMEM((16, table.shape[1]), f32), pltpu.VMEM((2,) + activations.shape, activations.dtype),
+            pltpu.SemaphoreType.DMA((2, 2)), pltpu.SemaphoreType.DMA((2, 2)),
+        ],
         name="prefix_network",
-        compiler_params=pltpu.CompilerParams(vmem_limit_bytes=48 * 2**20),
-    )(prefix_sum, hidden_grad, hidden_act, table, mid_w)
+        compiler_params=pltpu.CompilerParams(vmem_limit_bytes=60 * 2**20),
+    )(prefix_sum, hidden_grad, hidden_act, table, mid_w, activations, input_grads)
 
 
 def pair_body(
@@ -1332,9 +1350,9 @@
         attn_gain, attn_shift, out_bias, ffn_gain, ffn_shift, down_bias, up_projection_bias, qkv_bias,
         prefix_table, mid_weight, mid_bias, prefix_weight, prefix_bias, example_lengths[:, 0],
     )
-    table_grad, mid_weight_grad, mid_bias_grad, prefix_weight_grad, prefix_bias_grad = run_prefix_back(
-        prefix_sum, hidden_grad, hidden_act, prefix_table, mid_weight
-    )
+    (
+        table_grad, mid_weight_grad, mid_bias_grad, prefix_weight_grad, prefix_bias_grad, activations, input_grads,
+    ) = run_prefix_back(prefix_sum, hidden_grad, hidden_act, prefix_table, mid_weight, activations, input_grads)
     return (
         activations[None, :, None], input_grads[None, :, None],
         table_grad, mid_weight_grad, mid_bias_grad[0], prefix_weight_grad, prefix_bias_grad[0],

time: 293 us -> 290 us (0.990)
  local copies, waits for them, and re-layouts: 6.73 us -> 0 us
  Pallas kernels: 285 us -> 289 us
    unnamed x14 -> x0, local copies, waits for them, and re-layouts: 6.73 us -> none
    pallas_call x1, Pallas kernels: 2 us -> 5.4 us  [run_prefix_back(): pl.pallas_call(prefix_kernel, out_shape=tuple((jax.ShapeDtypeStruct(shape...]
where the time goes in v7:
time: 290 us; the launch traced here: 289 us
  Pallas kernels  289 us (100%)
    pallas_call x1, Pallas kernels, run_layers(): pl.pallas_call(layer_kernel, out_shape=(jax.ShapeDtypeStruct(x.shape, bf)...  283 us

profile of v7, /device:TPU:0, one launch (start us, length us, event | category | flops | bytes accessed | tf_op | source)
XLA Modules:
  0.0 289.5 jit_solution(17521662478338514161)
XLA Ops:
  0.6 283.2 %two_layers.1 = (bf16[2,256,1024]{2,1,0:T(8,128)(2,1)}, bf16[2,256,1024]{2,1,0:T(8,128)(2,1)}, f32[16,512]{1,0:T(8,128)}, f32[16,512]{1,0:T(8,128)}, f32[16,512]{1,0:T(8,128)}) custom-call(bf16[2,256,1024]{2,1,0:T(8,128)(2,1)} %bitcast.18, bf16[2,256,1024]{2,1,0:T(8,128)(2,1)} %bitcast.19, bf16[1024,768]{1,0:T(8,128)(2,1)} %bitcast.17, ...), custom_call_target="tpu_custom_call" | custom-call | tf_op jit(solution)/shard_map/two_layers/pallas_call | solution.py:1276
  283.9 5.4 %prefix_network.1 = (f32[10,1024]{1,0:T(8,128)}, f32[1024,512]{1,0:T(8,128)}, f32[1,512]{1,0:T(1,128)}, f32[512,512]{1,0:T(8,128)}, f32[1,512]{1,0:T(1,128)}, /*...) custom-call(f32[16,512]{1,0:T(8,128)} %get-tuple-element.19.prefix_sum, ...), custom_call_target="tpu_custom_call" | custom-call | tf_op jit(solution)/shard_map/prefix_network/pallas_call | solution.py:1325

commit v8 on v7

--- a/solution.py
+++ b/solution.py
@@ -922,12 +922,10 @@
         rows = block_rows(j)
         q = quarter(i)
         u = dot_nn(normed[rows, :], wud[q, 0:1024, :]) + vec[q, 6:7, :]
-        u2 = u * u
-        t = jnp.tanh(u * (GELU_A + (GELU_A * GELU_B) * u2))
-        half_t = 0.5 + 0.5 * t
+        v = u * (GELU_A + (GELU_A * GELU_B) * (u * u))
+        half_t = 0.5 + 0.5 * jnp.tanh(v)
         wide[rows, :] = (u * half_t).astype(jnp.bfloat16)
-        inner = u * (GELU_A + (3.0 * GELU_A * GELU_B) * u2)
-        slope[q, rows, :] = (half_t + 0.5 * inner * (1.0 - t * t)).astype(jnp.bfloat16)
+        slope[q, rows, :] = (half_t + half_t * (1.0 - half_t) * (6.0 * v - (4.0 * GELU_A) * u)).astype(jnp.bfloat16)
         acc[rows, :] += dot_nn(wide[rows, :], wud[q, 1024:2048, :])
 
     def hand_copies(j, k):

time: 290 us -> 289 us (level)
  no operation moved by 1% of the time
where the time goes in v8:
time: 289 us
  Pallas kernels  288 us (100%)
    pallas_call x1, Pallas kernels, run_layers(): pl.pallas_call(layer_kernel, out_shape=(jax.ShapeDtypeStruct(x.shape, bf)...  283 us

profile of v8, /device:TPU:0, one launch (start us, length us, event | category | flops | bytes accessed | tf_op | source)
XLA Modules:
  0.0 289.1 jit_solution(6437667264012162981)
XLA Ops:
  0.6 282.9 %two_layers.1 = (bf16[2,256,1024]{2,1,0:T(8,128)(2,1)}, bf16[2,256,1024]{2,1,0:T(8,128)(2,1)}, f32[16,512]{1,0:T(8,128)}, f32[16,512]{1,0:T(8,128)}, f32[16,512]{1,0:T(8,128)}) custom-call(bf16[2,256,1024]{2,1,0:T(8,128)(2,1)} %bitcast.18, bf16[2,256,1024]{2,1,0:T(8,128)(2,1)} %bitcast.19, bf16[1024,768]{1,0:T(8,128)(2,1)} %bitcast.17, ...), custom_call_target="tpu_custom_call" | custom-call | tf_op jit(solution)/shard_map/two_layers/pallas_call | solution.py:1274
  283.6 5.4 %prefix_network.1 = (f32[10,1024]{1,0:T(8,128)}, f32[1024,512]{1,0:T(8,128)}, f32[1,512]{1,0:T(1,128)}, f32[512,512]{1,0:T(8,128)}, f32[1,512]{1,0:T(1,128)}, /*...) custom-call(f32[16,512]{1,0:T(8,128)} %get-tuple-element.19.prefix_sum, ...), custom_call_target="tpu_custom_call" | custom-call | tf_op jit(solution)/shard_map/prefix_network/pallas_call | solution.py:1323

commit v9 on v8

--- a/solution.py
+++ b/solution.py
@@ -351,7 +351,7 @@
 MESH = pl.DeviceIdType.MESH
 BLOCK = 256
 LOG2E = 1.4426950408889634
-CHUNK = 128
+CHUNK = 256
 UNITS = 12
 AHEAD = 10
 UNIT_ROWS = 512

time: 289 us -> 288 us (level)
  no operation moved by 1% of the time
where the time goes in v9:
time: 288 us; the launch traced here: 287 us
  Pallas kernels  287 us (100%)
    pallas_call x1, Pallas kernels, run_layers(): pl.pallas_call(layer_kernel, out_shape=(jax.ShapeDtypeStruct(x.shape, bf)...  281 us

profile of v9, /device:TPU:0, one launch (start us, length us, event | category | flops | bytes accessed | tf_op | source)
XLA Modules:
  0.0 287.5 jit_solution(4546957191179455457)
XLA Ops:
  0.6 281.3 %two_layers.1 = (bf16[2,256,1024]{2,1,0:T(8,128)(2,1)}, bf16[2,256,1024]{2,1,0:T(8,128)(2,1)}, f32[16,512]{1,0:T(8,128)}, f32[16,512]{1,0:T(8,128)}, f32[16,512]{1,0:T(8,128)}) custom-call(bf16[2,256,1024]{2,1,0:T(8,128)(2,1)} %bitcast.18, bf16[2,256,1024]{2,1,0:T(8,128)(2,1)} %bitcast.19, bf16[1024,768]{1,0:T(8,128)(2,1)} %bitcast.17, ...), custom_call_target="tpu_custom_call" | custom-call | tf_op jit(solution)/shard_map/two_layers/pallas_call | solution.py:1274
  281.9 5.4 %prefix_network.1 = (f32[10,1024]{1,0:T(8,128)}, f32[1024,512]{1,0:T(8,128)}, f32[1,512]{1,0:T(1,128)}, f32[512,512]{1,0:T(8,128)}, f32[1,512]{1,0:T(1,128)}, /*...) custom-call(f32[16,512]{1,0:T(8,128)} %get-tuple-element.19.prefix_sum, ...), custom_call_target="tpu_custom_call" | custom-call | tf_op jit(solution)/shard_map/prefix_network/pallas_call | solution.py:1323
